TPU v7x, 256 devices: a whole 4x4x8 slice. The times are simulated.
256 devices in a mesh: samp: 8 (over x, core), var: 32 (over y, z).
Axes of the slice: x: 4, y: 4, z: 8, core: 2. Of those that a mesh axis runs over, the one named last changes fastest.
Arguments:
- samples: bfloat16 [2048, 8192], P('samp', 'var'), may hold values from -12 to 12
- theta_diag: float32 [8192], P('var'), may hold values from 3 to 6
- theta_vals: float32 [2048, 128, 128], P('var'), may hold values from -0.046875 to 0.046875
- theta_cols: int32 [2048, 1], P('var'), may hold values from 0 to 63; in each aligned block of 64 rows (0 to 63, 64 to 127, ...) at most 2 rows name the same one
- theta_count: int32 [64], P('var'), may hold values from 16 to 32
- panel_blocks: int32 [8], replicated, may hold values from 0 to 63, as said below
- act_pan: int32 [256], P('var'), may hold values from 0 to 7, as said below
Outputs:
- inverse: float32 [8192, 1024], P('var', 'samp')
- residual: float32 [8192, 1024], P('var', 'samp')
- gradient: float32 [256, 128, 128], P('var', 'samp')
Inputs may be any that keep to these rules, and one draw needn't show every extreme that they name: `theta_cols`: within the slots of one index of var (64 aligned rows), no column block is named more than 2 times. `panel_blocks`: all different. `act_pan`: the 4 entries of one row block are all different.
All inputs are finite; a program needn't handle non-finite values.
Results may differ from a plain program's by a relative error of at most 0.0003.
Values may be sent and summed in bfloat16 or wider, within the bound.
No kernel may reach another device: no remote copies, remote signals or barrier semaphores. Data moves between devices by JAX's collectives and lax.ppermute only.
A program may use at most 128 MiB of HBM per device.

v0:
```python
import jax
import jax.numpy as jnp
from jax import lax
from jax.sharding import PartitionSpec as P

BLK = 128
BLK_DEV = 2
PAN_DEV = 1
SLOTS = 32
ACTS = 4
CG_STEPS = 2


HIGH = lax.Precision.HIGHEST


def per_device(samples, theta_diag, theta_vals, theta_cols, theta_count, panel_blocks, act_pan):
    owners = lax.axis_size("var")
    groups = lax.axis_size("samp")
    owner_index = lax.axis_index("var")
    group_index = lax.axis_index("samp")
    nblocks = BLK_DEV * owners
    panel_width = PAN_DEV * BLK
    local_size = BLK_DEV * BLK
    columns = theta_cols[:, 0]
    slot_ids = jnp.arange(BLK_DEV * SLOTS)
    local_rows = slot_ids // SLOTS
    usable = (slot_ids % SLOTS < theta_count[local_rows]).astype(jnp.float32)
    weights = theta_vals * usable[:, None, None]
    mine_panels = lax.dynamic_slice_in_dim(panel_blocks, group_index * PAN_DEV, PAN_DEV)
    row_blocks = owner_index * BLK_DEV + jnp.arange(BLK_DEV)
    panel_hits = (row_blocks[:, None] == mine_panels[None, :]).astype(jnp.float32)
    eye_block = jnp.eye(BLK, dtype=jnp.float32)
    target = (panel_hits[:, None, :, None] * eye_block[None, :, None, :]).reshape(
        local_size, panel_width
    )

    def column_squares(field_value):
        return lax.psum(jnp.sum(field_value * field_value, axis=0), "var")

    inverse = jnp.zeros_like(target)
    residual = target
    direction = target
    norm_now = column_squares(residual)
    for iteration in range(CG_STEPS):
        gathered = lax.all_gather(direction, "var", axis=0, tiled=True)
        blocks = gathered.reshape(nblocks, BLK, panel_width)
        picked = blocks[columns]
        forward_part = jnp.einsum("eij,ejc->eic", weights, picked, precision=HIGH)
        forward_part = (
            forward_part.reshape(BLK_DEV, SLOTS, BLK, panel_width)
            .sum(axis=1)
            .reshape(local_size, panel_width)
        )
        own_blocks = direction.reshape(BLK_DEV, BLK, panel_width)[local_rows]
        turned = jnp.einsum("eji,ejc->eic", weights, own_blocks, precision=HIGH)
        block_count = local_size * lax.axis_size("var") // BLK
        matches = (columns[:, None] == jnp.arange(block_count)[None, :]).astype(jnp.float32)
        transposed_part = lax.psum_scatter(
            jnp.einsum("en,eic->nic", matches, turned, precision=HIGH).reshape(
                local_size * lax.axis_size("var"), panel_width
            ),
            "var",
            scatter_dimension=0,
            tiled=True,
        )
        image_field = theta_diag[:, None] * direction + forward_part + transposed_part
        curvature = lax.psum(jnp.sum(direction * image_field, axis=0), "var")
        step_size = norm_now / curvature
        inverse = inverse + step_size * direction
        residual = residual - step_size * image_field
        norm_next = column_squares(residual)
        direction = residual + norm_next / norm_now * direction
        norm_now = norm_next
    gathered_x = lax.all_gather(samples, "var", axis=1, tiled=True)
    count_rows = samples.shape[0]
    active_rows = jnp.arange(BLK_DEV * ACTS) // ACTS
    active_cols = panel_blocks[act_pan]
    left_cols = samples.reshape(count_rows, BLK_DEV, BLK)[:, active_rows]
    right_cols = gathered_x.reshape(count_rows, nblocks, BLK)[:, active_cols]
    gram_part = jnp.einsum(
        "ska,skb->kab", left_cols, right_cols, preferred_element_type=jnp.float32
    )
    offsets = act_pan - group_index * PAN_DEV
    owned_panel = ((offsets >= 0) & (offsets < PAN_DEV)).astype(jnp.float32)
    clipped = jnp.clip(offsets, 0, PAN_DEV - 1)
    chosen = inverse.reshape(BLK_DEV, BLK, PAN_DEV, BLK)[active_rows, :, clipped, :]
    grad_term = gram_part / float(count_rows * groups) - owned_panel[:, None, None] * chosen
    rows_each = BLK // groups
    totals = lax.psum(grad_term, "samp")
    gradient = lax.dynamic_slice_in_dim(totals, group_index * rows_each, rows_each, 1)
    return (inverse, residual, gradient)


def solution(mesh):
    in_specs = (
        P("samp", "var"),
        P("var"),
        P("var", None, None),
        P("var", None),
        P("var"),
        P(),
        P("var"),
    )
    out_specs = (P("var", "samp"), P("var", "samp"), P("var", "samp", None))
    return jax.shard_map(
        per_device, mesh=mesh, in_specs=in_specs, out_specs=out_specs, check_vma=False
    )
```

profile of v0, /device:TPU:8, one launch (start us, length us, event | category | flops | bytes accessed | tf_op | source)
XLA Modules:
  0.0 907.5 jit_solution(16795607073447639259)
XLA Ops:
  7.2 1.2 dynamic_slice.6
  10.2 2.7 gather_fusion.1
  13.5 1.3 compare_convert_fusion
  14.8 9.4 %fusion.8 = f32[64,128,128]{2,1,0:T(8,128)S(1)} fusion(f32[64,128,128]{2,1,0:T(8,128)} %gather_fusion.1, f32[64,128,128]{2,1,0:T(8,128)} %param.9, f32[64]{0:T(128)S(1)} %compare_convert_fusion), kind=kOutput, calls=%fused_computation.18 | convolution fusion | flops 1611661312 | bytes 12583168 | tf_op jit(solution)/shard_map/eji,ejc->eic/dot_general | solution.py:56
  24.3 4.8 fusion.2
  29.1 4.4 copy.15
  33.5 12.0 %all-gather.8.cloned.1.call-start = ((), (), s32[]{:S(2)}) async-start(), calls=%async_computation.6 | async-start | bytes 4325376 | tf_op jit(solution)/shard_map/all_gather | solution.py:75
  45.6 0.8 copy.19
  46.5 48.1 %all-gather.4.cloned.1.call-done = f32[8192,128]{1,0:T(8,128)} async-done(((f32[256,128]{1,0:T(8,128)}), f32[8192,128]{1,0:T(8,128)}) %all-gather.4.cloned.1.call-update) | async-done | bytes 4194320 | tf_op jit(solution)/shard_map/all_gather | solution.py:46
  94.6 5.0 gather_fusion
  99.6 8.2 bitcast_reduce_fusion.1
  107.8 209.6 %reduce-scatter.3.cloned.1.call-done = f32[256,128]{1,0:T(8,128)} async-done(((f32[8192,128]{1,0:T(8,128)}), f32[256,128]{1,0:T(8,128)}) %reduce-scatter.3.cloned.1.call-update) | async-done | bytes 131088 | tf_op jit(solution)/shard_map/reduce_scatter | solution.py:59
  317.4 1.1 fusion.30
  318.5 63.0 %all-reduce = (f32[128]{0:T(128)S(1)}, f32[128]{0:T(128)S(1)}) all-reduce(f32[128]{0:T(128)S(1)} %get-tuple-element.9, f32[128]{0:T(128)S(1)} %get-tuple-element.5), channel_id=1, replica_groups=mesh['samp'=8,'var'=32] {'var'}, use_global_device_ids=true, to_apply=%region_1.2 | all-reduce | flops 256 | bytes 2048 | tf_op jit(solution)/shard_map/psum | solution.py:39
  381.6 68.1 %psum.37 = f32[128]{0:T(128)S(1)} all-reduce(f32[128]{0:T(128)S(1)} %multiply_reduce_fusion.1), channel_id=1, replica_groups=mesh['samp'=8,'var'=32] {'var'}, use_global_device_ids=true, to_apply=%region_7.8 | all-reduce | flops 128 | bytes 1024 | tf_op jit(solution)/shard_map/psum | solution.py:39
  449.8 0.8 fusion.32
  450.6 3.7 gather_fusion.3
  454.3 9.4 %fusion.4 = f32[64,128,128]{2,1,0:T(8,128)S(1)} fusion(f32[64,128,128]{2,1,0:T(8,128)} %gather_fusion.3, f32[64,128,128]{2,1,0:T(8,128)} %param.9, f32[64]{0:T(128)S(1)} %compare_convert_fusion), kind=kOutput, calls=%fused_computation.14 | convolution fusion | flops 1611661312 | bytes 12583168 | tf_op jit(solution)/shard_map/eji,ejc->eic/dot_general | solution.py:56
  463.7 4.8 fusion
  468.5 4.4 copy.18
  475.2 6.4 copy.22
  481.6 2.9 gather_fusion.6
  484.4 53.8 %all-gather.6.cloned.1.call-done = f32[8192,128]{1,0:T(8,128)} async-done(((f32[256,128]{1,0:T(8,128)}), f32[8192,128]{1,0:T(8,128)}) %all-gather.6.cloned.1.call-update) | async-done | bytes 4194320 | tf_op jit(solution)/shard_map/all_gather | solution.py:46
  538.3 4.9 gather_fusion.2
  543.2 8.2 bitcast_reduce_fusion
  551.4 210.0 %reduce-scatter.5.cloned.1.call-done = f32[256,128]{1,0:T(8,128)} async-done(((f32[8192,128]{1,0:T(8,128)}), f32[256,128]{1,0:T(8,128)}) %reduce-scatter.5.cloned.1.call-update) | async-done | bytes 131088 | tf_op jit(solution)/shard_map/reduce_scatter | solution.py:59
  761.4 1.1 multiply_reduce_fusion
  762.5 62.7 %psum.38 = f32[128]{0:T(128)S(1)} all-reduce(f32[128]{0:T(128)S(1)} %multiply_reduce_fusion), channel_id=1, replica_groups=mesh['samp'=8,'var'=32] {'var'}, use_global_device_ids=true, to_apply=%region_11.12 | all-reduce | flops 128 | bytes 1024 | tf_op jit(solution)/shard_map/psum | solution.py:68
  825.2 1.7 multiply_subtract_fusion
  827.5 1.2 fusion.20
  828.7 70.1 %all-reduce.3.cloned.1.call-done = f32[8,128,128]{2,1,0:T(8,128)} async-done(((f32[8,128,128]{2,1,0:T(8,128)}), f32[8,128,128]{2,1,0:T(8,128)}) %all-reduce.3.cloned.1.call-update) | async-done | bytes 524304 | tf_op jit(solution)/shard_map/psum | solution.py:90
  898.8 1.5 constant_dynamic-slice_fusion
  (54 shorter events, 5.3 us)
Async XLA Ops:
  7.2 87.4 %all-gather.4.cloned.1.call-start = ((), (), s32[]{:S(2)}) async-start(), calls=%async_computation.2 | async-start | bytes 4325376 | tf_op jit(solution)/shard_map/all_gather | solution.py:46
  10.0 307.4 %reduce-scatter.3.cloned.1.call-start = ((), (), s32[]{:S(2)}) async-start(), calls=%async_computation.3 | async-start | bytes 4325376 | tf_op jit(solution)/shard_map/reduce_scatter | solution.py:59
  10.2 2.7 copy-start.6
  14.8 9.5 %copy-start.5 = (s32[64,1]{0,1:T(1,128)S(1)}, s32[64,1]{0,1:T(1,128)}, u32[]{:S(2)}) copy-start(s32[64,1]{0,1:T(1,128)} %param.10) | copy-start | bytes 772
  33.5 12.1 %copy-start.3 = (bf16[256,256]{1,0:T(8,128)(2,1)S(1)}, bf16[256,256]{1,0:T(8,128)(2,1)}, u32[]{:S(2)}) copy-start(bf16[256,256]{1,0:T(8,128)(2,1)} %param.7) | copy-start | bytes 393220
  33.5 441.6 %all-gather.8.cloned.1.call-start = ((), (), s32[]{:S(2)}) async-start(), calls=%async_computation.6 | async-start | bytes 4325376 | tf_op jit(solution)/shard_map/all_gather | solution.py:75
  46.4 491.9 %all-gather.6.cloned.1.call-start = ((), (), s32[]{:S(2)}) async-start(), calls=%async_computation.4 | async-start | bytes 4325376 | tf_op jit(solution)/shard_map/all_gather | solution.py:46
  99.6 217.9 %copy-start.4 = (f32[256]{0:T(256)S(1)}, f32[256]{0:T(256)}, u32[]{:S(2)}) copy-start(f32[256]{0:T(256)} %param.8) | copy-start | bytes 3076
  450.5 310.9 %reduce-scatter.5.cloned.1.call-start = ((), (), s32[]{:S(2)}) async-start(), calls=%async_computation.5 | async-start | bytes 4325376 | tf_op jit(solution)/shard_map/reduce_scatter | solution.py:59
  472.9 0.7 copy-start.7
  473.0 0.7 copy-start
  473.0 1.3 copy-start.2
  473.0 425.8 %all-reduce.3.cloned.1.call-start = ((), (), s32[]{:S(2)}) async-start(), calls=%async_computation.7 | async-start | bytes 1048576 | tf_op jit(solution)/shard_map/psum | solution.py:90
  826.9 73.4 %copy-start.1 = (f32[256,128]{1,0:T(8,128)}, f32[256,128]{1,0:T(8,128)S(1)}, u32[]{:S(2)}) copy-start(f32[256,128]{1,0:T(8,128)S(1)} %get-tuple-element.8) | copy-start | bytes 393220
Sparse Core Ops, SparseCore 0:
  11.2 83.3 all-gather.3
  98.5 218.8 reduce-scatter.2
  320.9 80.5 all-gather.7
  450.7 87.5 all-gather.5
  542.5 218.9 reduce-scatter.4
  828.8 69.9 all-reduce.2
where the time goes:
time: 916 us; the launch traced here: 907 us
  waiting for transfers between devices  592 us (65%)
  blocking collectives  194 us (21%)
  matrix products  46.1 us (5%)
  local copies, waits for them, and re-layouts  40.9 us (4%)
  between operations  14.7 us (2%)
  starting transfers between devices  12.4 us (1%)
    reduce_scatter x2, waiting for transfers between devices, per_device(): lax.psum_scatter(jnp.einsum('en,eic->nic', matches, turned, precision=HIG...  420 us
    psum x2, blocking collectives, column_squares(): return lax.psum(jnp.sum(field_value * field_value, axis=0), 'var')  131 us
    all_gather x2, waiting for transfers between devices, per_device(): gathered = lax.all_gather(direction, 'var', axis=0, tiled=True)  102 us
    psum x1, waiting for transfers between devices, per_device(): totals = lax.psum(grad_term, 'samp')  70.1 us
    psum x1, blocking collectives, per_device(): curvature = lax.psum(jnp.sum(direction * image_field, axis=0), 'var')  62.7 us
    dot_general x2, matrix products, per_device(): turned = jnp.einsum('eji,ejc->eic', weights, own_blocks, precision=HIGH)  18.9 us
  transfers between devices with their start and end apart: 6, of which 5 were waited for; matrix products, arithmetic and copies ran while one was open for 9% of the time, Pallas kernels for 0%

commit v1 on v0

v1 whole, which is shorter than its diff:
```python
import jax
import jax.numpy as jnp
from jax import lax
from jax.sharding import PartitionSpec as P

BLK = 128
BLK_DEV = 2
SLOTS = 32
ACTS = 4
HIGH = lax.Precision.HIGHEST
F32 = jnp.float32
BF16 = jnp.bfloat16
YS = 4
ZS = 8


def y_shift(x, k):
    return lax.ppermute(x, "var", [(i, (i + ZS * k) % (YS * ZS)) for i in range(YS * ZS)])


def z_shift(x, k):
    return lax.ppermute(
        x, "var", [(i, (i // ZS) * ZS + (i % ZS + k) % ZS) for i in range(YS * ZS)]
    )


def ring_gather(x):
    h = x.shape[0] // 2
    left, right = y_shift(x, 1), y_shift(x, -1)
    far = [y_shift(left[:h], 1), y_shift(right[h:], -1)]
    block = jnp.concatenate([x, left, right] + far)
    h = block.shape[0] // 2
    parts = [block]
    left = right = block
    for _ in range(3):
        left, right = z_shift(left, 1), z_shift(right, -1)
        parts += [left, right]
    parts += [z_shift(left[:h], 1), z_shift(right[h:], -1)]
    return jnp.concatenate(parts)


def split(v):
    head = lax.reduce_precision(v, 8, 7)
    return head.astype(BF16), (v - head).astype(BF16)


Y_ORDER = (0, -1, 1, 2)
Z_ORDER = (0, -1, 1, -2, 2, -3, 3, 4)


def per_device(samples, theta_diag, theta_vals, theta_cols, theta_count, panel_blocks, act_pan):
    owners = lax.axis_size("var")
    groups = lax.axis_size("samp")
    j = lax.axis_index("var")
    s = lax.axis_index("samp")
    nb = BLK_DEV * owners
    sl = BLK // groups
    rows = BLK_DEV * sl
    size = BLK_DEV * BLK
    pans = groups
    columns = theta_cols[:, 0].reshape(BLK_DEV, SLOTS)
    usable = jnp.arange(SLOTS)[None, :] < theta_count[:, None]
    match = ((columns[:, None, :] == jnp.arange(nb)[None, :, None]) & usable[:, None, :]).astype(F32)

    gathered_x = lax.all_gather(samples, "var", axis=1, tiled=True)

    vals = theta_vals.reshape(BLK_DEV, SLOTS, BLK, BLK)
    row_slice = lax.dynamic_slice_in_dim(vals, s * sl, sl, 2)
    x_local = jnp.einsum("rce,reak->crak", match, row_slice, precision=HIGH)
    got = lax.all_to_all(
        x_local.reshape(owners, BLK_DEV * rows, BLK), "var", 0, 0
    ).reshape(owners, BLK_DEV, BLK_DEV, sl, BLK)

    mine = x_local[panel_blocks]
    from_rows = mine.transpose(1, 2, 0, 3).reshape(rows, pans * BLK)
    picked = got.transpose(0, 2, 1, 3, 4).reshape(nb, BLK_DEV, sl, BLK)[panel_blocks]
    turned = picked.transpose(1, 3, 0, 2).reshape(BLK_DEV, groups, sl, pans * sl)
    turned = turned.transpose(1, 0, 2, 3).reshape(groups, rows, pans * sl)
    turned = lax.all_to_all(turned, "samp", 0, 0)
    from_cols = (
        turned.reshape(groups, rows, pans, sl).transpose(1, 2, 0, 3).reshape(rows, pans * BLK)
    )
    e_slice = from_rows + from_cols
    slice_row = (jnp.arange(BLK_DEV)[:, None] * BLK + s * sl + jnp.arange(sl)[None, :]).reshape(rows)
    global_row = j * size + slice_row
    target_row = (panel_blocks[:, None] * BLK + jnp.arange(BLK)[None, :]).reshape(pans * BLK)
    on_diag = global_row[:, None] == target_row[None, :]
    diag_slice = lax.dynamic_slice_in_dim(theta_diag.reshape(BLK_DEV, BLK), s * sl, sl, 1).reshape(rows)
    u_slice = jnp.where(on_diag, 0.0, e_slice)
    d_part = jnp.sum(jnp.where(on_diag, e_slice + diag_slice[:, None], 0.0), axis=0)
    s2_part = jnp.sum(u_slice * u_slice, axis=0)

    u_all = ring_gather(jnp.concatenate(split(u_slice)))

    col_slice = lax.dynamic_slice_in_dim(vals, s * sl, sl, 3)
    own = jnp.einsum("rce,remk->ckrm", match, col_slice, precision=HIGH)
    a_mat = got.transpose(0, 2, 3, 1, 4).reshape(YS, ZS, rows, size) + own.reshape(
        YS, ZS, rows, size
    )
    y, z = j // ZS, j % ZS
    a_mat = a_mat[(y + jnp.array(Y_ORDER)) % YS]
    a_mat = a_mat[:, (z + jnp.array(Z_ORDER)) % ZS].transpose(1, 0, 2, 3)
    a_hi, a_lo = split(a_mat)

    def doubled(v):
        return jnp.concatenate([v, v], axis=2).reshape(owners * 2 * rows, size)

    def product(v):
        return lax.dot_general(
            doubled(v), u_all, (((0,), (0,)), ((), ())), preferred_element_type=F32
        )

    w_part = product(a_hi) + product(a_lo)

    count_rows = samples.shape[0]
    active_cols = panel_blocks[act_pan]
    left_cols = samples.reshape(count_rows, BLK_DEV, 1, BLK)
    left_cols = jnp.broadcast_to(left_cols, (count_rows, BLK_DEV, ACTS, BLK)).reshape(
        count_rows, BLK_DEV * ACTS, BLK
    )
    right_cols = gathered_x.reshape(count_rows, nb, BLK)[:, active_cols]
    gram_part = jnp.einsum(
        "ska,skb->kab", left_cols, right_cols, preferred_element_type=F32
    )
    gram = lax.psum_scatter(gram_part, "samp", scatter_dimension=1, tiled=True)

    def by_panel(v):
        return v.reshape(-1, pans, BLK).transpose(1, 0, 2)

    scalars = jnp.concatenate([d_part[None], s2_part[None], jnp.zeros((6, pans * BLK), F32)])
    bundle = jnp.concatenate([by_panel(w_part), by_panel(u_slice), by_panel(scalars)], axis=1)
    bundle = lax.all_to_all(bundle, "samp", 0, 0)
    w_sum = jnp.sum(bundle[:, :size], axis=0)
    u = bundle[:, size : size + rows].reshape(groups, BLK_DEV, sl, BLK)
    u = u.transpose(1, 0, 2, 3).reshape(size, BLK)
    ds = jnp.sum(bundle[:, size + rows :], axis=0)
    w = w_sum + theta_diag[:, None] * u
    q_part = jnp.sum(u * w, axis=0)
    tiny = jnp.concatenate([ds[:2], q_part[None], jnp.zeros((5, BLK), F32)])
    tiny = lax.all_to_all(jnp.broadcast_to(tiny[None], (owners, 8, BLK)), "var", 0, 0)
    tiny = jnp.sum(tiny, axis=0)
    d, s2, q = tiny[0], tiny[1], tiny[2]

    alpha1 = 1.0 / d
    rr = s2 * alpha1 * alpha1
    alpha2 = s2 / (q - alpha1 * s2 * s2)
    mine_panel = lax.dynamic_slice_in_dim(panel_blocks, s, 1)
    own_rows = j * size + jnp.arange(size)
    target = (own_rows[:, None] == (mine_panel * BLK + jnp.arange(BLK))[None, :]).astype(F32)
    inverse = (alpha1 + alpha2 * rr) * target - (alpha1 * alpha2) * u
    residual = (alpha1 * alpha2) * w - (alpha1 + alpha2 * rr) * u - (alpha2 * rr * d) * target

    sent = inverse.reshape(BLK_DEV, groups, sl, BLK).transpose(1, 0, 2, 3)
    rows_all = lax.all_to_all(sent.reshape(groups, rows, BLK), "samp", 0, 0)
    rows_all = rows_all.reshape(pans, BLK_DEV, sl, BLK)
    active_rows = jnp.arange(BLK_DEV * ACTS) // ACTS
    chosen = rows_all[act_pan, active_rows]
    gradient = gram * (1.0 / float(count_rows * groups)) - chosen
    return (inverse, residual, gradient)


def solution(mesh):
    in_specs = (
        P("samp", "var"),
        P("var"),
        P("var", None, None),
        P("var", None),
        P("var"),
        P(),
        P("var"),
    )
    out_specs = (P("var", "samp"), P("var", "samp"), P("var", "samp", None))
    return jax.shard_map(
        per_device, mesh=mesh, in_specs=in_specs, out_specs=out_specs, check_vma=False
    )
```

time: 916 us -> 241 us (0.26)
  waiting for transfers between devices: 592 us -> 93.6 us
  blocking collectives: 194 us -> 0 us
  matrix products: 46.1 us -> 6.65 us
  starting transfers between devices: 12.4 us -> 51.1 us
  local copies, waits for them, and re-layouts: 40.9 us -> 55.7 us
  other arithmetic: 7.64 us -> 17.8 us
    reduce_scatter x2 -> x1, waiting for transfers between devices: 420 us -> 21.8 us  [per_device(): gram = lax.psum_scatter(gram_part, 'samp', scatter_dimension=1, tiled=True)]
    psum x3 -> x0, blocking collectives: 194 us -> none  [the longest x2 131 us: column_squares(): return lax.psum(jnp.sum(field_value * field_value, axis=0), 'var')]
    all_gather x2 -> x0, waiting for transfers between devices: 102 us -> none  [per_device(): gathered = lax.all_gather(direction, 'var', axis=0, tiled=True)]
    psum x1 -> x0, waiting for transfers between devices: 70.1 us -> none  [per_device(): totals = lax.psum(grad_term, 'samp')]
    dot_general x6 -> x4, matrix products: 44.9 us -> 6.3 us  [the longest x2 4.88 us: product(): lax.dot_general(doubled(v), u_all, (((0,), (0,)), ((), ())), preferred_el...]
    ppermute x0 -> x12, waiting for transfers between devices: none -> 36.7 us  [the longest x8 33.2 us: z_shift(): lax.ppermute(x, 'var', [(i, i // ZS * ZS + (i % ZS + k) % ZS) for i in ra...]
    all_to_all x0 -> x5, waiting for transfers between devices: none -> 35.1 us  [the longest x1 15.4 us: per_device(): bundle = lax.all_to_all(bundle, 'samp', 0, 0)]
    all_to_all x0 -> x5, starting transfers between devices: none -> 32.1 us  [the longest x1 11.7 us: per_device(): lax.all_to_all(x_local.reshape(owners, BLK_DEV * rows, BLK), 'var', 0, 0)]
  transfers between devices with their start and end apart: 6 -> 19, of which waited for: 5 -> 11; matrix products, arithmetic and copies ran while one was open for 9% -> 30% of each run, Pallas kernels for 0% -> 0%
where the time goes in v1:
time: 241 us; the launch traced here: 240 us
  waiting for transfers between devices  93.6 us (39%)
  local copies, waits for them, and re-layouts  55.7 us (23%)
  starting transfers between devices  51.1 us (21%)
  other arithmetic  17.8 us (7%)
  between operations  15.3 us (6%)
  matrix products  6.65 us (3%)
    ppermute x8, waiting for transfers between devices, z_shift(): lax.ppermute(x, 'var', [(i, i // ZS * ZS + (i % ZS + k) % ZS) for i in ra...  33.2 us
    reduce_scatter x1, waiting for transfers between devices, per_device(): gram = lax.psum_scatter(gram_part, 'samp', scatter_dimension=1, tiled=True)  21.8 us
    unnamed x49, local copies, waits for them, and re-layouts  17.6 us
    all_to_all x1, waiting for transfers between devices, per_device(): bundle = lax.all_to_all(bundle, 'samp', 0, 0)  15.4 us
    all_to_all x1, waiting for transfers between devices, per_device(): lax.all_to_all(x_local.reshape(owners, BLK_DEV * rows, BLK), 'var', 0, 0)  14.5 us
    ppermute x8, starting transfers between devices, z_shift(): lax.ppermute(x, 'var', [(i, i // ZS * ZS + (i % ZS + k) % ZS) for i in ra...  13.1 us
    all_to_all x1, starting transfers between devices, per_device(): lax.all_to_all(x_local.reshape(owners, BLK_DEV * rows, BLK), 'var', 0, 0)  11.7 us
    all_to_all x1, starting transfers between devices, per_device(): lax.all_to_all(jnp.broadcast_to(tiny[None], (owners, 8, BLK)), 'var', 0, 0)  8.56 us
  transfers between devices with their start and end apart: 19, of which 11 were waited for; matrix products, arithmetic and copies ran while one was open for 30% of the time, Pallas kernels for 0%

profile of v1, /device:TPU:8, one launch (start us, length us, event | category | flops | bytes accessed | tf_op | source)
XLA Modules:
  0.0 240.1 jit_solution(2646426216763269286)
XLA Ops:
  11.6 1.6 copy.120
  13.3 11.7 %all-to-all-start = ((f32[32,64,128]{2,1,0:T(8,128)}), f32[32,64,128]{2,1,0:T(8,128)S(1)}, u32[]{:S(2)}, u32[]{:S(2)}) async-start(f32[32,64,128]{2,1,0:T(8,128)} %bitcast.5), calls=%async_computation | async-start | bytes 2097152 | tf_op jit(solution)/shard_map/all_to_all | solution.py:70
  25.9 5.4 %constant_dynamic-slice_fusion.1 = f32[2,32,128,16]{3,2,1,0:T(8,128)} fusion(f32[2,32,128,128]{3,2,1,0:T(8,128)} %bitcast.130, s32[]{:T(128)S(6)} %select_n.93), kind=kLoop, calls=%fused_computation.112 | loop fusion | bytes 1048580 | tf_op jit(solution)/shard_map/dynamic_slice | solution.py:95
  31.5 2.9 %copy.152 = f32[2,32,128,16]{2,1,3,0:T(8,128)S(1)} copy(f32[2,32,128,16]{3,2,1,0:T(8,128)} %constant_dynamic-slice_fusion.1) | data formatting | bytes 1048576
  37.5 14.5 %all-to-all-done = f32[32,64,128]{2,1,0:T(8,128)S(1)} async-done(((f32[32,64,128]{2,1,0:T(8,128)}), f32[32,64,128]{2,1,0:T(8,128)S(1)}, u32[]{:S(2)}, u32[]{:S(2)}) %all-to-all-start) | async-done | bytes 1048608 | tf_op jit(solution)/shard_map/all_to_all | solution.py:70
  54.1 4.3 %all-to-all-start.1 = ((f32[8,32,128]{2,1,0:T(8,128)}), f32[8,32,128]{2,1,0:T(8,128)S(1)}, u32[]{:S(2)}, u32[]{:S(2)}) async-start(f32[8,32,128]{2,1,0:T(8,128)} %bitcast.17), calls=%async_computation.1 | async-start | bytes 262144 | tf_op jit(solution)/shard_map/all_to_all | solution.py:79
  59.0 1.8 gather_fusion.2
  72.5 2.8 %collective-permute-done = bf16[64,1024]{1,0:T(8,128)(2,1)S(1)} collective-permute-done((bf16[64,1024]{1,0:T(8,128)(2,1)S(1)}, bf16[64,1024]{1,0:T(8,128)(2,1)S(1)}, u32[]{:S(2)}, u32[]{:S(2)}) %collective-permute-start) | collective-permute-done | bytes 131104 | tf_op jit(solution)/shard_map/ppermute | solution.py:18
  75.6 2.7 %collective-permute-start.3 = (bf16[32,1024]{1,0:T(8,128)(2,1)S(1)}, bf16[32,1024]{1,0:T(8,128)(2,1)S(1)}, u32[]{:S(2)}, u32[]{:S(2)}) collective-permute-start(bf16[32,1024]{1,0:T(8,128)(2,1)S(1)} %slice.59), channel_id=1, source_target_pairs={{0,24},{1,25},{2,26},{3,27},{4,28},{5,29},{6,30},{7,31},{8,0},{9,1... | collective-permute-start | bytes 196616 | tf_op jit(solution)/shard_map/ppermute | solution.py:18
  81.8 1.7 collective-permute-start.4
  83.5 1.6 collective-permute-start.5
  85.2 1.8 copy.177
  87.0 3.1 %reshape.283 = f32[4,8,32,256]{3,2,1,0:T(8,128)} reshape(f32[32,2,16,2,128]{4,3,2,1,0:T(2,128)} %bitcast.136) | data formatting | bytes 2097152 | tf_op jit(solution)/shard_map/reshape | solution.py:97
  94.4 14.2 %collective-permute-done.4 = bf16[256,1024]{1,0:T(8,128)(2,1)} collective-permute-done((bf16[256,1024]{1,0:T(8,128)(2,1)}, bf16[256,1024]{1,0:T(8,128)(2,1)}, u32[]{:S(2)}, u32[]{:S(2)}) %collective-permute-start.4) | collective-permute-done | bytes 524320 | tf_op jit(solution)/shard_map/ppermute | solution.py:22
  108.6 3.2 %collective-permute-start.7 = (bf16[256,1024]{1,0:T(8,128)(2,1)}, bf16[256,1024]{1,0:T(8,128)(2,1)}, u32[]{:S(2)}, u32[]{:S(2)}) collective-permute-start(bf16[256,1024]{1,0:T(8,128)(2,1)} %collective-permute-done.5), channel_id=1, source_target_pairs={{0,7},{1,0},{2,1},{3,2},{4,3},{5,4},{6,5},{7,6},{8,15},{9,8},{10,9... | collective-permute-start | bytes 1572872 | tf_op jit(solution)/shard_map/ppermute | solution.py:22
  114.1 12.4 %collective-permute-done.6 = bf16[256,1024]{1,0:T(8,128)(2,1)} collective-permute-done((bf16[256,1024]{1,0:T(8,128)(2,1)}, bf16[256,1024]{1,0:T(8,128)(2,1)}, u32[]{:S(2)}, u32[]{:S(2)}) %collective-permute-start.6) | collective-permute-done | bytes 524320 | tf_op jit(solution)/shard_map/ppermute | solution.py:22
  127.0 2.8 %collective-permute-start.9 = (bf16[256,1024]{1,0:T(8,128)(2,1)}, bf16[256,1024]{1,0:T(8,128)(2,1)S(1)}, u32[]{:S(2)}, u32[]{:S(2)}) collective-permute-start(bf16[256,1024]{1,0:T(8,128)(2,1)} %collective-permute-done.7), channel_id=1, source_target_pairs={{0,7},{1,0},{2,1},{3,2},{4,3},{5,4},{6,5},{7,6},{8,15},{9,8},{10,9... | collective-permute-start | bytes 1572872 | tf_op jit(solution)/shard_map/ppermute | solution.py:22
  130.0 2.0 constant_dynamic-update-slice_fusion.13
  132.0 1.9 constant_dynamic-update-slice_fusion.12
  133.9 1.9 constant_dynamic-update-slice_fusion.11
  135.7 5.1 %collective-permute-done.8 = bf16[256,1024]{1,0:T(8,128)(2,1)S(1)} collective-permute-done((bf16[256,1024]{1,0:T(8,128)(2,1)}, bf16[256,1024]{1,0:T(8,128)(2,1)S(1)}, u32[]{:S(2)}, u32[]{:S(2)}) %collective-permute-start.8) | collective-permute-done | bytes 524320 | tf_op jit(solution)/shard_map/ppermute | solution.py:22
  140.9 1.9 constant_dynamic-update-slice_fusion.10
  142.8 3.3 %collective-permute-start.11 = (bf16[128,1024]{1,0:T(8,128)(2,1)S(1)}, bf16[128,1024]{1,0:T(8,128)(2,1)S(1)}, u32[]{:S(2)}, u32[]{:S(2)}) collective-permute-start(bf16[128,1024]{1,0:T(8,128)(2,1)S(1)} %slice.61), channel_id=1, source_target_pairs={{0,7},{1,0},{2,1},{3,2},{4,3},{5,4},{6,5},{7,6},{8,15},{9,8},{10,9... | collective-permute-start | bytes 786440 | tf_op jit(solution)/shard_map/ppermute | solution.py:22
  150.8 3.6 %fusion.39 = f32[256,1024]{1,0:T(8,128)S(1)} fusion(bf16[2048,256]{1,0:T(8,128)(2,1)S(1)} %bitcast.147, bf16[2048,1024]{1,0:T(8,128)(2,1)} %constant_dynamic-update-slice_fusion.6), kind=kOutput, calls=%fused_computation.134 | convolution fusion | flops 1073741824 | bytes 6291456 | tf_op jit(solution)/shard_map/dot_general | solution.py:109
  156.9 4.1 %all-to-all-start.2 = ((f32[8,296,128]{2,1,0:T(8,128)}), f32[8,296,128]{2,1,0:T(8,128)S(1)}, u32[]{:S(2)}, u32[]{:S(2)}) async-start(f32[8,296,128]{2,1,0:T(8,128)} %pad_maximum_fusion), calls=%async_computation.2 | async-start | bytes 2424832 | tf_op jit(solution)/shard_map/all_to_all | solution.py:132
  163.4 15.4 %all-to-all-done.2 = f32[8,296,128]{2,1,0:T(8,128)S(1)} async-done(((f32[8,296,128]{2,1,0:T(8,128)}), f32[8,296,128]{2,1,0:T(8,128)S(1)}, u32[]{:S(2)}, u32[]{:S(2)}) %all-to-all-start.2) | async-done | bytes 1212448 | tf_op jit(solution)/shard_map/all_to_all | solution.py:132
  179.7 8.6 %all-to-all-start.3 = ((f32[32,8,128]{2,1,0:T(8,128)}), f32[32,8,128]{2,1,0:T(8,128)S(1)}, u32[]{:S(2)}, u32[]{:S(2)}) async-start(f32[32,8,128]{2,1,0:T(8,128)} %broadcast_in_dim.39), calls=%async_computation.3 | async-start | bytes 262144 | tf_op jit(solution)/shard_map/all_to_all | solution.py:140
  188.4 6.4 %copy.142 = bf16[256,64,128]{2,0,1:T(8,128)(2,1)} copy(bf16[256,64,128]{0,2,1:T(8,128)(2,1)} %bitcast.135) | data formatting | bytes 8388608 | tf_op jit(solution)/shard_map/reshape | solution.py:121
  194.8 2.8 %gather_fusion.5 = bf16[8,256,128]{2,1,0:T(8,128)(2,1)S(1)} fusion(bf16[256,64,128]{2,0,1:T(8,128)(2,1)} %copy.142, s32[1024]{0:T(1024)S(1)} %pad_clamp_fusion), kind=kCustom, calls=%fused_computation.5 | custom fusion | bytes 1048608 | tf_op jit(solution)/shard_map/gather | solution.py:121
  200.0 3.4 %all-to-all-start.4 = ((f32[8,32,128]{2,1,0:T(8,128)}), f32[8,32,128]{2,1,0:T(8,128)S(1)}, u32[]{:S(2)}, u32[]{:S(2)}) async-start(f32[8,32,128]{2,1,0:T(8,128)} %multiply_subtract_fusion), calls=%async_computation.5 | async-start | bytes 262144 | tf_op jit(solution)/shard_map/all_to_all | solution.py:154
  204.2 5.2 %all-to-all-done.4 = f32[8,32,128]{2,1,0:T(8,128)S(1)} async-done(((f32[8,32,128]{2,1,0:T(8,128)}), f32[8,32,128]{2,1,0:T(8,128)S(1)}, u32[]{:S(2)}, u32[]{:S(2)}) %all-to-all-start.4) | async-done | bytes 131104 | tf_op jit(solution)/shard_map/all_to_all | solution.py:154
  210.0 21.8 %reduce-scatter.2.cloned.1.call-done = f32[8,16,128]{2,0,1:T(8,128)} async-done(((f32[8,128,128]{2,0,1:T(8,128)}), f32[8,16,128]{2,0,1:T(8,128)}) %reduce-scatter.2.cloned.1.call-update) | async-done | bytes 65552 | tf_op jit(solution)/shard_map/reduce_scatter | solution.py:125
  (157 shorter events, 48.9 us)
Async XLA Ops:
  7.2 17.9 %copy-start.4 = (bf16[256,256]{1,0:T(8,128)(2,1)S(1)}, bf16[256,256]{1,0:T(8,128)(2,1)}, u32[]{:S(2)}) copy-start(bf16[256,256]{1,0:T(8,128)(2,1)} %param.9) | copy-start | bytes 393220
  13.3 38.7 %all-to-all-start = ((f32[32,64,128]{2,1,0:T(8,128)}), f32[32,64,128]{2,1,0:T(8,128)S(1)}, u32[]{:S(2)}, u32[]{:S(2)}) async-start(f32[32,64,128]{2,1,0:T(8,128)} %bitcast.5), calls=%async_computation | async-start | bytes 2097152 | tf_op jit(solution)/shard_map/all_to_all | solution.py:70
  25.0 163.4 %all-gather.2.cloned.1.call-start = ((), (), s32[]{:S(2)}) async-start(), calls=%async_computation.6 | async-start | bytes 4325376 | tf_op jit(solution)/shard_map/all_gather | solution.py:65
  25.8 5.4 %copy-start = (s32[8]{0:T(128)S(1)}, s32[8]{0:T(128)}, u32[]{:S(2)}) copy-start(s32[8]{0:T(128)} %param.14) | copy-start | bytes 100
  31.5 20.5 %copy-start.9 = (s32[32]{0:T(128)}, s32[32]{0:T(128)S(1)}, u32[]{:S(2)}) copy-start(s32[32]{0:T(128)S(1)} %add.255) | copy-start | bytes 388
  54.1 11.4 %all-to-all-start.1 = ((f32[8,32,128]{2,1,0:T(8,128)}), f32[8,32,128]{2,1,0:T(8,128)S(1)}, u32[]{:S(2)}, u32[]{:S(2)}) async-start(f32[8,32,128]{2,1,0:T(8,128)} %bitcast.17), calls=%async_computation.1 | async-start | bytes 262144 | tf_op jit(solution)/shard_map/all_to_all | solution.py:79
  62.6 22.5 %copy-start.6 = (f32[256]{0:T(256)S(1)}, f32[256]{0:T(256)}, u32[]{:S(2)}) copy-start(f32[256]{0:T(256)} %param.10) | copy-start | bytes 3076
  68.4 6.9 %collective-permute-start = (bf16[64,1024]{1,0:T(8,128)(2,1)S(1)}, bf16[64,1024]{1,0:T(8,128)(2,1)S(1)}, u32[]{:S(2)}, u32[]{:S(2)}) collective-permute-start(bf16[64,1024]{1,0:T(8,128)(2,1)S(1)} %pad_maximum_fusion.3), channel_id=1, source_target_pairs={{0,8},{1,9},{2,10},{3,11},{4,12},{5,13},{6,14},{7,15},{8,16},{9,17... | collective-permute-start | bytes 393224 | tf_op jit(solution)/shard_map/ppermute | solution.py:18
  69.7 5.9 %collective-permute-start.1 = (bf16[64,1024]{1,0:T(8,128)(2,1)S(1)}, bf16[64,1024]{1,0:T(8,128)(2,1)S(1)}, u32[]{:S(2)}, u32[]{:S(2)}) collective-permute-start(bf16[64,1024]{1,0:T(8,128)(2,1)S(1)} %pad_maximum_fusion.3), channel_id=1, source_target_pairs={{0,24},{1,25},{2,26},{3,27},{4,28},{5,29},{6,30},{7,31},{8,0},{9,1... | collective-permute-start | bytes 393224 | tf_op jit(solution)/shard_map/ppermute | solution.py:18
  75.3 5.2 %collective-permute-start.2 = (bf16[32,1024]{1,0:T(8,128)(2,1)S(1)}, bf16[32,1024]{1,0:T(8,128)(2,1)S(1)}, u32[]{:S(2)}, u32[]{:S(2)}) collective-permute-start(bf16[32,1024]{1,0:T(8,128)(2,1)S(1)} %slice.58), channel_id=1, source_target_pairs={{0,8},{1,9},{2,10},{3,11},{4,12},{5,13},{6,14},{7,15},{8,16},{9,17... | collective-permute-start | bytes 196616 | tf_op jit(solution)/shard_map/ppermute | solution.py:18
  75.6 5.5 %collective-permute-start.3 = (bf16[32,1024]{1,0:T(8,128)(2,1)S(1)}, bf16[32,1024]{1,0:T(8,128)(2,1)S(1)}, u32[]{:S(2)}, u32[]{:S(2)}) collective-permute-start(bf16[32,1024]{1,0:T(8,128)(2,1)S(1)} %slice.59), channel_id=1, source_target_pairs={{0,24},{1,25},{2,26},{3,27},{4,28},{5,29},{6,30},{7,31},{8,0},{9,1... | collective-permute-start | bytes 196616 | tf_op jit(solution)/shard_map/ppermute | solution.py:18
  81.8 26.8 %collective-permute-start.4 = (bf16[256,1024]{1,0:T(8,128)(2,1)}, bf16[256,1024]{1,0:T(8,128)(2,1)}, u32[]{:S(2)}, u32[]{:S(2)}) collective-permute-start(bf16[256,1024]{1,0:T(8,128)(2,1)} %get-tuple-element.29), channel_id=1, source_target_pairs={{0,1},{1,2},{2,3},{3,4},{4,5},{5,6},{6,7},{7,0},{8,9},{9,10},{10,1... | collective-permute-start | bytes 1572872 | tf_op jit(solution)/shard_map/ppermute | solution.py:22
  83.5 25.1 %collective-permute-start.5 = (bf16[256,1024]{1,0:T(8,128)(2,1)}, bf16[256,1024]{1,0:T(8,128)(2,1)}, u32[]{:S(2)}, u32[]{:S(2)}) collective-permute-start(bf16[256,1024]{1,0:T(8,128)(2,1)} %get-tuple-element.29), channel_id=1, source_target_pairs={{0,7},{1,0},{2,1},{3,2},{4,3},{5,4},{6,5},{7,6},{8,15},{9,8},{10,9... | collective-permute-start | bytes 1572872 | tf_op jit(solution)/shard_map/ppermute | solution.py:22
  93.0 20.7 %copy-start.8 = (s32[2,16]{1,0:T(2,128)S(1)}, s32[2,16]{1,0:T(2,128)}, u32[]{:S(2)}) copy-start(s32[2,16]{1,0:T(2,128)} %add_add_fusion.1) | copy-start | bytes 388
  93.1 20.8 %copy-start.1 = (f32[32,8,128]{0,2,1:T(8,128)S(1)}, f32[32,8,128]{0,2,1:T(8,128)}, u32[]{:S(2)}) copy-start(f32[32,8,128]{0,2,1:T(8,128)} %copy.134) | copy-start | bytes 393220
  93.1 20.8 %copy-start.7 = (s32[32]{0:T(128)S(1)}, s32[32]{0:T(128)}, u32[]{:S(2)}) copy-start(s32[32]{0:T(128)} %add_add_fusion.2) | copy-start | bytes 388
  93.3 36.5 %copy-start.14 = (f32[8]{0:T(128)S(1)}, f32[8]{0:T(128)}, u32[]{:S(2)}) copy-start(f32[8]{0:T(128)} %pad.8.clone) | copy-start | bytes 100
  108.6 17.9 %collective-permute-start.6 = (bf16[256,1024]{1,0:T(8,128)(2,1)}, bf16[256,1024]{1,0:T(8,128)(2,1)}, u32[]{:S(2)}, u32[]{:S(2)}) collective-permute-start(bf16[256,1024]{1,0:T(8,128)(2,1)} %collective-permute-done.4), channel_id=1, source_target_pairs={{0,1},{1,2},{2,3},{3,4},{4,5},{5,6},{6,7},{7,0},{8,9},{9,10},{10,1... | collective-permute-start | bytes 1572872 | tf_op jit(solution)/shard_map/ppermute | solution.py:22
  108.6 18.3 %collective-permute-start.7 = (bf16[256,1024]{1,0:T(8,128)(2,1)}, bf16[256,1024]{1,0:T(8,128)(2,1)}, u32[]{:S(2)}, u32[]{:S(2)}) collective-permute-start(bf16[256,1024]{1,0:T(8,128)(2,1)} %collective-permute-done.5), channel_id=1, source_target_pairs={{0,7},{1,0},{2,1},{3,2},{4,3},{5,4},{6,5},{7,6},{8,15},{9,8},{10,9... | collective-permute-start | bytes 1572872 | tf_op jit(solution)/shard_map/ppermute | solution.py:22
  126.5 14.3 %collective-permute-start.8 = (bf16[256,1024]{1,0:T(8,128)(2,1)}, bf16[256,1024]{1,0:T(8,128)(2,1)S(1)}, u32[]{:S(2)}, u32[]{:S(2)}) collective-permute-start(bf16[256,1024]{1,0:T(8,128)(2,1)} %collective-permute-done.6), channel_id=1, source_target_pairs={{0,1},{1,2},{2,3},{3,4},{4,5},{5,6},{6,7},{7,0},{8,9},{9,10},{10,1... | collective-permute-start | bytes 1572872 | tf_op jit(solution)/shard_map/ppermute | solution.py:22
  127.0 15.8 %collective-permute-start.9 = (bf16[256,1024]{1,0:T(8,128)(2,1)}, bf16[256,1024]{1,0:T(8,128)(2,1)S(1)}, u32[]{:S(2)}, u32[]{:S(2)}) collective-permute-start(bf16[256,1024]{1,0:T(8,128)(2,1)} %collective-permute-done.7), channel_id=1, source_target_pairs={{0,7},{1,0},{2,1},{3,2},{4,3},{5,4},{6,5},{7,6},{8,15},{9,8},{10,9... | collective-permute-start | bytes 1572872 | tf_op jit(solution)/shard_map/ppermute | solution.py:22
  130.0 20.8 %copy-start.2 = (bf16[8,4,64,256]{3,2,1,0:T(8,128)(2,1)S(1)}, bf16[8,4,64,256]{3,2,1,0:T(8,128)(2,1)}, u32[]{:S(2)}) copy-start(bf16[8,4,64,256]{3,2,1,0:T(8,128)(2,1)} %pad_maximum_fusion.2) | copy-start | bytes 3145732
  140.8 7.7 %collective-permute-start.10 = (bf16[128,1024]{1,0:T(8,128)(2,1)S(1)}, bf16[128,1024]{1,0:T(8,128)(2,1)S(1)}, u32[]{:S(2)}, u32[]{:S(2)}) collective-permute-start(bf16[128,1024]{1,0:T(8,128)(2,1)S(1)} %slice.60), channel_id=1, source_target_pairs={{0,1},{1,2},{2,3},{3,4},{4,5},{5,6},{6,7},{7,0},{8,9},{9,10},{10,1... | collective-permute-start | bytes 786440 | tf_op jit(solution)/shard_map/ppermute | solution.py:22
  142.8 7.2 %collective-permute-start.11 = (bf16[128,1024]{1,0:T(8,128)(2,1)S(1)}, bf16[128,1024]{1,0:T(8,128)(2,1)S(1)}, u32[]{:S(2)}, u32[]{:S(2)}) collective-permute-start(bf16[128,1024]{1,0:T(8,128)(2,1)S(1)} %slice.61), channel_id=1, source_target_pairs={{0,7},{1,0},{2,1},{3,2},{4,3},{5,4},{6,5},{7,6},{8,15},{9,8},{10,9... | collective-permute-start | bytes 786440 | tf_op jit(solution)/shard_map/ppermute | solution.py:22
  147.8 6.5 %copy-start.3 = (bf16[8,4,64,256]{3,2,1,0:T(8,128)(2,1)S(1)}, bf16[8,4,64,256]{3,2,1,0:T(8,128)(2,1)}, u32[]{:S(2)}) copy-start(bf16[8,4,64,256]{3,2,1,0:T(8,128)(2,1)} %pad_maximum_fusion.1) | copy-start | bytes 3145732
  155.7 7.7 %copy-start.13 = (s32[8]{0:T(128)S(1)}, s32[8]{0:T(128)}, u32[]{:S(2)}) copy-start(s32[8]{0:T(128)} %param.15) | copy-start | bytes 100
  155.7 7.7 %copy-start.10 = (s32[32]{0:T(128)S(1)}, s32[32]{0:T(128)}, u32[]{:S(2)}) copy-start(s32[32]{0:T(128)} %copy-done.9) | copy-start | bytes 388
  155.7 7.7 %copy-start.5 = (bf16[256,256]{1,0:T(8,128)(2,1)S(1)}, bf16[256,256]{1,0:T(8,128)(2,1)}, u32[]{:S(2)}) copy-start(bf16[256,256]{1,0:T(8,128)(2,1)} %param.9) | copy-start | bytes 393220
  156.9 21.8 %all-to-all-start.2 = ((f32[8,296,128]{2,1,0:T(8,128)}), f32[8,296,128]{2,1,0:T(8,128)S(1)}, u32[]{:S(2)}, u32[]{:S(2)}) async-start(f32[8,296,128]{2,1,0:T(8,128)} %pad_maximum_fusion), calls=%async_computation.2 | async-start | bytes 2424832 | tf_op jit(solution)/shard_map/all_to_all | solution.py:132
  179.7 19.4 %all-to-all-start.3 = ((f32[32,8,128]{2,1,0:T(8,128)}), f32[32,8,128]{2,1,0:T(8,128)S(1)}, u32[]{:S(2)}, u32[]{:S(2)}) async-start(f32[32,8,128]{2,1,0:T(8,128)} %broadcast_in_dim.39), calls=%async_computation.3 | async-start | bytes 262144 | tf_op jit(solution)/shard_map/all_to_all | solution.py:140
  188.3 43.4 %reduce-scatter.2.cloned.1.call-start = ((), (), s32[]{:S(2)}) async-start(), calls=%async_computation.7 | async-start | bytes 589824 | tf_op jit(solution)/shard_map/reduce_scatter | solution.py:125
  200.0 9.4 %all-to-all-start.4 = ((f32[8,32,128]{2,1,0:T(8,128)}), f32[8,32,128]{2,1,0:T(8,128)S(1)}, u32[]{:S(2)}, u32[]{:S(2)}) async-start(f32[8,32,128]{2,1,0:T(8,128)} %multiply_subtract_fusion), calls=%async_computation.5 | async-start | bytes 262144 | tf_op jit(solution)/shard_map/all_to_all | solution.py:154
  (4 other events, 16.0 us)
Sparse Core Ops, SparseCore 0:
  29.0 91.9 all-gather.1
  199.2 32.4 reduce-scatter.1

commit v2 on v0

v2 whole, which is shorter than its diff:
```python
import functools

import jax
import jax.numpy as jnp
from jax import lax
from jax.experimental import pallas as pl
from jax.experimental.pallas import tpu as pltpu
from jax.sharding import PartitionSpec as P

BLK = 128
BLK_DEV = 2
SLOTS = 32
ACTS = 4
F32 = jnp.float32
BF16 = jnp.bfloat16
I16 = jnp.int16
HIGH = lax.Precision.HIGHEST
YS = 4
ZS = 8
OWN = YS * ZS
GRP = 8
SL = BLK // GRP
ROWS = BLK_DEV * SL
SIZE = BLK_DEV * BLK
NB = BLK_DEV * OWN
KACT = BLK_DEV * ACTS
Y_ORDER = (0, -1, 1, 2)
VMEM_LIMIT = 48 * 1024 * 1024
PARAMS = pltpu.CompilerParams(vmem_limit_bytes=VMEM_LIMIT)


def y_shift(x, k):
    return lax.ppermute(x, "var", [(i, (i + ZS * k) % OWN) for i in range(OWN)])


def z_shift(x, k):
    return lax.ppermute(
        x, "var", [(i, (i // ZS) * ZS + (i % ZS + k) % ZS) for i in range(OWN)]
    )


def ring_parts(x):
    block = jnp.concatenate([x, y_shift(x, 1), y_shift(x, -1), y_shift(x, 2)])
    h = block.shape[0] // 2
    parts = [(0, block)]
    left = right = block
    for step in range(1, 4):
        left, right = z_shift(left, 1), z_shift(right, -1)
        parts += [(-step, left), (step, right)]
    parts += [(4, z_shift(left[:h], 1)), (4, z_shift(right[h:], -1))]
    return parts


def whole(shape, dtype):
    return jax.ShapeDtypeStruct(shape, dtype)


def vmem_spec():
    return pl.BlockSpec(memory_space=pltpu.VMEM)


def smem_spec():
    return pl.BlockSpec(memory_space=pltpu.SMEM)


def scale_of(e):
    return jnp.exp2(e.astype(F32) - 15.0)


def code(x, axis):
    most = jnp.max(jnp.abs(x), axis=axis, keepdims=True)
    e = jnp.floor(jnp.log2(jnp.maximum(most, 1e-30))) + 1.0
    q = jnp.floor(x * jnp.exp2(15.0 - e) + 0.5)
    q = jnp.minimum(jnp.maximum(q, -32767.0), 32767.0)
    return q.astype(jnp.int32).astype(I16), e


def value(q):
    return q.astype(jnp.int32).astype(F32)


X_ROWS = BLK_DEV * ROWS
S_ROWS = 16
CHUNK = X_ROWS + S_ROWS + 16


def prep_kernel(meta, v_ref, smp_ref, out_ref, rows_ref, acc, exps):
    acc[...] = jnp.zeros_like(acc)
    exps[...] = jnp.zeros_like(exps)
    for r in range(BLK_DEV):

        def body(e, carry):
            @pl.when(e < meta[1 + r])
            def _():
                c = meta[1 + BLK_DEV + GRP + r * SLOTS + e]
                at = pl.multiple_of((c % BLK_DEV) * ROWS + r * SL, SL)
                acc[c // BLK_DEV, pl.ds(at, SL), :] += v_ref[r * SLOTS + e]

            return carry

        lax.fori_loop(0, SLOTS, body, 0)
    for c in range(BLK_DEV):
        q, e = code(acc[:, c * ROWS : (c + 1) * ROWS, :], 1)
        out_ref[:, c * ROWS : (c + 1) * ROWS, :] = q
        exps[:, c : c + 1, :] = e
    few = S_ROWS // BLK_DEV
    smp = smp_ref[...].astype(F32)
    parts = []
    for c in range(BLK_DEV):
        q, e = code(smp[:, c * few : (c + 1) * few], 1)
        parts.append(value(q))
        exps[:, BLK_DEV + c : BLK_DEV + c + 1, :] = e
    smp = jnp.concatenate(parts, axis=1).astype(jnp.int32)
    out_ref[:, X_ROWS : X_ROWS + S_ROWS, :] = smp.astype(I16)
    out_ref[:, X_ROWS + S_ROWS : CHUNK, :] = exps[...].astype(jnp.int32).astype(I16)
    for p in range(GRP):
        b = meta[1 + BLK_DEV + p]
        at = pl.multiple_of((b % BLK_DEV) * ROWS, ROWS)
        rows_ref[:, p * BLK : (p + 1) * BLK] = acc[b // BLK_DEV, pl.ds(at, ROWS), :]


def prep(meta, theta_vals, smp):
    grid_spec = pltpu.PrefetchScalarGridSpec(
        num_scalar_prefetch=1,
        grid=(1,),
        in_specs=[
            pl.BlockSpec((BLK_DEV * SLOTS, SL, BLK), lambda i, m: (0, m[0], 0)),
            pl.BlockSpec((OWN, S_ROWS, BLK), lambda i, m: (0, 0, 0)),
        ],
        out_specs=[
            pl.BlockSpec((OWN, CHUNK, BLK), lambda i, m: (0, 0, 0)),
            pl.BlockSpec((ROWS, GRP * BLK), lambda i, m: (0, 0)),
        ],
        scratch_shapes=[
            pltpu.VMEM((OWN, X_ROWS, BLK), F32),
            pltpu.VMEM((OWN, 16, BLK), F32),
        ],
    )
    return pl.pallas_call(
        prep_kernel,
        grid_spec=grid_spec,
        out_shape=[whole((OWN, CHUNK, BLK), I16), whole((ROWS, GRP * BLK), F32)],
        compiler_params=PARAMS,
    )(meta, theta_vals, smp)


def pick_kernel(pan, got_ref, out_ref, smp_ref, exp_ref):
    exps = []
    for p in range(GRP):
        e = value(got_ref[pan[p] // BLK_DEV, X_ROWS + S_ROWS : CHUNK, :])
        exps.append(e)
        r = pan[p] % BLK_DEV
        exp_ref[p : p + 1, :] = jnp.where(r == 0, e[2:3], e[3:4])
    for c in range(BLK_DEV):
        stack = []
        for p in range(GRP):
            b = pan[p]
            at = pl.multiple_of(c * ROWS + (b % BLK_DEV) * SL, SL)
            q = value(got_ref[b // BLK_DEV, pl.ds(at, SL), :])
            stack.append(q * scale_of(exps[p][c : c + 1]))
        turned = jnp.concatenate(stack, axis=0).T
        for g in range(GRP):
            out_ref[g, c * SL : (c + 1) * SL, :] = turned[g * SL : (g + 1) * SL]
    few = []
    for p in range(GRP):
        b = pan[p]
        x = value(got_ref[b // BLK_DEV, X_ROWS : X_ROWS + S_ROWS, :])
        few.append(jnp.where(b % BLK_DEV == 0, x[:8], x[8:]))
    smp_ref[...] = jnp.concatenate(few, axis=0)


def pick(pan, got):
    return pl.pallas_call(
        pick_kernel,
        in_specs=[smem_spec(), vmem_spec()],
        out_specs=[vmem_spec()] * 3,
        out_shape=[
            whole((GRP, ROWS, BLK), F32),
            whole((GRP * 8, BLK), F32),
            whole((GRP, BLK), F32),
        ],
        compiler_params=PARAMS,
    )(pan, got)


U_ROWS = GRP * ROWS
F_ROWS = GRP * 8
RING = U_ROWS + F_ROWS + 2 * GRP


def slice_kernel(
    meta, turned_ref, rows_ref, smp_ref, exp_ref, diag_ref, ring_ref, u_ref, d_ref, exps
):
    lane = lax.broadcasted_iota(jnp.int32, (ROWS, BLK), 1)
    row = lax.broadcasted_iota(jnp.int32, (ROWS, BLK), 0)
    in_block = meta[0] * SL + row % SL
    diag = jnp.broadcast_to(diag_ref[...], (ROWS, BLK))
    for p in range(GRP):
        e = rows_ref[:, p * BLK : (p + 1) * BLK]
        for g in range(GRP):
            moved = turned_ref[g]
            if g != p:
                moved = pltpu.roll(moved, ((g - p) * SL) % BLK, 1)
            e = e + jnp.where(lane // SL == g, moved, 0.0)
        hit = (meta[1] * BLK_DEV + row // SL == meta[2 + p]) & (in_block == lane)
        u = jnp.where(hit, 0.0, e)
        u_ref[:, p * BLK : (p + 1) * BLK] = u
        d_ref[p : p + 1, :] = jnp.sum(jnp.where(hit, e + diag, 0.0), axis=0, keepdims=True)
        q, e = code(u, 0)
        ring_ref[p * ROWS : (p + 1) * ROWS, :] = q
        exps[p : p + 1, :] = e
    exps[GRP : 2 * GRP, :] = exp_ref[...]
    ring_ref[U_ROWS : U_ROWS + F_ROWS, :] = smp_ref[...].astype(jnp.int32).astype(I16)
    ring_ref[U_ROWS + F_ROWS :, :] = exps[...].astype(jnp.int32).astype(I16)


def u_slices(meta, turned, from_rows, smp, smp_exp, diag):
    return pl.pallas_call(
        slice_kernel,
        in_specs=[smem_spec()] + [vmem_spec()] * 5,
        out_specs=[vmem_spec()] * 3,
        out_shape=[
            whole((RING, BLK), I16),
            whole((ROWS, GRP * BLK), F32),
            whole((GRP, BLK), F32),
        ],
        scratch_shapes=[pltpu.VMEM((2 * GRP, BLK), F32)],
        compiler_params=PARAMS,
    )(meta, turned, from_rows, smp, smp_exp, diag)


def theta_kernel(meta, got_ref, own_ref, hi_ref, lo_ref):
    for z in range(ZS):
        stack = []
        for dy in Y_ORDER:
            i = ((meta[0] + dy + YS) % YS) * ZS + z
            sc = scale_of(value(got_ref[i, X_ROWS + S_ROWS : CHUNK, :]))
            cols = []
            for c in range(BLK_DEV):
                q = value(got_ref[i, c * ROWS : (c + 1) * ROWS, :])
                cols.append(q * sc[c : c + 1])
            stack.append(jnp.concatenate(cols, axis=1) + own_ref[i])
        x = jnp.concatenate(stack, axis=0).T
        hi = x.astype(BF16)
        lo = (x - hi.astype(F32)).astype(BF16)
        hi_ref[z] = jnp.concatenate([hi, hi], axis=1)
        lo_ref[z] = jnp.concatenate([lo, lo], axis=1)


def theta_parts(meta, got, own):
    return pl.pallas_call(
        theta_kernel,
        in_specs=[smem_spec()] + [vmem_spec()] * 2,
        out_specs=[vmem_spec()] * 2,
        out_shape=[whole((ZS, SIZE, 2 * YS * ROWS), BF16)] * 2,
        compiler_params=PARAMS,
        cost_estimate=pl.CostEstimate(flops=0, bytes_accessed=6_000_000, transcendentals=0),
    )(meta, got, own)


def products(groups, z, a_hi, a_lo, left):
    his, los, fews, lhs_hi, lhs_lo, lhs_few = [], [], [], [], [], []
    for dz, refs in groups:
        zi = (z + dz + ZS) % ZS
        hi, lo = [], []
        for ref in refs:
            for m in range(ref.shape[0] // RING):
                at = m * RING
                sc = scale_of(value(ref[at + U_ROWS + F_ROWS : at + RING, :]))
                u = jnp.concatenate(
                    [
                        value(ref[at + p * ROWS : at + (p + 1) * ROWS, :]) * sc[p : p + 1]
                        for p in range(GRP)
                    ],
                    axis=1,
                )
                head = u.astype(BF16)
                hi.append(head)
                lo.append((u - head.astype(F32)).astype(BF16))
                few = value(ref[at + U_ROWS : at + U_ROWS + F_ROWS, :])
                few = [
                    few[p * 8 : (p + 1) * 8] * sc[GRP + p : GRP + p + 1] for p in range(GRP)
                ]
                fews.append(jnp.concatenate(few, axis=1))
        his += hi + lo
        lhs_hi.append(a_hi[zi])
        lhs_lo.append(a_lo[zi])
        lhs_few.append(left[zi])
    u = jnp.concatenate(his, axis=0)
    w = jnp.dot(jnp.concatenate(lhs_hi, axis=1), u, preferred_element_type=F32)
    w = w + jnp.dot(jnp.concatenate(lhs_lo, axis=1), u, preferred_element_type=F32)
    g = lax.dot_general(
        jnp.concatenate(lhs_few, axis=0).astype(BF16),
        jnp.concatenate(fews, axis=0).astype(BF16),
        (((0,), (0,)), ((), ())),
        preferred_element_type=F32,
    )
    return w, g


BUNDLE = SIZE + KACT * SL + 24


def grouped(shape, refs):
    at, out = 0, []
    for dz, n in shape:
        out.append((dz, refs[at : at + n]))
        at += n
    return out, refs[at:]


def early_kernel(shape, fresh, meta, a_hi, a_lo, left, *refs):
    groups, rest = grouped(shape, refs)
    w, g = products(groups, meta[0], a_hi, a_lo, left)
    if fresh:
        w_ref, g_ref = rest
        w_ref[...], g_ref[...] = w, g
    else:
        w_in, g_in, w_ref, g_ref = rest
        w_ref[...] = w_in[...] + w
        g_ref[...] = g_in[...] + g


def last_kernel(shape, meta, a_hi, a_lo, left, *refs):
    groups, rest = grouped(shape, refs)
    w_in, g_in, u_ref, out_ref, q_ref, s2_ref, g_by = rest
    w_all, g_all = products(groups, meta[0], a_hi, a_lo, left)
    for p in range(GRP):
        cols = slice(p * BLK, (p + 1) * BLK)
        w = w_in[:, cols] + w_all[:, cols]
        u = u_ref[:, cols]
        out_ref[p, 0:SIZE, :] = w
        q_ref[p : p + 1, :] = jnp.sum(u * w, axis=0, keepdims=True)
        s2_ref[p : p + 1, :] = jnp.sum(u * u, axis=0, keepdims=True)
        g_by[p] = g_in[:, cols] + g_all[:, cols]
    for k in range(KACT):
        r = k // ACTS
        mine = g_by[meta[1 + k], r * BLK : (r + 1) * BLK, :]
        for g in range(GRP):
            at = SIZE + k * SL
            out_ref[g, at : at + SL, :] = mine[g * SL : (g + 1) * SL]
    out_ref[:, SIZE + KACT * SL :, :] = jnp.zeros((GRP, 24, BLK), F32)


def flat(groups):
    return tuple((dz, len(refs)) for dz, refs in groups), [r for _, refs in groups for r in refs]


def early_products(meta, theta, left, groups, before):
    shape, refs = flat(groups)
    flops = len(groups) * 2 * 2 * SIZE * SIZE * GRP * BLK
    return pl.pallas_call(
        functools.partial(early_kernel, shape, not before),
        in_specs=[smem_spec()] + [vmem_spec()] * (3 + len(refs) + len(before)),
        out_specs=[vmem_spec()] * 2,
        out_shape=[whole((SIZE, GRP * BLK), F32)] * 2,
        compiler_params=PARAMS,
        cost_estimate=pl.CostEstimate(
            flops=flops, bytes_accessed=len(groups) * 3_000_000, transcendentals=0
        ),
    )(meta, *theta, left, *refs, *before)


def last_products(meta, theta, left, groups, before, u_rows):
    shape, refs = flat(groups)
    return pl.pallas_call(
        functools.partial(last_kernel, shape),
        in_specs=[smem_spec()] + [vmem_spec()] * (6 + len(refs)),
        out_specs=[vmem_spec()] * 3,
        out_shape=[
            whole((GRP, BUNDLE, BLK), F32),
            whole((GRP, BLK), F32),
            whole((GRP, BLK), F32),
        ],
        scratch_shapes=[pltpu.VMEM((GRP, SIZE, BLK), F32)],
        compiler_params=PARAMS,
    )(meta, *theta, left, *refs, *before, u_rows)


def per_device(samples, theta_diag, theta_vals, theta_cols, theta_count, panel_blocks, act_pan):
    j = lax.axis_index("var")
    s = lax.axis_index("samp")
    y, z = j // ZS, j % ZS
    count_rows = samples.shape[0]
    few = count_rows // OWN
    columns = theta_cols[:, 0]

    meta = jnp.concatenate([s[None], theta_count, panel_blocks, columns])
    smp = samples.reshape(OWN, few, BLK_DEV, BLK).transpose(0, 2, 1, 3)
    chunks, from_rows = prep(meta, theta_vals, smp.reshape(OWN, BLK_DEV * few, BLK))
    got = lax.all_to_all(chunks, "var", 0, 0)

    match = (columns.reshape(BLK_DEV, 1, SLOTS) == jnp.arange(NB)[None, :, None]) & (
        jnp.arange(SLOTS)[None, None, :] < theta_count[:, None, None]
    )
    vals = theta_vals.reshape(BLK_DEV, SLOTS, BLK, BLK)
    col_slice = lax.dynamic_slice_in_dim(vals, s * SL, SL, 3)
    own = jnp.einsum("rce,remk->ckrm", match.astype(F32), col_slice, precision=HIGH)
    own = own.reshape(OWN, ROWS, SIZE)
    left = samples.reshape(YS, ZS, few, SIZE)[(y + jnp.array(Y_ORDER)) % YS]
    left = left.transpose(1, 0, 2, 3).reshape(ZS, YS * few, SIZE).astype(F32)
    got, own, left = lax.optimization_barrier((got, own, left))

    turned, few_cols, few_exps = pick(panel_blocks, got)
    turned = lax.all_to_all(turned, "samp", 0, 0)
    diag_slice = lax.dynamic_slice_in_dim(theta_diag.reshape(BLK_DEV, BLK), s * SL, SL, 1)
    diag_slice = diag_slice.reshape(ROWS, 1)
    where = jnp.concatenate([s[None], j[None], panel_blocks])
    ring, u_slice, d_part = u_slices(where, turned, from_rows, few_cols, few_exps, diag_slice)
    parts = ring_parts(ring)

    u_rows = lax.all_to_all(
        jnp.broadcast_to(u_slice[None], (GRP, ROWS, GRP * BLK)), "samp", 0, 0
    )
    u_rows = u_rows.reshape(GRP, BLK_DEV, SL, GRP * BLK).transpose(1, 0, 2, 3)
    u_rows = u_rows.reshape(SIZE, GRP * BLK)

    theta = theta_parts(y[None], got, own)
    where = jnp.concatenate([z[None], act_pan])
    groups = [(dz, [part]) for dz, part in parts[:7]] + [(4, [parts[7][1], parts[8][1]])]
    sums = early_products(where, theta, left, groups[:5], ())
    sums = early_products(where, theta, left, groups[5:7], sums)
    bundle, q_part, s2_part = last_products(where, theta, left, groups[7:], sums, u_rows)

    q_part = q_part + jnp.sum(diag_slice * u_slice * u_slice, axis=0).reshape(GRP, BLK)
    tiny = jnp.concatenate([q_part, d_part, s2_part])
    tiny = lax.all_to_all(jnp.broadcast_to(tiny[None], (OWN, 3 * GRP, BLK)), "var", 0, 0)
    tiny = jnp.sum(tiny, axis=0)
    bundle = bundle.at[:, SIZE + KACT * SL :].set(
        jnp.broadcast_to(tiny[None], (GRP, 3 * GRP, BLK))
    )
    bundle = lax.all_to_all(bundle, "samp", 0, 0)
    total = jnp.sum(bundle, axis=0)
    u = lax.dynamic_slice_in_dim(u_rows, s * BLK, BLK, 1)
    w = total[:SIZE] + theta_diag[:, None] * u
    gram = total[SIZE : SIZE + KACT * SL].reshape(KACT, SL, BLK)
    q = total[SIZE + KACT * SL : SIZE + KACT * SL + GRP]
    d = total[SIZE + KACT * SL + GRP : SIZE + KACT * SL + 2 * GRP]
    s2 = bundle[0, SIZE + KACT * SL + 2 * GRP :]

    alpha1 = 1.0 / d
    rr = s2 * alpha1 * alpha1
    alpha2 = s2 / (q - alpha1 * s2 * s2)
    c_u = alpha1 * alpha2
    c_t = alpha1 + alpha2 * rr
    c_r = alpha2 * rr * d

    def own_panel(v):
        return lax.dynamic_slice_in_dim(v, s, 1, 0)

    mine_panel = lax.dynamic_slice_in_dim(panel_blocks, s, 1)
    own_rows = j * SIZE + jnp.arange(SIZE)
    target = (own_rows[:, None] == (mine_panel * BLK + jnp.arange(BLK))[None, :]).astype(F32)
    inverse = own_panel(c_t) * target - own_panel(c_u) * u
    residual = own_panel(c_u) * w - own_panel(c_t) * u - own_panel(c_r) * target

    slice_row = jnp.arange(BLK_DEV)[:, None] * BLK + s * SL + jnp.arange(SL)[None, :]
    slice_row = j * SIZE + slice_row.reshape(ROWS)
    target_row = (panel_blocks[:, None] * BLK + jnp.arange(BLK)[None, :]).reshape(GRP * BLK)
    on_diag = slice_row[:, None] == target_row[None, :]
    inv_slice = jnp.where(on_diag, c_t.reshape(1, -1), 0.0) - c_u.reshape(1, -1) * u_slice
    inv_slice = inv_slice.reshape(BLK_DEV, SL, GRP, BLK).transpose(2, 0, 1, 3)
    active_rows = jnp.arange(KACT) // ACTS
    gradient = gram * (1.0 / float(count_rows * GRP)) - inv_slice[act_pan, active_rows]
    return (inverse, residual, gradient)


def solution(mesh):
    in_specs = (
        P("samp", "var"),
        P("var"),
        P("var", None, None),
        P("var", None),
        P("var"),
        P(),
        P("var"),
    )
    out_specs = (P("var", "samp"), P("var", "samp"), P("var", "samp", None))
    return jax.shard_map(
        per_device, mesh=mesh, in_specs=in_specs, out_specs=out_specs, check_vma=False
    )
```

time: 916 us -> 162 us (0.18)
  waiting for transfers between devices: 592 us -> 52 us
  blocking collectives: 194 us -> 20.3 us
  matrix products: 46.1 us -> 0.69 us
  starting transfers between devices: 12.4 us -> 41.8 us
  local copies, waits for them, and re-layouts: 40.9 us -> 25.7 us
  Pallas kernels: 0 us -> 13.6 us
  between operations: 14.7 us -> 1.7 us
    reduce_scatter x2 -> x0, waiting for transfers between devices: 420 us -> none  [per_device(): lax.psum_scatter(jnp.einsum('en,eic->nic', matches, turned, precision=HIG...]
    psum x3 -> x0, blocking collectives: 194 us -> none  [the longest x2 131 us: column_squares(): return lax.psum(jnp.sum(field_value * field_value, axis=0), 'var')]
    all_gather x3 -> x0, waiting for transfers between devices: 102 us -> none  [the longest x2 102 us: per_device(): gathered = lax.all_gather(direction, 'var', axis=0, tiled=True)]
    psum x1 -> x0, waiting for transfers between devices: 70.1 us -> none  [per_device(): totals = lax.psum(grad_term, 'samp')]
    dot_general x7 -> x1, matrix products: 46.1 us -> 0.69 us  [per_device(): jnp.einsum('rce,remk->ckrm', match.astype(F32), col_slice, precision=HIGH)]
    all_to_all x0 -> x4, waiting for transfers between devices: none -> 35.2 us  [the longest x1 21.1 us: per_device(): bundle = lax.all_to_all(bundle, 'samp', 0, 0)]
    all_to_all x0 -> x4, starting transfers between devices: none -> 25.8 us  [the longest x1 11.7 us: per_device(): got = lax.all_to_all(chunks, 'var', 0, 0)]
    gather x9 -> x2, local copies, waits for them, and re-layouts: 21.6 us -> 1.13 us  [the longest x1 0.57 us: per_device(): inv_slice[act_pan, active_rows]]
  transfers between devices with their start and end apart: 6 -> 15, of which waited for: 5 -> 10; matrix products, arithmetic and copies ran while one was open for 9% -> 11% of each run, Pallas kernels for 0% -> 3%
where the time goes in v2:
time: 162 us; the launch traced here: 159 us
  waiting for transfers between devices  52 us (32%)
  starting transfers between devices  41.8 us (26%)
  local copies, waits for them, and re-layouts  25.7 us (16%)
  blocking collectives  20.3 us (13%)
  Pallas kernels  13.6 us (8%)
  other arithmetic  3.69 us (2%)
  between operations  1.7 us (1%)
    all_to_all x1, waiting for transfers between devices, per_device(): bundle = lax.all_to_all(bundle, 'samp', 0, 0)  21.1 us
    all_to_all x1, blocking collectives, per_device(): lax.all_to_all(jnp.broadcast_to(tiny[None], (OWN, 3 * GRP, BLK)), 'var',...  20.3 us
    ppermute x8, waiting for transfers between devices, z_shift(): lax.ppermute(x, 'var', [(i, i // ZS * ZS + (i % ZS + k) % ZS) for i in ra...  12.5 us
    all_to_all x1, starting transfers between devices, per_device(): got = lax.all_to_all(chunks, 'var', 0, 0)  11.7 us
    unnamed x46, local copies, waits for them, and re-layouts  11.4 us
    ppermute x8, starting transfers between devices, z_shift(): lax.ppermute(x, 'var', [(i, i // ZS * ZS + (i % ZS + k) % ZS) for i in ra...  11.1 us
    all_to_all x1, waiting for transfers between devices, per_device(): got = lax.all_to_all(chunks, 'var', 0, 0)  8.21 us
    all_to_all x1, waiting for transfers between devices, per_device(): turned = lax.all_to_all(turned, 'samp', 0, 0)  5.89 us
  transfers between devices with their start and end apart: 15, of which 10 were waited for; matrix products, arithmetic and copies ran while one was open for 11% of the time, Pallas kernels for 3%

profile of v2, /device:TPU:8, one launch (start us, length us, event | category | flops | bytes accessed | tf_op | source)
XLA Modules:
  0.0 159.5 jit_solution(508807223078645172)
XLA Ops:
  1.4 2.2 %copy-done = f32[64,128,128]{2,1,0:T(8,128)S(1)} copy-done((f32[64,128,128]{2,1,0:T(8,128)S(1)}, f32[64,128,128]{2,1,0:T(8,128)}, u32[]{:S(2)}) %copy-start) | copy-done | bytes 4194328
  4.5 3.5 %shard_map.103 = (s16[32,96,128]{2,1,0:T(8,128)(2,1)}, f32[32,1024]{1,0:T(8,128)S(1)}) custom-call(s32[75]{0:T(128)S(1)} %pad_add_fusion.1.meta, f32[64,128,128]{2,1,0:T(8,128)S(1)} %copy-done, bf16[32,16,128]{2,1,0:T(8,128)(2,1)S(1)} %bitcast.72), custom_call_target="tpu_custom_call" | custom-call | tf_op jit(solution)/shard_map/pallas_call | solution.py:139
  8.0 11.7 %all-to-all-start = ((s16[32,96,128]{2,1,0:T(8,128)(2,1)}), s16[32,96,128]{2,1,0:T(8,128)(2,1)S(1)}, u32[]{:S(2)}, u32[]{:S(2)}) async-start(s16[32,96,128]{2,1,0:T(8,128)(2,1)} %get-tuple-element.35), calls=%async_computation | async-start | bytes 1572864 | tf_op jit(solution)/shard_map/all_to_all | solution.py:391
  19.7 5.3 %constant_dynamic-slice_fusion.4 = f32[2,32,128,16]{3,2,1,0:T(8,128)} fusion(f32[2,32,128,128]{3,2,1,0:T(8,128)} %bitcast.69, s32[]{:T(128)S(6)} %select_n.67), kind=kLoop, calls=%fused_computation.50 | loop fusion | bytes 1048580 | tf_op jit(solution)/shard_map/dynamic_slice | solution.py:397
  25.1 2.9 %copy.26 = f32[2,32,128,16]{2,1,3,0:T(8,128)S(1)} copy(f32[2,32,128,16]{3,2,1,0:T(8,128)} %constant_dynamic-slice_fusion.4) | data formatting | bytes 1048576
  32.4 8.2 %all-to-all-done.got_ref = s16[32,96,128]{2,1,0:T(8,128)(2,1)S(1)} async-done(((s16[32,96,128]{2,1,0:T(8,128)(2,1)}), s16[32,96,128]{2,1,0:T(8,128)(2,1)S(1)}, u32[]{:S(2)}, u32[]{:S(2)}) %all-to-all-start) | async-done | bytes 786464 | tf_op jit(solution)/shard_map/all_to_all | solution.py:391
  40.6 1.4 shard_map.105
  41.9 4.3 %all-to-all-start.1 = ((f32[8,32,128]{2,1,0:T(8,128)}), f32[8,32,128]{2,1,0:T(8,128)S(1)}, u32[]{:S(2)}, u32[]{:S(2)}) async-start(f32[8,32,128]{2,1,0:T(8,128)} %get-tuple-element.41), calls=%async_computation.1 | async-start | bytes 262144 | tf_op jit(solution)/shard_map/all_to_all | solution.py:405
  46.5 5.9 %all-to-all-done.1.turned_ref = f32[8,32,128]{2,1,0:T(8,128)S(1)} async-done(((f32[8,32,128]{2,1,0:T(8,128)}), f32[8,32,128]{2,1,0:T(8,128)S(1)}, u32[]{:S(2)}, u32[]{:S(2)}) %all-to-all-start.1) | async-done | bytes 131104 | tf_op jit(solution)/shard_map/all_to_all | solution.py:405
  53.2 1.6 collective-permute-start
  54.8 1.4 collective-permute-start.1
  56.2 2.0 %collective-permute-start.2 = (s16[336,128]{1,0:T(8,128)(2,1)S(1)}, s16[336,128]{1,0:T(8,128)(2,1)S(1)}, u32[]{:S(2)}, u32[]{:S(2)}) collective-permute-start(s16[336,128]{1,0:T(8,128)(2,1)S(1)} %get-tuple-element.45), channel_id=1, source_target_pairs={{0,16},{1,17},{2,18},{3,19},{4,20},{5,21},{6,22},{7,23},{8,24},{9,... | collective-permute-start | bytes 258056 | tf_op jit(solution)/shard_map/ppermute | solution.py:33
  59.3 3.1 %collective-permute-done.2 = s16[336,128]{1,0:T(8,128)(2,1)S(1)} collective-permute-done((s16[336,128]{1,0:T(8,128)(2,1)S(1)}, s16[336,128]{1,0:T(8,128)(2,1)S(1)}, u32[]{:S(2)}, u32[]{:S(2)}) %collective-permute-start.2) | collective-permute-done | bytes 86048 | tf_op jit(solution)/shard_map/ppermute | solution.py:33
  63.3 1.2 collective-permute-start.3
  64.6 1.1 broadcast_in_dim.31
  65.7 4.2 %all-to-all-start.2 = ((f32[8,32,1024]{2,1,0:T(8,128)}), f32[8,32,1024]{2,1,0:T(8,128)}, u32[]{:S(2)}, u32[]{:S(2)}) async-start(f32[8,32,1024]{2,1,0:T(8,128)} %broadcast_in_dim.31), calls=%async_computation.2 | async-start | bytes 2097152 | tf_op jit(solution)/shard_map/all_to_all | solution.py:412
  69.9 1.4 collective-permute-done.7.refs_2_
  71.3 1.8 %collective-permute-start.8 = (s16[1344,128]{1,0:T(8,128)(2,1)S(1)}, s16[1344,128]{1,0:T(8,128)(2,1)}, u32[]{:S(2)}, u32[]{:S(2)}) collective-permute-start(s16[1344,128]{1,0:T(8,128)(2,1)S(1)} %collective-permute-done.7.refs_2_), channel_id=1, source_target_pairs={{0,7},{1,0},{2,1},{3,2},{4,3},{5,4},{6,5},{7,6},{8,15},{9,8},{10,9... | collective-permute-start | bytes 1032200 | tf_op jit(solution)/shard_map/ppermute | solution.py:37
  74.8 5.6 %collective-permute-done.8.refs_4_ = s16[1344,128]{1,0:T(8,128)(2,1)} collective-permute-done((s16[1344,128]{1,0:T(8,128)(2,1)S(1)}, s16[1344,128]{1,0:T(8,128)(2,1)}, u32[]{:S(2)}, u32[]{:S(2)}) %collective-permute-start.8) | collective-permute-done | bytes 344096 | tf_op jit(solution)/shard_map/ppermute | solution.py:37
  80.5 3.1 %collective-permute-start.9 = (s16[1344,128]{1,0:T(8,128)(2,1)}, s16[1344,128]{1,0:T(8,128)(2,1)}, u32[]{:S(2)}, u32[]{:S(2)}) collective-permute-start(s16[1344,128]{1,0:T(8,128)(2,1)} %collective-permute-done.8.refs_4_), channel_id=1, source_target_pairs={{0,7},{1,0},{2,1},{3,2},{4,3},{5,4},{6,5},{7,6},{8,15},{9,8},{10,9... | collective-permute-start | bytes 1032200 | tf_op jit(solution)/shard_map/ppermute | solution.py:37
  84.7 5.0 %collective-permute-done.9.refs_1_ = s16[1344,128]{1,0:T(8,128)(2,1)} collective-permute-done((s16[1344,128]{1,0:T(8,128)(2,1)}, s16[1344,128]{1,0:T(8,128)(2,1)}, u32[]{:S(2)}, u32[]{:S(2)}) %collective-permute-start.9) | collective-permute-done | bytes 344096 | tf_op jit(solution)/shard_map/ppermute | solution.py:37
  90.6 3.8 %collective-permute-start.10 = (s16[672,128]{1,0:T(8,128)(2,1)S(1)}, s16[672,128]{1,0:T(8,128)(2,1)S(1)}, u32[]{:S(2)}, u32[]{:S(2)}) collective-permute-start(s16[672,128]{1,0:T(8,128)(2,1)S(1)} %slice.55), channel_id=1, source_target_pairs={{0,7},{1,0},{2,1},{3,2},{4,3},{5,4},{6,5},{7,6},{8,15},{9,8},{10,9... | collective-permute-start | bytes 516104 | tf_op jit(solution)/shard_map/ppermute | solution.py:37
  95.4 2.8 %shard_map.107 = (f32[256,1024]{1,0:T(8,128)S(1)}, f32[256,1024]{1,0:T(8,128)S(1)}) custom-call(s32[9]{0:T(128)S(1)} %pad_add_fusion.meta, bf16[8,256,256]{2,1,0:T(8,128)(2,1)S(1)} %get-tuple-element.38.a_hi, bf16[8,256,256]{2,1,0:T(8,128)(2,1)S(1)} %get-tuple-element.39.a_lo, f32[8,32,256]{2,1,0:T(8,128)S(1)} %copy_bitcast_fusion.left, ...), custom_call_target="tpu_custom_call" | custom-call | flops 1342177280 | bytes 15000000 | tf_op jit(solution)/shard_map/pallas_call | solution.py:352
  98.3 1.0 copy-done.1
  99.2 1.0 copy-done.3
  100.3 1.0 copy-done.5
  101.2 1.4 copy.23
  103.1 2.3 %shard_map.108 = (f32[256,1024]{1,0:T(8,128)S(1)}, f32[256,1024]{1,0:T(8,128)S(1)}) custom-call(s32[9]{0:T(128)S(1)} %pad_add_fusion.meta, bf16[8,256,256]{2,1,0:T(8,128)(2,1)S(1)} %get-tuple-element.38.a_hi, bf16[8,256,256]{2,1,0:T(8,128)(2,1)S(1)} %copy-done.2, f32[8,32,256]{2,1,0:T(8,128)S(1)} %copy_bitcast_fusion.left, ...), custom_call_target="tpu_custom_call" | custom-call | flops 536870912 | bytes 6000000 | tf_op jit(solution)/shard_map/pallas_call | solution.py:352
  105.5 2.4 %shard_map.109 = (f32[8,408,128]{2,1,0:T(8,128)}, f32[8,128]{1,0:T(8,128)S(1)}, f32[8,128]{1,0:T(8,128)S(1)}) custom-call(s32[9]{0:T(128)S(1)} %pad_add_fusion.meta, bf16[8,256,256]{2,1,0:T(8,128)(2,1)S(1)} %get-tuple-element.38.a_hi, bf16[8,256,256]{2,1,0:T(8,128)(2,1)S(1)} %copy-done.2, f32[8,32,256]{2,1,0:T(8,128)S(1)} %copy_bitcast_fusion.left, ...), custom_call_target="tpu_custom_call" | custom-call | tf_op jit(solution)/shard_map/pallas_call | solution.py:366
  107.9 20.3 %all_to_all.25 = f32[32,24,128]{2,1,0:T(8,128)S(1)} all-to-all(f32[32,24,128]{2,1,0:T(8,128)S(1)} %broadcast_in_dim.32), channel_id=1, replica_groups=mesh['samp'=8,'var'=32] {'var'}, dimensions={0} | all-to-all | bytes 786432 | tf_op jit(solution)/shard_map/all_to_all | solution.py:427
  128.9 5.6 %all-to-all-start.4 = ((f32[8,408,128]{2,1,0:T(8,128)}), f32[8,408,128]{2,1,0:T(8,128)S(1)}, u32[]{:S(2)}, u32[]{:S(2)}) async-start(f32[8,408,128]{2,1,0:T(8,128)} %broadcast_dynamic-update-slice_fusion), calls=%async_computation.4 | async-start | bytes 3342336 | tf_op jit(solution)/shard_map/all_to_all | solution.py:432
  136.0 21.1 %all-to-all-done.4 = f32[8,408,128]{2,1,0:T(8,128)S(1)} async-done(((f32[8,408,128]{2,1,0:T(8,128)}), f32[8,408,128]{2,1,0:T(8,128)S(1)}, u32[]{:S(2)}, u32[]{:S(2)}) %all-to-all-start.4) | async-done | bytes 1671200 | tf_op jit(solution)/shard_map/all_to_all | solution.py:432
  (100 shorter events, 18.3 us)
Async XLA Ops:
  1.4 2.2 %copy-start = (f32[64,128,128]{2,1,0:T(8,128)S(1)}, f32[64,128,128]{2,1,0:T(8,128)}, u32[]{:S(2)}) copy-start(f32[64,128,128]{2,1,0:T(8,128)} %v_ref.1) | copy-start | bytes 12582916
  8.0 32.6 %all-to-all-start = ((s16[32,96,128]{2,1,0:T(8,128)(2,1)}), s16[32,96,128]{2,1,0:T(8,128)(2,1)S(1)}, u32[]{:S(2)}, u32[]{:S(2)}) async-start(s16[32,96,128]{2,1,0:T(8,128)(2,1)} %get-tuple-element.35), calls=%async_computation | async-start | bytes 1572864 | tf_op jit(solution)/shard_map/all_to_all | solution.py:391
  25.0 3.4 %copy-start.16 = (s32[64,1]{0,1:T(1,128)S(1)}, s32[64,1]{0,1:T(1,128)}, u32[]{:S(2)}) copy-start(s32[64,1]{0,1:T(1,128)} %param.13) | copy-start | bytes 772
  25.0 4.2 %copy-start.17 = (s32[2]{0:T(128)S(1)}, s32[2]{0:T(128)}, u32[]{:S(2)}) copy-start(s32[2]{0:T(128)} %param.14) | copy-start | bytes 28
  30.0 1.7 %copy-start.19 = (s32[4]{0:T(128)S(1)}, s32[4]{0:T(128)}, u32[]{:S(2)}) copy-start(s32[4]{0:T(128)} %constant.117.clone) | copy-start | bytes 52
  30.0 1.8 %copy-start.7 = (bf16[256,256]{1,0:T(8,128)(2,1)S(1)}, bf16[256,256]{1,0:T(8,128)(2,1)}, u32[]{:S(2)}) copy-start(bf16[256,256]{1,0:T(8,128)(2,1)} %param.10) | copy-start | bytes 393220
  30.8 9.7 %copy-start.10 = (s32[8]{0:T(128)S(1)}, s32[8]{0:T(128)}, u32[]{:S(2)}) copy-start(s32[8]{0:T(128)} %pan.1) | copy-start | bytes 100
  30.8 15.4 %copy-start.15 = (f32[256]{0:T(256)S(1)}, f32[256]{0:T(256)}, u32[]{:S(2)}) copy-start(f32[256]{0:T(256)} %param.11) | copy-start | bytes 3076
  41.9 10.4 %all-to-all-start.1 = ((f32[8,32,128]{2,1,0:T(8,128)}), f32[8,32,128]{2,1,0:T(8,128)S(1)}, u32[]{:S(2)}, u32[]{:S(2)}) async-start(f32[8,32,128]{2,1,0:T(8,128)} %get-tuple-element.41), calls=%async_computation.1 | async-start | bytes 262144 | tf_op jit(solution)/shard_map/all_to_all | solution.py:405
  53.2 5.3 %collective-permute-start = (s16[336,128]{1,0:T(8,128)(2,1)S(1)}, s16[336,128]{1,0:T(8,128)(2,1)S(1)}, u32[]{:S(2)}, u32[]{:S(2)}) collective-permute-start(s16[336,128]{1,0:T(8,128)(2,1)S(1)} %get-tuple-element.45), channel_id=1, source_target_pairs={{0,8},{1,9},{2,10},{3,11},{4,12},{5,13},{6,14},{7,15},{8,16},{9,17... | collective-permute-start | bytes 258056 | tf_op jit(solution)/shard_map/ppermute | solution.py:33
  54.8 4.5 %collective-permute-start.1 = (s16[336,128]{1,0:T(8,128)(2,1)S(1)}, s16[336,128]{1,0:T(8,128)(2,1)S(1)}, u32[]{:S(2)}, u32[]{:S(2)}) collective-permute-start(s16[336,128]{1,0:T(8,128)(2,1)S(1)} %get-tuple-element.45), channel_id=1, source_target_pairs={{0,24},{1,25},{2,26},{3,27},{4,28},{5,29},{6,30},{7,31},{8,0},{9,1... | collective-permute-start | bytes 258056 | tf_op jit(solution)/shard_map/ppermute | solution.py:33
  56.2 6.2 %collective-permute-start.2 = (s16[336,128]{1,0:T(8,128)(2,1)S(1)}, s16[336,128]{1,0:T(8,128)(2,1)S(1)}, u32[]{:S(2)}, u32[]{:S(2)}) collective-permute-start(s16[336,128]{1,0:T(8,128)(2,1)S(1)} %get-tuple-element.45), channel_id=1, source_target_pairs={{0,16},{1,17},{2,18},{3,19},{4,20},{5,21},{6,22},{7,23},{8,24},{9,... | collective-permute-start | bytes 258056 | tf_op jit(solution)/shard_map/ppermute | solution.py:33
  62.4 21.8 %copy-start.8 = (s16[1344,128]{1,0:T(8,128)(2,1)}, s16[1344,128]{1,0:T(8,128)(2,1)S(1)}, u32[]{:S(2)}) copy-start(s16[1344,128]{1,0:T(8,128)(2,1)S(1)} %constant_dynamic-update-slice_fusion.refs_0_) | copy-start | bytes 1032196
  62.4 21.7 %copy-start.18 = (s32[8]{0:T(128)S(1)}, s32[8]{0:T(128)}, u32[]{:S(2)}) copy-start(s32[8]{0:T(128)} %param.16) | copy-start | bytes 100
  62.4 8.9 %collective-permute-start.7 = (s16[1344,128]{1,0:T(8,128)(2,1)S(1)}, s16[1344,128]{1,0:T(8,128)(2,1)S(1)}, u32[]{:S(2)}, u32[]{:S(2)}) collective-permute-start(s16[1344,128]{1,0:T(8,128)(2,1)S(1)} %constant_dynamic-update-slice_fusion.refs_0_), channel_id=1, source_target_pairs={{0,7},{1,0},{2,1},{3,2},{4,3},{5,4},{6,5},{7,6},{8,15},{9,8},{10,9... | collective-permute-start | bytes 1032200 | tf_op jit(solution)/shard_map/ppermute | solution.py:37
  63.3 10.5 %collective-permute-start.3 = (s16[1344,128]{1,0:T(8,128)(2,1)S(1)}, s16[1344,128]{1,0:T(8,128)(2,1)S(1)}, u32[]{:S(2)}, u32[]{:S(2)}) collective-permute-start(s16[1344,128]{1,0:T(8,128)(2,1)S(1)} %constant_dynamic-update-slice_fusion.refs_0_), channel_id=1, source_target_pairs={{0,1},{1,2},{2,3},{3,4},{4,5},{5,6},{6,7},{7,0},{8,9},{9,10},{10,1... | collective-permute-start | bytes 1032200 | tf_op jit(solution)/shard_map/ppermute | solution.py:37
  65.7 35.6 %all-to-all-start.2 = ((f32[8,32,1024]{2,1,0:T(8,128)}), f32[8,32,1024]{2,1,0:T(8,128)}, u32[]{:S(2)}, u32[]{:S(2)}) async-start(f32[8,32,1024]{2,1,0:T(8,128)} %broadcast_in_dim.31), calls=%async_computation.2 | async-start | bytes 2097152 | tf_op jit(solution)/shard_map/all_to_all | solution.py:412
  71.3 9.1 %collective-permute-start.8 = (s16[1344,128]{1,0:T(8,128)(2,1)S(1)}, s16[1344,128]{1,0:T(8,128)(2,1)}, u32[]{:S(2)}, u32[]{:S(2)}) collective-permute-start(s16[1344,128]{1,0:T(8,128)(2,1)S(1)} %collective-permute-done.7.refs_2_), channel_id=1, source_target_pairs={{0,7},{1,0},{2,1},{3,2},{4,3},{5,4},{6,5},{7,6},{8,15},{9,8},{10,9... | collective-permute-start | bytes 1032200 | tf_op jit(solution)/shard_map/ppermute | solution.py:37
  73.8 10.2 %collective-permute-start.4 = (s16[1344,128]{1,0:T(8,128)(2,1)S(1)}, s16[1344,128]{1,0:T(8,128)(2,1)}, u32[]{:S(2)}, u32[]{:S(2)}) collective-permute-start(s16[1344,128]{1,0:T(8,128)(2,1)S(1)} %collective-permute-done.3.refs_1_), channel_id=1, source_target_pairs={{0,1},{1,2},{2,3},{3,4},{4,5},{5,6},{6,7},{7,0},{8,9},{9,10},{10,1... | collective-permute-start | bytes 1032200 | tf_op jit(solution)/shard_map/ppermute | solution.py:37
  80.5 9.2 %collective-permute-start.9 = (s16[1344,128]{1,0:T(8,128)(2,1)}, s16[1344,128]{1,0:T(8,128)(2,1)}, u32[]{:S(2)}, u32[]{:S(2)}) collective-permute-start(s16[1344,128]{1,0:T(8,128)(2,1)} %collective-permute-done.8.refs_4_), channel_id=1, source_target_pairs={{0,7},{1,0},{2,1},{3,2},{4,3},{5,4},{6,5},{7,6},{8,15},{9,8},{10,9... | collective-permute-start | bytes 1032200 | tf_op jit(solution)/shard_map/ppermute | solution.py:37
  84.1 10.3 %collective-permute-start.5 = (s16[1344,128]{1,0:T(8,128)(2,1)}, s16[1344,128]{1,0:T(8,128)(2,1)}, u32[]{:S(2)}, u32[]{:S(2)}) collective-permute-start(s16[1344,128]{1,0:T(8,128)(2,1)} %collective-permute-done.4.refs_3_), channel_id=1, source_target_pairs={{0,1},{1,2},{2,3},{3,4},{4,5},{5,6},{6,7},{7,0},{8,9},{9,10},{10,1... | collective-permute-start | bytes 1032200 | tf_op jit(solution)/shard_map/ppermute | solution.py:37
  84.1 11.3 %copy-start.12 = (s16[1344,128]{1,0:T(8,128)(2,1)S(1)}, s16[1344,128]{1,0:T(8,128)(2,1)}, u32[]{:S(2)}) copy-start(s16[1344,128]{1,0:T(8,128)(2,1)} %copy-done.11) | copy-start | bytes 1032196
  84.1 11.3 %copy-start.14 = (s16[1344,128]{1,0:T(8,128)(2,1)S(1)}, s16[1344,128]{1,0:T(8,128)(2,1)}, u32[]{:S(2)}) copy-start(s16[1344,128]{1,0:T(8,128)(2,1)} %copy-done.13) | copy-start | bytes 1032196
  84.2 11.2 %copy-start.9 = (s16[1344,128]{1,0:T(8,128)(2,1)S(1)}, s16[1344,128]{1,0:T(8,128)(2,1)}, u32[]{:S(2)}) copy-start(s16[1344,128]{1,0:T(8,128)(2,1)} %copy-done.8) | copy-start | bytes 1032196
  90.6 14.8 %collective-permute-start.10 = (s16[672,128]{1,0:T(8,128)(2,1)S(1)}, s16[672,128]{1,0:T(8,128)(2,1)S(1)}, u32[]{:S(2)}, u32[]{:S(2)}) collective-permute-start(s16[672,128]{1,0:T(8,128)(2,1)S(1)} %slice.55), channel_id=1, source_target_pairs={{0,7},{1,0},{2,1},{3,2},{4,3},{5,4},{6,5},{7,6},{8,15},{9,8},{10,9... | collective-permute-start | bytes 516104 | tf_op jit(solution)/shard_map/ppermute | solution.py:37
  95.3 10.1 %collective-permute-start.6 = (s16[672,128]{1,0:T(8,128)(2,1)S(1)}, s16[672,128]{1,0:T(8,128)(2,1)S(1)}, u32[]{:S(2)}, u32[]{:S(2)}) collective-permute-start(s16[672,128]{1,0:T(8,128)(2,1)S(1)} %slice.54), channel_id=1, source_target_pairs={{0,1},{1,2},{2,3},{3,4},{4,5},{5,6},{6,7},{7,0},{8,9},{9,10},{10,1... | collective-permute-start | bytes 516104 | tf_op jit(solution)/shard_map/ppermute | solution.py:37
  98.3 1.0 copy-start.1
  99.2 1.0 copy-start.3
  100.3 1.0 copy-start.5
  101.2 1.5 copy-start.2
  101.2 1.9 %copy-start.4 = (f32[256,1024]{1,0:T(8,128)S(1)}, f32[256,1024]{1,0:T(8,128)}, u32[]{:S(2)}) copy-start(f32[256,1024]{1,0:T(8,128)} %copy-done.3) | copy-start | bytes 3145732
  128.9 28.2 %all-to-all-start.4 = ((f32[8,408,128]{2,1,0:T(8,128)}), f32[8,408,128]{2,1,0:T(8,128)S(1)}, u32[]{:S(2)}, u32[]{:S(2)}) async-start(f32[8,408,128]{2,1,0:T(8,128)} %broadcast_dynamic-update-slice_fusion), calls=%async_computation.4 | async-start | bytes 3342336 | tf_op jit(solution)/shard_map/all_to_all | solution.py:432
  (3 other events, 2.4 us)

commit v3 on v2

v3 whole, which is shorter than its diff:
```python
import functools

import jax
import jax.numpy as jnp
from jax import lax
from jax.experimental import pallas as pl
from jax.experimental.pallas import tpu as pltpu
from jax.sharding import PartitionSpec as P

BLK = 128
BLK_DEV = 2
SLOTS = 32
ACTS = 4
F32 = jnp.float32
BF16 = jnp.bfloat16
I16 = jnp.int16
HIGH = lax.Precision.HIGHEST
YS = 4
ZS = 8
OWN = YS * ZS
GRP = 8
SL = BLK // GRP
ROWS = BLK_DEV * SL
SIZE = BLK_DEV * BLK
NB = BLK_DEV * OWN
KACT = BLK_DEV * ACTS
Y_ORDER = (0, -1, 1, 2)
PARAMS = pltpu.CompilerParams(vmem_limit_bytes=16 * 1024 * 1024)
WIDE = pltpu.CompilerParams(vmem_limit_bytes=28 * 1024 * 1024)


def y_shift(x, k):
    return lax.ppermute(x, "var", [(i, (i + ZS * k) % OWN) for i in range(OWN)])


def z_shift(x, k):
    return lax.ppermute(
        x, "var", [(i, (i // ZS) * ZS + (i % ZS + k) % ZS) for i in range(OWN)]
    )


def z_across(x):
    pairs = []
    for s in range(GRP):
        for i in range(OWN):
            k = 1 if s % 2 == 0 else -1
            pairs.append((s * OWN + i, s * OWN + (i // ZS) * ZS + (i % ZS + k) % ZS))
    return lax.ppermute(x, ("samp", "var"), pairs)


def whole(shape, dtype):
    return jax.ShapeDtypeStruct(shape, dtype)


def vmem_spec():
    return pl.BlockSpec(memory_space=pltpu.VMEM)


def smem_spec():
    return pl.BlockSpec(memory_space=pltpu.SMEM)


def scale_of(e):
    return jnp.exp2(e.astype(F32) - 15.0)


def code(x, axis):
    most = jnp.max(jnp.abs(x), axis=axis, keepdims=True)
    e = jnp.floor(jnp.log2(jnp.maximum(most, 1e-30))) + 1.0
    q = jnp.floor(x * jnp.exp2(15.0 - e) + 0.5)
    q = jnp.minimum(jnp.maximum(q, -32767.0), 32767.0)
    return q.astype(jnp.int32).astype(I16), e


def value(q):
    return q.astype(jnp.int32).astype(F32)


def spread(diag_ref):
    full = [jnp.broadcast_to(diag_ref[r : r + 1, :], (BLK, BLK)).T for r in range(BLK_DEV)]
    return jnp.concatenate(full, axis=0)


X_ROWS = BLK_DEV * ROWS
S_ROWS = 16
CHUNK = X_ROWS + S_ROWS + 16


def prep_kernel(meta, v_ref, smp_ref, out_ref, rows_ref, acc, exps):
    acc[...] = jnp.zeros_like(acc)
    exps[...] = jnp.zeros_like(exps)
    for r in range(BLK_DEV):

        def body(e, carry):
            @pl.when(e < meta[1 + r])
            def _():
                c = meta[1 + BLK_DEV + GRP + r * SLOTS + e]
                at = pl.multiple_of((c % BLK_DEV) * ROWS + r * SL, SL)
                acc[c // BLK_DEV, pl.ds(at, SL), :] += v_ref[r * SLOTS + e]

            return carry

        lax.fori_loop(0, SLOTS, body, 0)
    for c in range(BLK_DEV):
        q, e = code(acc[:, c * ROWS : (c + 1) * ROWS, :], 1)
        out_ref[:, c * ROWS : (c + 1) * ROWS, :] = q
        exps[:, c : c + 1, :] = e
    few = S_ROWS // BLK_DEV
    smp = smp_ref[...].astype(F32)
    parts = []
    for c in range(BLK_DEV):
        q, e = code(smp[:, c * few : (c + 1) * few], 1)
        parts.append(value(q))
        exps[:, BLK_DEV + c : BLK_DEV + c + 1, :] = e
    smp = jnp.concatenate(parts, axis=1).astype(jnp.int32)
    out_ref[:, X_ROWS : X_ROWS + S_ROWS, :] = smp.astype(I16)
    out_ref[:, X_ROWS + S_ROWS : CHUNK, :] = exps[...].astype(jnp.int32).astype(I16)
    for p in range(GRP):
        b = meta[1 + BLK_DEV + p]
        at = pl.multiple_of((b % BLK_DEV) * ROWS, ROWS)
        rows_ref[:, p * BLK : (p + 1) * BLK] = acc[b // BLK_DEV, pl.ds(at, ROWS), :]


def prep(meta, theta_vals, smp):
    return pl.pallas_call(
        prep_kernel,
        in_specs=[smem_spec()] + [vmem_spec()] * 2,
        out_specs=[vmem_spec()] * 2,
        out_shape=[whole((OWN, CHUNK, BLK), I16), whole((ROWS, GRP * BLK), F32)],
        scratch_shapes=[
            pltpu.VMEM((OWN, X_ROWS, BLK), F32),
            pltpu.VMEM((OWN, 16, BLK), F32),
        ],
        compiler_params=PARAMS,
    )(meta, theta_vals, smp)


def pick_kernel(pan, got_ref, out_ref, smp_ref, exp_ref):
    exps = []
    for p in range(GRP):
        e = value(got_ref[pan[p] // BLK_DEV, X_ROWS + S_ROWS : CHUNK, :])
        exps.append(e)
        r = pan[p] % BLK_DEV
        exp_ref[p : p + 1, :] = jnp.where(r == 0, e[2:3], e[3:4])
    for c in range(BLK_DEV):
        stack = []
        for p in range(GRP):
            b = pan[p]
            at = pl.multiple_of(c * ROWS + (b % BLK_DEV) * SL, SL)
            q = value(got_ref[b // BLK_DEV, pl.ds(at, SL), :])
            stack.append(q * scale_of(exps[p][c : c + 1]))
        turned = jnp.concatenate(stack, axis=0).T
        for g in range(GRP):
            out_ref[g, c * SL : (c + 1) * SL, :] = turned[g * SL : (g + 1) * SL]
    few = []
    for p in range(GRP):
        b = pan[p]
        x = value(got_ref[b // BLK_DEV, X_ROWS : X_ROWS + S_ROWS, :])
        few.append(jnp.where(b % BLK_DEV == 0, x[:8], x[8:]))
    smp_ref[...] = jnp.concatenate(few, axis=0)


def pick(pan, got):
    return pl.pallas_call(
        pick_kernel,
        in_specs=[smem_spec(), vmem_spec()],
        out_specs=[vmem_spec()] * 3,
        out_shape=[
            whole((GRP, ROWS, BLK), F32),
            whole((GRP * 8, BLK), F32),
            whole((GRP, BLK), F32),
        ],
        compiler_params=PARAMS,
    )(pan, got)


U_ROWS = GRP * ROWS
F_ROWS = GRP * 8
RING = U_ROWS + F_ROWS + 2 * GRP
OWN_ROWS = U_ROWS + 2 * GRP


def slice_kernel(
    meta, turned_ref, rows_ref, smp_ref, exp_ref, ring_ref, e_ref, own_ref, exps, own_exps
):
    lane = lax.broadcasted_iota(jnp.int32, (ROWS, BLK), 1)
    row = lax.broadcasted_iota(jnp.int32, (ROWS, BLK), 0)
    in_block = meta[1] * SL + row % SL
    for p in range(GRP):
        e = rows_ref[:, p * BLK : (p + 1) * BLK]
        for g in range(GRP):
            moved = turned_ref[g]
            if g != p:
                moved = pltpu.roll(moved, ((g - p) * SL) % BLK, 1)
            e = e + jnp.where(lane // SL == g, moved, 0.0)
        e_ref[p] = e
        q, x = code(e, 0)
        own_ref[p * ROWS : (p + 1) * ROWS, :] = q
        own_exps[p : p + 1, :] = x
        hit = (meta[2] * BLK_DEV + row // SL == meta[3 + p]) & (in_block == lane)
        q, e = code(jnp.where(hit, 0.0, e), 0)
        ring_ref[p * ROWS : (p + 1) * ROWS, :] = q
        exps[p : p + 1, :] = e
    own_exps[GRP : 2 * GRP, :] = jnp.zeros((GRP, BLK), F32)
    own_ref[U_ROWS:, :] = own_exps[...].astype(jnp.int32).astype(I16)
    exps[GRP : 2 * GRP, :] = exp_ref[...]
    ring_ref[U_ROWS : U_ROWS + F_ROWS, :] = smp_ref[...].astype(jnp.int32).astype(I16)
    ring_ref[U_ROWS + F_ROWS :, :] = exps[...].astype(jnp.int32).astype(I16)


def u_slices(meta, turned, from_rows, smp, smp_exp):
    return pl.pallas_call(
        slice_kernel,
        in_specs=[smem_spec()] + [vmem_spec()] * 4,
        out_specs=[vmem_spec()] * 3,
        out_shape=[
            whole((RING, BLK), I16),
            whole((GRP, ROWS, BLK), F32),
            whole((OWN_ROWS, BLK), I16),
        ],
        scratch_shapes=[pltpu.VMEM((2 * GRP, BLK), F32)] * 2,
        compiler_params=PARAMS,
    )(meta, turned, from_rows, smp, smp_exp)


def theta_kernel(meta, got_ref, own_ref, hi_ref, lo_ref):
    for z in range(ZS):
        stack = []
        for dy in Y_ORDER:
            i = ((meta[0] + dy + YS) % YS) * ZS + z
            sc = scale_of(value(got_ref[i, X_ROWS + S_ROWS : CHUNK, :]))
            cols = []
            for c in range(BLK_DEV):
                q = value(got_ref[i, c * ROWS : (c + 1) * ROWS, :])
                cols.append(q * sc[c : c + 1])
            stack.append(jnp.concatenate(cols, axis=1) + own_ref[i])
        x = jnp.concatenate(stack, axis=0).T
        hi = x.astype(BF16)
        lo = (x - hi.astype(F32)).astype(BF16)
        hi_ref[z] = jnp.concatenate([hi, hi], axis=1)
        lo_ref[z] = jnp.concatenate([lo, lo], axis=1)


def theta_parts(meta, got, own):
    return pl.pallas_call(
        theta_kernel,
        in_specs=[smem_spec()] + [vmem_spec()] * 2,
        out_specs=[vmem_spec()] * 2,
        out_shape=[whole((ZS, SIZE, 2 * YS * ROWS), BF16)] * 2,
        compiler_params=PARAMS,
        cost_estimate=pl.CostEstimate(flops=0, bytes_accessed=6_000_000, transcendentals=0),
    )(meta, got, own)


def products(groups, mats):
    his, los, fews, lhs_hi, lhs_lo, lhs_few = [], [], [], [], [], []
    for refs, (a_hi, a_lo, left) in zip(groups, mats):
        hi, lo = [], []
        for ref in refs:
            for m in range(ref.shape[0] // RING):
                at = m * RING
                sc = scale_of(value(ref[at + U_ROWS + F_ROWS : at + RING, :]))
                u = jnp.concatenate(
                    [
                        value(ref[at + p * ROWS : at + (p + 1) * ROWS, :]) * sc[p : p + 1]
                        for p in range(GRP)
                    ],
                    axis=1,
                )
                head = u.astype(BF16)
                hi.append(head)
                lo.append((u - head.astype(F32)).astype(BF16))
                few = value(ref[at + U_ROWS : at + U_ROWS + F_ROWS, :])
                few = [
                    few[p * 8 : (p + 1) * 8] * sc[GRP + p : GRP + p + 1] for p in range(GRP)
                ]
                fews.append(jnp.concatenate(few, axis=1))
        his += hi + lo
        lhs_hi.append(a_hi[0])
        lhs_lo.append(a_lo[0])
        lhs_few.append(left[0])
    u = jnp.concatenate(his, axis=0)
    w = jnp.dot(jnp.concatenate(lhs_hi, axis=1), u, preferred_element_type=F32)
    w = w + jnp.dot(jnp.concatenate(lhs_lo, axis=1), u, preferred_element_type=F32)
    g = lax.dot_general(
        jnp.concatenate(lhs_few, axis=0).astype(BF16),
        jnp.concatenate(fews, axis=0).astype(BF16),
        (((0,), (0,)), ((), ())),
        preferred_element_type=F32,
    )
    return w, g


G_ROWS = KACT * SL
E_AT = SIZE + G_ROWS
T_AT = E_AT + 16
BUNDLE = T_AT + 48


def grouped(n, refs):
    groups = [[ref] for ref in refs[:n]]
    mats = [refs[n + 3 * i : n + 3 * i + 3] for i in range(n)]
    return groups, mats, refs[4 * n :]


def early_kernel(n, meta, *refs):
    groups, mats, (w_ref, g_ref) = grouped(n, refs)
    w_ref[...], g_ref[...] = products(groups, mats)


def last_kernel(n, meta, *refs):
    groups, mats, rest = grouped(n, refs)
    w_in, g_in, e_ref, diag_ref, out_ref, tiny_ref, u_ref, g_by, u_by, d_by, s2_by = rest
    w_all, g_all = products(groups, mats)
    lane = lax.broadcasted_iota(jnp.int32, (SIZE, BLK), 1)
    row = lax.broadcasted_iota(jnp.int32, (SIZE, BLK), 0)
    in_block = row % BLK
    block = meta[2] * BLK_DEV + row // BLK
    diag = spread(diag_ref)
    mine = jnp.where(in_block // SL == meta[1], diag, 0.0)
    tail = jnp.zeros((14, BLK), F32)
    exps = []
    e_sc = [scale_of(value(e_ref[g, U_ROWS:OWN_ROWS, :])) for g in range(GRP)]
    for p in range(GRP):
        cols = slice(p * BLK, (p + 1) * BLK)
        w = w_in[:, cols] + w_all[:, cols]
        e = jnp.concatenate(
            [
                value(e_ref[g, p * ROWS + r * SL : p * ROWS + (r + 1) * SL, :]) * e_sc[g][p : p + 1]
                for r in range(BLK_DEV)
                for g in range(GRP)
            ],
            axis=0,
        )
        hit = (block == meta[3 + p]) & (in_block == lane)
        u = jnp.where(hit, 0.0, e)
        u_by[p] = u
        d_by[p : p + 1, :] = jnp.sum(jnp.where(hit, e + diag, 0.0), axis=0, keepdims=True)
        s2_by[p : p + 1, :] = jnp.sum(u * u, axis=0, keepdims=True)
        tiny_ref[p : p + 1, :] = jnp.sum(u * (w + mine * u), axis=0, keepdims=True)
        q, x = code(w, 0)
        out_ref[p, 0:SIZE, :] = q
        exps.append(x)
        g_by[p] = g_in[:, cols] + g_all[:, cols]
    own = meta[1]
    u_ref[...] = u_by[own]
    tiny_ref[GRP : GRP + 1, :] = s2_by[pl.ds(own, 1), :]
    tiny_ref[GRP + 1 : GRP + 2, :] = d_by[pl.ds(own, 1), :]
    tiny_ref[GRP + 2 :, :] = jnp.zeros((GRP - 2, BLK), F32)
    active = []
    for k in range(KACT):
        r = k // ACTS
        active.append(g_by[meta[3 + GRP + k], r * BLK : (r + 1) * BLK, :])
    for g in range(GRP):
        x = jnp.concatenate([v[g * SL : (g + 1) * SL] for v in active], axis=0)
        q, x = code(x, 0)
        out_ref[g, SIZE:E_AT, :] = q
        x = jnp.concatenate([exps[g], x, tail], axis=0)
        out_ref[g, E_AT:T_AT, :] = x.astype(jnp.int32).astype(I16)
    out_ref[:, T_AT:, :] = jnp.zeros((GRP, 48, BLK), I16)


def full_spec(shape):
    return pl.BlockSpec(shape, lambda i, m: (0,) * len(shape))


def z_spec(x, dz):
    return pl.BlockSpec((1,) + x.shape[1:], lambda i, m: ((m[0] + dz + ZS) % ZS, 0, 0))


def grouped_call(kernel, meta, theta, left, groups, extra, out_shape, scratch, flops):
    args, specs = [], []
    for _, part in groups:
        args.append(part)
        specs.append(full_spec(part.shape))
    for dz, _ in groups:
        for x in (*theta, left):
            args.append(x)
            specs.append(z_spec(x, dz))
    for x in extra:
        args.append(x)
        specs.append(full_spec(x.shape))
    grid_spec = pltpu.PrefetchScalarGridSpec(
        num_scalar_prefetch=1,
        grid=(1,),
        in_specs=specs,
        out_specs=[full_spec(x.shape) for x in out_shape],
        scratch_shapes=scratch,
    )
    return pl.pallas_call(
        functools.partial(kernel, len(groups)),
        grid_spec=grid_spec,
        out_shape=out_shape,
        compiler_params=WIDE,
        cost_estimate=pl.CostEstimate(
            flops=flops, bytes_accessed=len(groups) * 3_000_000, transcendentals=0
        ),
    )(meta, *args)


def early_products(meta, theta, left, groups):
    flops = len(groups) * 2 * 2 * SIZE * SIZE * GRP * BLK
    out_shape = [whole((SIZE, GRP * BLK), F32)] * 2
    return grouped_call(early_kernel, meta, theta, left, groups, [], out_shape, [], flops)


def last_products(meta, theta, left, groups, before, e_rows, diag):
    flops = len(groups) * 2 * 2 * SIZE * SIZE * GRP * BLK
    out_shape = [
        whole((GRP, BUNDLE, BLK), I16),
        whole((2 * GRP, BLK), F32),
        whole((SIZE, BLK), F32),
    ]
    scratch = [pltpu.VMEM((GRP, SIZE, BLK), F32)] * 2 + [pltpu.VMEM((GRP, BLK), F32)] * 2
    extra = [*before, e_rows, diag]
    return grouped_call(last_kernel, meta, theta, left, groups, extra, out_shape, scratch, flops)


def scalar_kernel(tiny_ref, out_ref):
    x = tiny_ref[0]
    for i in range(1, OWN):
        x = x + tiny_ref[i]
    e = jnp.floor(jnp.log2(jnp.maximum(jnp.abs(x), 1e-30))) + 2.0
    x = x * jnp.exp2(15.0 - e)
    hi = jnp.floor(x)
    lo = jnp.floor((x - hi) * 32768.0)
    x = jnp.concatenate([hi, lo, e], axis=0)
    out_ref[...] = x.astype(jnp.int32).astype(I16)


def scalar_rows(tiny):
    return pl.pallas_call(
        scalar_kernel,
        in_specs=[vmem_spec()],
        out_specs=vmem_spec(),
        out_shape=whole((48, BLK), I16),
        compiler_params=PARAMS,
    )(tiny)


def finish_kernel(
    count, meta, bundle_ref, u_ref, diag_ref, e_ref, inv_ref, res_ref, grad_ref, ct_ref, cu_ref, cr_ref
):
    w, gram, q, s2, d = 0.0, 0.0, 0.0, [], []
    for g in range(GRP):
        sc = scale_of(value(bundle_ref[g, E_AT:T_AT, :]))
        w = w + value(bundle_ref[g, 0:SIZE, :]) * sc[0:1]
        gram = gram + value(bundle_ref[g, SIZE:E_AT, :]) * sc[1:2]
        x = value(bundle_ref[g, T_AT:BUNDLE, :])
        x = (x[0:16] + x[16:32] * (1.0 / 32768.0)) * scale_of(x[32:48])
        q = q + x[0:GRP]
        s2.append(x[GRP : GRP + 1])
        d.append(x[GRP + 1 : GRP + 2])
    s2 = jnp.concatenate(s2, axis=0)
    d = jnp.concatenate(d, axis=0)
    alpha1 = 1.0 / d
    rr = s2 * alpha1 * alpha1
    alpha2 = s2 / (q - alpha1 * s2 * s2)
    ct_ref[...] = alpha1 + alpha2 * rr
    cu_ref[...] = alpha1 * alpha2
    cr_ref[...] = alpha2 * rr * d

    own = pl.ds(meta[1], 1)
    lane = lax.broadcasted_iota(jnp.int32, (SIZE, BLK), 1)
    row = lax.broadcasted_iota(jnp.int32, (SIZE, BLK), 0)
    hit = (meta[2] * BLK_DEV + row // BLK == meta[3 + meta[1]]) & (row % BLK == lane)
    u = u_ref[...]
    w = w + spread(diag_ref) * u
    c_t, c_u, c_r = ct_ref[own, :], cu_ref[own, :], cr_ref[own, :]
    inv_ref[...] = jnp.where(hit, c_t, 0.0) - c_u * u
    res_ref[...] = c_u * w - c_t * u - jnp.where(hit, c_r, 0.0)

    lane = lax.broadcasted_iota(jnp.int32, (SL, BLK), 1)
    row = lax.broadcasted_iota(jnp.int32, (SL, BLK), 0)
    for k in range(KACT):
        p, r = meta[3 + GRP + k], k // ACTS
        e = e_ref[p, r * SL : (r + 1) * SL, :]
        hit = (meta[2] * BLK_DEV + r == meta[3 + p]) & (meta[1] * SL + row == lane)
        part = jnp.where(hit, ct_ref[pl.ds(p, 1), :], -cu_ref[pl.ds(p, 1), :] * e)
        grad_ref[k] = gram[k * SL : (k + 1) * SL] * (1.0 / count) - part


def finish(count, meta, bundle, u, diag, e_slice):
    return pl.pallas_call(
        functools.partial(finish_kernel, count),
        in_specs=[smem_spec()] + [vmem_spec()] * 4,
        out_specs=[vmem_spec()] * 3,
        out_shape=[
            whole((SIZE, BLK), F32),
            whole((SIZE, BLK), F32),
            whole((KACT, SL, BLK), F32),
        ],
        scratch_shapes=[pltpu.VMEM((GRP, BLK), F32)] * 3,
        compiler_params=PARAMS,
    )(meta, bundle, u, diag, e_slice)


def per_device(samples, theta_diag, theta_vals, theta_cols, theta_count, panel_blocks, act_pan):
    j = lax.axis_index("var")
    s = lax.axis_index("samp")
    y, z = j // ZS, j % ZS
    count_rows = samples.shape[0]
    few = count_rows // OWN
    columns = theta_cols[:, 0]
    diag = theta_diag.reshape(BLK_DEV, BLK)

    meta = jnp.concatenate([s[None], theta_count, panel_blocks, columns])
    smp = samples.reshape(OWN, few, BLK_DEV, BLK).transpose(0, 2, 1, 3)
    row_slice = lax.dynamic_slice_in_dim(theta_vals, s * SL, SL, 1)
    chunks, from_rows = prep(meta, row_slice, smp.reshape(OWN, BLK_DEV * few, BLK))
    got = lax.all_to_all(chunks, "var", 0, 0)

    match = (columns.reshape(BLK_DEV, 1, SLOTS) == jnp.arange(NB)[None, :, None]) & (
        jnp.arange(SLOTS)[None, None, :] < theta_count[:, None, None]
    )
    vals = theta_vals.reshape(BLK_DEV, SLOTS, BLK, BLK)
    col_slice = lax.dynamic_slice_in_dim(vals, s * SL, SL, 3)
    own = jnp.einsum("rce,remk->ckrm", match.astype(F32), col_slice, precision=HIGH)
    own = own.reshape(OWN, ROWS, SIZE)
    left = samples.reshape(YS, ZS, few, SIZE)[(y + jnp.array(Y_ORDER)) % YS]
    left = left.transpose(1, 0, 2, 3).reshape(ZS, YS * few, SIZE).astype(F32)
    got, own, left = lax.optimization_barrier((got, own, left))

    turned, few_cols, few_exps = pick(panel_blocks, got)
    turned = lax.all_to_all(turned, "samp", 0, 0)
    place = jnp.concatenate([z[None], s[None], j[None], panel_blocks, act_pan])
    ring, e_slice, e_sent = u_slices(place, turned, from_rows, few_cols, few_exps)

    e_rows = lax.all_to_all(jnp.broadcast_to(e_sent[None], (GRP, OWN_ROWS, BLK)), "samp", 0, 0)

    block = jnp.concatenate([ring, y_shift(ring, 1), y_shift(ring, -1), y_shift(ring, 2)])
    groups = [(0, block)]
    down = up = block
    for step in range(1, 4):
        if step == 3:
            down, up, e_rows = lax.optimization_barrier((down, up, e_rows))
        down, up = z_shift(down, 1), z_shift(up, -1)
        groups += [(-step, down), (step, up)]

    theta = theta_parts(y[None], got, own)
    sums = early_products(place, theta, left, groups[:5])
    across = z_across(jnp.where(s % 2 == 0, down, up))
    groups = [(-3, down), (3, up), (4, across)]
    bundle, tiny, u = last_products(place, theta, left, groups, sums, e_rows, diag)

    tiny = lax.all_to_all(jnp.broadcast_to(tiny[None], (OWN, 2 * GRP, BLK)), "var", 0, 0)
    tiny = scalar_rows(tiny)
    bundle = bundle.at[:, T_AT:].set(jnp.broadcast_to(tiny[None], (GRP, 48, BLK)))
    bundle = lax.all_to_all(bundle, "samp", 0, 0)
    return tuple(finish(float(count_rows * GRP), place, bundle, u, diag, e_slice))


def solution(mesh):
    in_specs = (
        P("samp", "var"),
        P("var"),
        P("var", None, None),
        P("var", None),
        P("var"),
        P(),
        P("var"),
    )
    out_specs = (P("var", "samp"), P("var", "samp"), P("var", "samp", None))
    return jax.shard_map(
        per_device, mesh=mesh, in_specs=in_specs, out_specs=out_specs, check_vma=False
    )
```

time: 162 us -> 142 us (0.88)
  waiting for transfers between devices: 52 us -> 35.4 us
  blocking collectives: 20.3 us -> 36.2 us
  local copies, waits for them, and re-layouts: 25.7 us -> 16.8 us
  starting transfers between devices: 41.8 us -> 34.9 us
  other arithmetic: 3.69 us -> 1.63 us
    all_to_all x2 -> x1, waiting for transfers between devices: 21.1 us -> 4.28 us  [per_device(): lax.all_to_all(jnp.broadcast_to(e_sent[None], (GRP, OWN_ROWS, BLK)), 'sam...]
    all_to_all x1 -> x2, blocking collectives: 20.3 us -> 36.2 us  [the longest x1 20.1 us: per_device(): bundle = lax.all_to_all(bundle, 'samp', 0, 0)]
    all_to_all x2 -> x1, starting transfers between devices: 9.79 us -> 3.54 us  [per_device(): lax.all_to_all(jnp.broadcast_to(e_sent[None], (GRP, OWN_ROWS, BLK)), 'sam...]
    unnamed x46 -> x29, local copies, waits for them, and re-layouts: 11.4 us -> 7.08 us
    ppermute x0 -> x1, waiting for transfers between devices: none -> 2.69 us  [z_across(): return lax.ppermute(x, ('samp', 'var'), pairs)]
    ppermute x8 -> x6, waiting for transfers between devices: 12.5 us -> 9.96 us  [z_shift(): lax.ppermute(x, 'var', [(i, i // ZS * ZS + (i % ZS + k) % ZS) for i in ra...]
    slice x2 -> x0, local copies, waits for them, and re-layouts: 1.86 us -> none  [ring_parts(): parts += [(4, z_shift(left[:h], 1)), (4, z_shift(right[h:], -1))]]
    ppermute x8 -> x6, starting transfers between devices: 11.1 us -> 10.2 us  [z_shift(): lax.ppermute(x, 'var', [(i, i // ZS * ZS + (i % ZS + k) % ZS) for i in ra...]
  transfers between devices with their start and end apart: 15 -> 13, of which waited for: 10 -> 11; matrix products, arithmetic and copies ran while one was open for 11% -> 10% of each run, Pallas kernels for 3% -> 3%
where the time goes in v3:
time: 142 us; the launch traced here: 140 us
  blocking collectives  36.2 us (25%)
  waiting for transfers between devices  35.4 us (25%)
  starting transfers between devices  34.9 us (25%)
  local copies, waits for them, and re-layouts  16.8 us (12%)
  Pallas kernels  13.6 us (10%)
  other arithmetic  1.63 us (1%)
    all_to_all x1, blocking collectives, per_device(): bundle = lax.all_to_all(bundle, 'samp', 0, 0)  20.1 us
    all_to_all x1, blocking collectives, per_device(): lax.all_to_all(jnp.broadcast_to(tiny[None], (OWN, 2 * GRP, BLK)), 'var',...  16 us
    all_to_all x1, starting transfers between devices, per_device(): got = lax.all_to_all(chunks, 'var', 0, 0)  11.8 us
    ppermute x6, starting transfers between devices, z_shift(): lax.ppermute(x, 'var', [(i, i // ZS * ZS + (i % ZS + k) % ZS) for i in ra...  10.2 us
    ppermute x6, waiting for transfers between devices, z_shift(): lax.ppermute(x, 'var', [(i, i // ZS * ZS + (i % ZS + k) % ZS) for i in ra...  9.96 us
    all_to_all x1, waiting for transfers between devices, per_device(): got = lax.all_to_all(chunks, 'var', 0, 0)  8.19 us
    unnamed x29, local copies, waits for them, and re-layouts  7.08 us
    all_to_all x1, waiting for transfers between devices, per_device(): turned = lax.all_to_all(turned, 'samp', 0, 0)  6.05 us
  transfers between devices with their start and end apart: 13, of which 11 were waited for; matrix products, arithmetic and copies ran while one was open for 10% of the time, Pallas kernels for 3%

profile of v3, /device:TPU:8, one launch (start us, length us, event | category | flops | bytes accessed | tf_op | source)
XLA Modules:
  0.0 140.0 jit_solution(10261565709480038207)
XLA Ops:
  0.6 1.1 constant_dynamic-slice_fusion.1.v_ref
  2.5 0.9 copy-done.2
  3.4 3.5 %shard_map.103 = (s16[32,96,128]{2,1,0:T(8,128)(2,1)}, f32[32,1024]{1,0:T(8,128)S(1)}) custom-call(s32[75]{0:T(128)S(1)} %pad_add_fusion.meta, f32[64,16,128]{2,1,0:T(8,128)S(1)} %constant_dynamic-slice_fusion.1.v_ref, bf16[32,16,128]{2,1,0:T(8,128)(2,1)S(1)} %bitcast.27), custom_call_target="tpu_custom_call" | custom-call | tf_op jit(solution)/shard_map/pallas_call | solution.py:125
  6.9 11.8 %all-to-all-start = ((s16[32,96,128]{2,1,0:T(8,128)(2,1)}), s16[32,96,128]{2,1,0:T(8,128)(2,1)S(1)}, u32[]{:S(2)}, u32[]{:S(2)}) async-start(s16[32,96,128]{2,1,0:T(8,128)(2,1)} %get-tuple-element.36), calls=%async_computation | async-start | bytes 1572864 | tf_op jit(solution)/shard_map/all_to_all | solution.py:511
  18.7 5.3 %constant_dynamic-slice_fusion = f32[2,32,128,16]{3,2,1,0:T(8,128)} fusion(f32[2,32,128,128]{3,2,1,0:T(8,128)} %bitcast.31, s32[]{:T(128)S(6)} %select_n.37), kind=kLoop, calls=%fused_computation.21 | loop fusion | bytes 1048580 | tf_op jit(solution)/shard_map/dynamic_slice | solution.py:517
  24.0 2.9 %copy.16 = f32[2,32,128,16]{2,1,3,0:T(8,128)S(1)} copy(f32[2,32,128,16]{3,2,1,0:T(8,128)} %constant_dynamic-slice_fusion) | data formatting | bytes 1048576
  31.3 8.2 %all-to-all-done.got_ref = s16[32,96,128]{2,1,0:T(8,128)(2,1)S(1)} async-done(((s16[32,96,128]{2,1,0:T(8,128)(2,1)}), s16[32,96,128]{2,1,0:T(8,128)(2,1)S(1)}, u32[]{:S(2)}, u32[]{:S(2)}) %all-to-all-start) | async-done | bytes 786464 | tf_op jit(solution)/shard_map/all_to_all | solution.py:511
  39.5 1.4 shard_map.104
  40.9 4.3 %all-to-all-start.1 = ((f32[8,32,128]{2,1,0:T(8,128)}), f32[8,32,128]{2,1,0:T(8,128)S(1)}, u32[]{:S(2)}, u32[]{:S(2)}) async-start(f32[8,32,128]{2,1,0:T(8,128)} %get-tuple-element.38), calls=%async_computation.1 | async-start | bytes 262144 | tf_op jit(solution)/shard_map/all_to_all | solution.py:525
  45.2 6.1 %all-to-all-done.1.turned_ref = f32[8,32,128]{2,1,0:T(8,128)S(1)} async-done(((f32[8,32,128]{2,1,0:T(8,128)}), f32[8,32,128]{2,1,0:T(8,128)S(1)}, u32[]{:S(2)}, u32[]{:S(2)}) %all-to-all-start.1) | async-done | bytes 131104 | tf_op jit(solution)/shard_map/all_to_all | solution.py:525
  51.3 0.9 shard_map.105
  52.2 1.6 %collective-permute-start = (s16[336,128]{1,0:T(8,128)(2,1)S(1)}, s16[336,128]{1,0:T(8,128)(2,1)S(1)}, u32[]{:S(2)}, u32[]{:S(2)}) collective-permute-start(s16[336,128]{1,0:T(8,128)(2,1)S(1)} %get-tuple-element.42), channel_id=1, source_target_pairs={{0,8},{1,9},{2,10},{3,11},{4,12},{5,13},{6,14},{7,15},{8,16},{9,17... | collective-permute-start | bytes 258056 | tf_op jit(solution)/shard_map/ppermute | solution.py:33
  53.8 1.4 collective-permute-start.1
  55.2 2.0 %collective-permute-start.2 = (s16[336,128]{1,0:T(8,128)(2,1)S(1)}, s16[336,128]{1,0:T(8,128)(2,1)S(1)}, u32[]{:S(2)}, u32[]{:S(2)}) collective-permute-start(s16[336,128]{1,0:T(8,128)(2,1)S(1)} %get-tuple-element.42), channel_id=1, source_target_pairs={{0,16},{1,17},{2,18},{3,19},{4,20},{5,21},{6,22},{7,23},{8,24},{9,... | collective-permute-start | bytes 258056 | tf_op jit(solution)/shard_map/ppermute | solution.py:33
  58.3 3.1 %collective-permute-done.2 = s16[336,128]{1,0:T(8,128)(2,1)S(1)} collective-permute-done((s16[336,128]{1,0:T(8,128)(2,1)S(1)}, s16[336,128]{1,0:T(8,128)(2,1)S(1)}, u32[]{:S(2)}, u32[]{:S(2)}) %collective-permute-start.2) | collective-permute-done | bytes 86048 | tf_op jit(solution)/shard_map/ppermute | solution.py:33
  61.4 1.9 %collective-permute-start.3 = (s16[1344,128]{1,0:T(8,128)(2,1)S(1)}, s16[1344,128]{1,0:T(8,128)(2,1)S(1)}, u32[]{:S(2)}, u32[]{:S(2)}) collective-permute-start(s16[1344,128]{1,0:T(8,128)(2,1)S(1)} %constant_dynamic-update-slice_fusion.refs_0_), channel_id=1, source_target_pairs={{0,1},{1,2},{2,3},{3,4},{4,5},{5,6},{6,7},{7,0},{8,9},{9,10},{10,1... | collective-permute-start | bytes 1032200 | tf_op jit(solution)/shard_map/ppermute | solution.py:37
  63.3 1.4 collective-permute-start.5
  65.6 3.5 %all-to-all-start.2 = ((s16[8,272,128]{2,1,0:T(8,128)(2,1)}), s16[8,272,128]{2,1,0:T(8,128)(2,1)S(1)}, u32[]{:S(2)}, u32[]{:S(2)}) async-start(s16[8,272,128]{2,1,0:T(8,128)(2,1)} %broadcast_in_dim.18), calls=%async_computation.2 | async-start | bytes 1114112 | tf_op jit(solution)/shard_map/all_to_all | solution.py:529
  69.1 2.4 %collective-permute-done.3.refs_1_ = s16[1344,128]{1,0:T(8,128)(2,1)S(1)} collective-permute-done((s16[1344,128]{1,0:T(8,128)(2,1)S(1)}, s16[1344,128]{1,0:T(8,128)(2,1)S(1)}, u32[]{:S(2)}, u32[]{:S(2)}) %collective-permute-start.3) | collective-permute-done | bytes 344096 | tf_op jit(solution)/shard_map/ppermute | solution.py:37
  72.7 2.8 %collective-permute-start.6 = (s16[1344,128]{1,0:T(8,128)(2,1)}, s16[1344,128]{1,0:T(8,128)(2,1)}, u32[]{:S(2)}, u32[]{:S(2)}) collective-permute-start(s16[1344,128]{1,0:T(8,128)(2,1)} %collective-permute-done.5.refs_2_), channel_id=1, source_target_pairs={{0,7},{1,0},{2,1},{3,2},{4,3},{5,4},{6,5},{7,6},{8,15},{9,8},{10,9... | collective-permute-start | bytes 1032200 | tf_op jit(solution)/shard_map/ppermute | solution.py:37
  75.5 4.3 %all-to-all-done.2.refs_14_ = s16[8,272,128]{2,1,0:T(8,128)(2,1)S(1)} async-done(((s16[8,272,128]{2,1,0:T(8,128)(2,1)}), s16[8,272,128]{2,1,0:T(8,128)(2,1)S(1)}, u32[]{:S(2)}, u32[]{:S(2)}) %all-to-all-start.2) | async-done | bytes 557088 | tf_op jit(solution)/shard_map/all_to_all | solution.py:529
  79.8 1.1 collective-permute-done.4.refs_3_
  81.2 3.5 %collective-permute-start.8 = (s16[1344,128]{1,0:T(8,128)(2,1)}, s16[1344,128]{1,0:T(8,128)(2,1)S(1)}, u32[]{:S(2)}, u32[]{:S(2)}) collective-permute-start(s16[1344,128]{1,0:T(8,128)(2,1)} %collective-permute-done.6.refs_4_), channel_id=1, source_target_pairs={{0,7},{1,0},{2,1},{3,2},{4,3},{5,4},{6,5},{7,6},{8,15},{9,8},{10,9... | collective-permute-start | bytes 1032200 | tf_op jit(solution)/shard_map/ppermute | solution.py:37
  84.7 6.3 %collective-permute-done.7.refs_0_ = s16[1344,128]{1,0:T(8,128)(2,1)S(1)} collective-permute-done((s16[1344,128]{1,0:T(8,128)(2,1)}, s16[1344,128]{1,0:T(8,128)(2,1)S(1)}, u32[]{:S(2)}, u32[]{:S(2)}) %collective-permute-start.7) | collective-permute-done | bytes 344096 | tf_op jit(solution)/shard_map/ppermute | solution.py:37
  91.6 1.0 copy-done.1
  92.6 1.0 copy-done.5
  93.6 3.4 %shard_map.107 = (f32[256,1024]{1,0:T(8,128)S(1)}, f32[256,1024]{1,0:T(8,128)S(1)}) custom-call(s32[19]{0:T(128)S(1)} %concatenate.11.meta, s16[1344,128]{1,0:T(8,128)(2,1)S(1)} %copy-done.1, s16[1344,128]{1,0:T(8,128)(2,1)S(1)} %copy-done.5, s16[1344,128]{1,0:T(8,128)(2,1)} %collective-permute-done.5.refs_2_, ...), custom_call_target="tpu_custom_call" | custom-call | flops 1342177280 | bytes 15000000 | tf_op jit(solution)/shard_map/pallas_call | solution.py:390
  97.0 2.7 %collective-permute-done.9.refs_2_ = s16[1344,128]{1,0:T(8,128)(2,1)S(1)} collective-permute-done((s16[1344,128]{1,0:T(8,128)(2,1)S(1)}, s16[1344,128]{1,0:T(8,128)(2,1)S(1)}, u32[]{:S(2)}, u32[]{:S(2)}) %collective-permute-start.9) | collective-permute-done | bytes 344096 | tf_op jit(solution)/shard_map/ppermute | solution.py:48
  99.7 2.5 %shard_map.108 = (s16[8,448,128]{2,1,0:T(8,128)(2,1)S(1)}, f32[16,128]{1,0:T(8,128)S(1)}, f32[256,128]{1,0:T(8,128)S(1)}) custom-call(s32[19]{0:T(128)S(1)} %concatenate.11.meta, s16[1344,128]{1,0:T(8,128)(2,1)S(1)} %collective-permute-done.7.refs_0_, s16[1344,128]{1,0:T(8,128)(2,1)S(1)} %collective-permute-done.8.refs_1_, ...), custom_call_target="tpu_custom_call" | custom-call | flops 805306368 | bytes 9000000 | tf_op jit(solution)/shard_map/pallas_call | solution.py:390
  102.3 16.0 %all_to_all.25.tiny_ref = f32[32,16,128]{2,1,0:T(8,128)S(1)} all-to-all(f32[32,16,128]{2,1,0:T(8,128)S(1)} %broadcast_in_dim.20), channel_id=1, replica_groups=mesh['samp'=8,'var'=32] {'var'}, dimensions={0} | all-to-all | bytes 524288 | tf_op jit(solution)/shard_map/all_to_all | solution.py:546
  118.4 20.1 %all_to_all.26.bundle_ref = s16[8,448,128]{2,1,0:T(8,128)(2,1)S(1)} all-to-all(s16[8,448,128]{2,1,0:T(8,128)(2,1)S(1)} %broadcast_dynamic-update-slice_fusion), channel_id=1, replica_groups=mesh['samp'=8,'var'=32] {'samp'}, dimensions={0} | all-to-all | bytes 1835008 | tf_op jit(solution)/shard_map/all_to_all | solution.py:549
  138.5 1.5 %shard_map.110 = (f32[256,128]{1,0:T(8,128)}, f32[256,128]{1,0:T(8,128)}, f32[8,16,128]{2,1,0:T(8,128)}) custom-call(s32[19]{0:T(128)S(1)} %concatenate.11.meta, s16[8,448,128]{2,1,0:T(8,128)(2,1)S(1)} %all_to_all.26.bundle_ref, f32[256,128]{1,0:T(8,128)S(1)} %get-tuple-element.55.u_ref, f32[2,128]{1,0:T(2,128)S(1)} %bitcast.30, ...), custom_call_target="tpu_custom_call" | custom-call | tf_op jit(solution)/shard_map/pallas_call | solution.py:484
  (52 shorter events, 9.4 us)
Async XLA Ops:
  2.5 0.9 copy-start.2
  6.9 32.6 %all-to-all-start = ((s16[32,96,128]{2,1,0:T(8,128)(2,1)}), s16[32,96,128]{2,1,0:T(8,128)(2,1)S(1)}, u32[]{:S(2)}, u32[]{:S(2)}) async-start(s16[32,96,128]{2,1,0:T(8,128)(2,1)} %get-tuple-element.36), calls=%async_computation | async-start | bytes 1572864 | tf_op jit(solution)/shard_map/all_to_all | solution.py:511
  24.0 3.5 %copy-start.8 = (s32[64,1]{0,1:T(1,128)S(1)}, s32[64,1]{0,1:T(1,128)}, u32[]{:S(2)}) copy-start(s32[64,1]{0,1:T(1,128)} %param.13) | copy-start | bytes 772
  24.0 4.2 %copy-start.9 = (s32[2]{0:T(128)S(1)}, s32[2]{0:T(128)}, u32[]{:S(2)}) copy-start(s32[2]{0:T(128)} %param.14) | copy-start | bytes 28
  24.0 6.7 %copy-start.11 = (s32[4]{0:T(128)S(1)}, s32[4]{0:T(128)}, u32[]{:S(2)}) copy-start(s32[4]{0:T(128)} %constant.94.clone) | copy-start | bytes 52
  24.0 6.7 %copy-start.3 = (bf16[256,256]{1,0:T(8,128)(2,1)S(1)}, bf16[256,256]{1,0:T(8,128)(2,1)}, u32[]{:S(2)}) copy-start(bf16[256,256]{1,0:T(8,128)(2,1)} %param.10) | copy-start | bytes 393220
  26.9 12.6 %copy-start.6 = (s32[8]{0:T(128)S(1)}, s32[8]{0:T(128)}, u32[]{:S(2)}) copy-start(s32[8]{0:T(128)} %pan.1) | copy-start | bytes 100
  26.9 18.2 %copy-start.10 = (s32[8]{0:T(128)S(1)}, s32[8]{0:T(128)}, u32[]{:S(2)}) copy-start(s32[8]{0:T(128)} %param.16) | copy-start | bytes 100
  40.9 10.4 %all-to-all-start.1 = ((f32[8,32,128]{2,1,0:T(8,128)}), f32[8,32,128]{2,1,0:T(8,128)S(1)}, u32[]{:S(2)}, u32[]{:S(2)}) async-start(f32[8,32,128]{2,1,0:T(8,128)} %get-tuple-element.38), calls=%async_computation.1 | async-start | bytes 262144 | tf_op jit(solution)/shard_map/all_to_all | solution.py:525
  52.2 5.3 %collective-permute-start = (s16[336,128]{1,0:T(8,128)(2,1)S(1)}, s16[336,128]{1,0:T(8,128)(2,1)S(1)}, u32[]{:S(2)}, u32[]{:S(2)}) collective-permute-start(s16[336,128]{1,0:T(8,128)(2,1)S(1)} %get-tuple-element.42), channel_id=1, source_target_pairs={{0,8},{1,9},{2,10},{3,11},{4,12},{5,13},{6,14},{7,15},{8,16},{9,17... | collective-permute-start | bytes 258056 | tf_op jit(solution)/shard_map/ppermute | solution.py:33
  53.8 4.5 %collective-permute-start.1 = (s16[336,128]{1,0:T(8,128)(2,1)S(1)}, s16[336,128]{1,0:T(8,128)(2,1)S(1)}, u32[]{:S(2)}, u32[]{:S(2)}) collective-permute-start(s16[336,128]{1,0:T(8,128)(2,1)S(1)} %get-tuple-element.42), channel_id=1, source_target_pairs={{0,24},{1,25},{2,26},{3,27},{4,28},{5,29},{6,30},{7,31},{8,0},{9,1... | collective-permute-start | bytes 258056 | tf_op jit(solution)/shard_map/ppermute | solution.py:33
  55.2 6.2 %collective-permute-start.2 = (s16[336,128]{1,0:T(8,128)(2,1)S(1)}, s16[336,128]{1,0:T(8,128)(2,1)S(1)}, u32[]{:S(2)}, u32[]{:S(2)}) collective-permute-start(s16[336,128]{1,0:T(8,128)(2,1)S(1)} %get-tuple-element.42), channel_id=1, source_target_pairs={{0,16},{1,17},{2,18},{3,19},{4,20},{5,21},{6,22},{7,23},{8,24},{9,... | collective-permute-start | bytes 258056 | tf_op jit(solution)/shard_map/ppermute | solution.py:33
  61.4 19.4 %copy-start = (s16[1344,128]{1,0:T(8,128)(2,1)}, s16[1344,128]{1,0:T(8,128)(2,1)S(1)}, u32[]{:S(2)}) copy-start(s16[1344,128]{1,0:T(8,128)(2,1)S(1)} %constant_dynamic-update-slice_fusion.refs_0_) | copy-start | bytes 1032196
  61.4 10.1 %collective-permute-start.3 = (s16[1344,128]{1,0:T(8,128)(2,1)S(1)}, s16[1344,128]{1,0:T(8,128)(2,1)S(1)}, u32[]{:S(2)}, u32[]{:S(2)}) collective-permute-start(s16[1344,128]{1,0:T(8,128)(2,1)S(1)} %constant_dynamic-update-slice_fusion.refs_0_), channel_id=1, source_target_pairs={{0,1},{1,2},{2,3},{3,4},{4,5},{5,6},{6,7},{7,0},{8,9},{9,10},{10,1... | collective-permute-start | bytes 1032200 | tf_op jit(solution)/shard_map/ppermute | solution.py:37
  63.3 9.4 %collective-permute-start.5 = (s16[1344,128]{1,0:T(8,128)(2,1)S(1)}, s16[1344,128]{1,0:T(8,128)(2,1)}, u32[]{:S(2)}, u32[]{:S(2)}) collective-permute-start(s16[1344,128]{1,0:T(8,128)(2,1)S(1)} %constant_dynamic-update-slice_fusion.refs_0_), channel_id=1, source_target_pairs={{0,7},{1,0},{2,1},{3,2},{4,3},{5,4},{6,5},{7,6},{8,15},{9,8},{10,9... | collective-permute-start | bytes 1032200 | tf_op jit(solution)/shard_map/ppermute | solution.py:37
  65.6 14.2 %all-to-all-start.2 = ((s16[8,272,128]{2,1,0:T(8,128)(2,1)}), s16[8,272,128]{2,1,0:T(8,128)(2,1)S(1)}, u32[]{:S(2)}, u32[]{:S(2)}) async-start(s16[8,272,128]{2,1,0:T(8,128)(2,1)} %broadcast_in_dim.18), calls=%async_computation.2 | async-start | bytes 1114112 | tf_op jit(solution)/shard_map/all_to_all | solution.py:529
  71.5 9.3 %collective-permute-start.4 = (s16[1344,128]{1,0:T(8,128)(2,1)S(1)}, s16[1344,128]{1,0:T(8,128)(2,1)}, u32[]{:S(2)}, u32[]{:S(2)}) collective-permute-start(s16[1344,128]{1,0:T(8,128)(2,1)S(1)} %collective-permute-done.3.refs_1_), channel_id=1, source_target_pairs={{0,1},{1,2},{2,3},{3,4},{4,5},{5,6},{6,7},{7,0},{8,9},{9,10},{10,1... | collective-permute-start | bytes 1032200 | tf_op jit(solution)/shard_map/ppermute | solution.py:37
  72.0 0.7 copy-start.4
  72.7 8.3 %collective-permute-start.6 = (s16[1344,128]{1,0:T(8,128)(2,1)}, s16[1344,128]{1,0:T(8,128)(2,1)}, u32[]{:S(2)}, u32[]{:S(2)}) collective-permute-start(s16[1344,128]{1,0:T(8,128)(2,1)} %collective-permute-done.5.refs_2_), channel_id=1, source_target_pairs={{0,7},{1,0},{2,1},{3,2},{4,3},{5,4},{6,5},{7,6},{8,15},{9,8},{10,9... | collective-permute-start | bytes 1032200 | tf_op jit(solution)/shard_map/ppermute | solution.py:37
  81.1 10.0 %collective-permute-start.7 = (s16[1344,128]{1,0:T(8,128)(2,1)}, s16[1344,128]{1,0:T(8,128)(2,1)S(1)}, u32[]{:S(2)}, u32[]{:S(2)}) collective-permute-start(s16[1344,128]{1,0:T(8,128)(2,1)} %collective-permute-done.4.refs_3_), channel_id=1, source_target_pairs={{0,1},{1,2},{2,3},{3,4},{4,5},{5,6},{6,7},{7,0},{8,9},{9,10},{10,1... | collective-permute-start | bytes 1032200 | tf_op jit(solution)/shard_map/ppermute | solution.py:37
  81.2 9.8 %collective-permute-start.8 = (s16[1344,128]{1,0:T(8,128)(2,1)}, s16[1344,128]{1,0:T(8,128)(2,1)S(1)}, u32[]{:S(2)}, u32[]{:S(2)}) collective-permute-start(s16[1344,128]{1,0:T(8,128)(2,1)} %collective-permute-done.6.refs_4_), channel_id=1, source_target_pairs={{0,7},{1,0},{2,1},{3,2},{4,3},{5,4},{6,5},{7,6},{8,15},{9,8},{10,9... | collective-permute-start | bytes 1032200 | tf_op jit(solution)/shard_map/ppermute | solution.py:37
  91.2 8.5 %collective-permute-start.9 = (s16[1344,128]{1,0:T(8,128)(2,1)S(1)}, s16[1344,128]{1,0:T(8,128)(2,1)S(1)}, u32[]{:S(2)}, u32[]{:S(2)}) collective-permute-start(s16[1344,128]{1,0:T(8,128)(2,1)S(1)} %broadcast_select_fusion), channel_id=1, source_target_pairs={{0,1},{1,2},{2,3},{3,4},{4,5},{5,6},{6,7},{7,0},{8,9},{9,10},{10,1... | collective-permute-start | bytes 1032200 | tf_op jit(solution)/shard_map/ppermute | solution.py:48
  91.6 1.0 copy-start.1
  92.6 1.0 copy-start.5
  93.6 6.1 %copy-start.7 = (f32[256]{0:T(256)S(1)}, f32[256]{0:T(256)}, u32[]{:S(2)}) copy-start(f32[256]{0:T(256)} %param.11) | copy-start | bytes 3076

commit v4 on v3

--- a/solution.py
+++ b/solution.py
@@ -24,6 +24,7 @@
 SIZE = BLK_DEV * BLK
 NB = BLK_DEV * OWN
 KACT = BLK_DEV * ACTS
+CORES = 2
 Y_ORDER = (0, -1, 1, 2)
 PARAMS = pltpu.CompilerParams(vmem_limit_bytes=16 * 1024 * 1024)
 WIDE = pltpu.CompilerParams(vmem_limit_bytes=28 * 1024 * 1024)
@@ -37,6 +38,10 @@
     return lax.ppermute(
         x, "var", [(i, (i // ZS) * ZS + (i % ZS + k) % ZS) for i in range(OWN)]
     )
+
+
+def core_swap(x):
+    return lax.ppermute(x, "samp", [(i, i ^ 1) for i in range(GRP)])
 
 
 def z_across(x):
@@ -310,7 +315,9 @@
 
 def last_kernel(n, meta, *refs):
     groups, mats, rest = grouped(n, refs)
-    w_in, g_in, e_ref, diag_ref, out_ref, tiny_ref, u_ref, g_by, u_by, d_by, s2_by = rest
+    w_in, g_in, e_ref, diag_ref, keep_ref, send_ref, tiny_ref, u_ref = rest[:8]
+    w_by, g_by, a_by, u_by, d_by, s2_by = rest[8:]
+    core = meta[1] % CORES
     w_all, g_all = products(groups, mats)
     lane = lax.broadcasted_iota(jnp.int32, (SIZE, BLK), 1)
     row = lax.broadcasted_iota(jnp.int32, (SIZE, BLK), 0)
@@ -318,8 +325,6 @@
     block = meta[2] * BLK_DEV + row // BLK
     diag = spread(diag_ref)
     mine = jnp.where(in_block // SL == meta[1], diag, 0.0)
-    tail = jnp.zeros((14, BLK), F32)
-    exps = []
     e_sc = [scale_of(value(e_ref[g, U_ROWS:OWN_ROWS, :])) for g in range(GRP)]
     for p in range(GRP):
         cols = slice(p * BLK, (p + 1) * BLK)
@@ -338,9 +343,7 @@
         d_by[p : p + 1, :] = jnp.sum(jnp.where(hit, e + diag, 0.0), axis=0, keepdims=True)
         s2_by[p : p + 1, :] = jnp.sum(u * u, axis=0, keepdims=True)
         tiny_ref[p : p + 1, :] = jnp.sum(u * (w + mine * u), axis=0, keepdims=True)
-        q, x = code(w, 0)
-        out_ref[p, 0:SIZE, :] = q
-        exps.append(x)
+        w_by[p] = jnp.where(hit, 0.0, w)
         g_by[p] = g_in[:, cols] + g_all[:, cols]
     own = meta[1]
     u_ref[...] = u_by[own]
@@ -353,11 +356,26 @@
         active.append(g_by[meta[3 + GRP + k], r * BLK : (r + 1) * BLK, :])
     for g in range(GRP):
         x = jnp.concatenate([v[g * SL : (g + 1) * SL] for v in active], axis=0)
-        q, x = code(x, 0)
-        out_ref[g, SIZE:E_AT, :] = q
-        x = jnp.concatenate([exps[g], x, tail], axis=0)
-        out_ref[g, E_AT:T_AT, :] = x.astype(jnp.int32).astype(I16)
-    out_ref[:, T_AT:, :] = jnp.zeros((GRP, 48, BLK), I16)
+        a_by[g] = x
+
+    def part(g):
+        return w_by[g], a_by[g]
+
+    for i in range(GRP // CORES):
+        w, x = part(CORES * i + core)
+        keep_ref[i, 0:SIZE, :] = w
+        keep_ref[i, SIZE:E_AT, :] = x
+        w, x = part(CORES * i + 1 - core)
+        fill(send_ref, i, w, x)
+
+
+def fill(ref, i, w, gram):
+    q, w_exp = code(w, 0)
+    ref[i, 0:SIZE, :] = q
+    q, g_exp = code(gram, 0)
+    ref[i, SIZE:E_AT, :] = q
+    x = jnp.concatenate([w_exp, g_exp, jnp.zeros((14, BLK), F32)], axis=0)
+    ref[i, E_AT:T_AT, :] = x.astype(jnp.int32).astype(I16)
 
 
 def full_spec(shape):
@@ -407,16 +425,24 @@
 def last_products(meta, theta, left, groups, before, e_rows, diag):
     flops = len(groups) * 2 * 2 * SIZE * SIZE * GRP * BLK
     out_shape = [
-        whole((GRP, BUNDLE, BLK), I16),
+        whole((GRP // CORES, E_AT, BLK), F32),
+        whole((GRP // CORES, T_AT, BLK), I16),
         whole((2 * GRP, BLK), F32),
         whole((SIZE, BLK), F32),
     ]
-    scratch = [pltpu.VMEM((GRP, SIZE, BLK), F32)] * 2 + [pltpu.VMEM((GRP, BLK), F32)] * 2
+    scratch = [
+        pltpu.VMEM((GRP, SIZE, BLK), F32),
+        pltpu.VMEM((GRP, SIZE, BLK), F32),
+        pltpu.VMEM((GRP, G_ROWS, BLK), F32),
+        pltpu.VMEM((GRP, SIZE, BLK), F32),
+        pltpu.VMEM((GRP, BLK), F32),
+        pltpu.VMEM((GRP, BLK), F32),
+    ]
     extra = [*before, e_rows, diag]
     return grouped_call(last_kernel, meta, theta, left, groups, extra, out_shape, scratch, flops)
 
 
-def scalar_kernel(tiny_ref, out_ref):
+def join_kernel(tiny_ref, keep_ref, got_ref, out_ref):
     x = tiny_ref[0]
     for i in range(1, OWN):
         x = x + tiny_ref[i]
@@ -424,33 +450,41 @@
     x = x * jnp.exp2(15.0 - e)
     hi = jnp.floor(x)
     lo = jnp.floor((x - hi) * 32768.0)
-    x = jnp.concatenate([hi, lo, e], axis=0)
-    out_ref[...] = x.astype(jnp.int32).astype(I16)
-
-
-def scalar_rows(tiny):
+    x = jnp.concatenate([hi, lo, e], axis=0).astype(jnp.int32).astype(I16)
+    for i in range(GRP // CORES):
+        sc = scale_of(value(got_ref[i, E_AT:T_AT, :]))
+        w = keep_ref[i, 0:SIZE, :] + value(got_ref[i, 0:SIZE, :]) * sc[0:1]
+        gram = keep_ref[i, SIZE:E_AT, :] + value(got_ref[i, SIZE:E_AT, :]) * sc[1:2]
+        fill(out_ref, i, w, gram)
+        out_ref[i, T_AT:BUNDLE, :] = x
+
+
+def join(tiny, keep, got):
     return pl.pallas_call(
-        scalar_kernel,
-        in_specs=[vmem_spec()],
+        join_kernel,
+        in_specs=[vmem_spec()] * 3,
         out_specs=vmem_spec(),
-        out_shape=whole((48, BLK), I16),
+        out_shape=whole((GRP // CORES, BUNDLE, BLK), I16),
         compiler_params=PARAMS,
-    )(tiny)
+    )(tiny, keep, got)
 
 
 def finish_kernel(
-    count, meta, bundle_ref, u_ref, diag_ref, e_ref, inv_ref, res_ref, grad_ref, ct_ref, cu_ref, cr_ref
+    count, meta, bundle_ref, u_ref, diag_ref, e_ref, inv_ref, res_ref, grad_ref, ct_ref, cu_ref, cr_ref, s2_ref
 ):
     w, gram, q, s2, d = 0.0, 0.0, 0.0, [], []
-    for g in range(GRP):
+    first = meta[1] % CORES == 0
+    for g in range(GRP // CORES):
         sc = scale_of(value(bundle_ref[g, E_AT:T_AT, :]))
         w = w + value(bundle_ref[g, 0:SIZE, :]) * sc[0:1]
         gram = gram + value(bundle_ref[g, SIZE:E_AT, :]) * sc[1:2]
         x = value(bundle_ref[g, T_AT:BUNDLE, :])
         x = (x[0:16] + x[16:32] * (1.0 / 32768.0)) * scale_of(x[32:48])
         q = q + x[0:GRP]
-        s2.append(x[GRP : GRP + 1])
-        d.append(x[GRP + 1 : GRP + 2])
+        own, other = x[GRP : GRP + 2], x[GRP + 2 : GRP + 4]
+        for v in (jnp.where(first, own, other), jnp.where(first, other, own)):
+            s2.append(v[0:1])
+            d.append(v[1:2])
     s2 = jnp.concatenate(s2, axis=0)
     d = jnp.concatenate(d, axis=0)
     alpha1 = 1.0 / d
@@ -459,13 +493,14 @@
     ct_ref[...] = alpha1 + alpha2 * rr
     cu_ref[...] = alpha1 * alpha2
     cr_ref[...] = alpha2 * rr * d
+    s2_ref[...] = s2
 
     own = pl.ds(meta[1], 1)
     lane = lax.broadcasted_iota(jnp.int32, (SIZE, BLK), 1)
     row = lax.broadcasted_iota(jnp.int32, (SIZE, BLK), 0)
     hit = (meta[2] * BLK_DEV + row // BLK == meta[3 + meta[1]]) & (row % BLK == lane)
     u = u_ref[...]
-    w = w + spread(diag_ref) * u
+    w = jnp.where(hit, s2_ref[own, :], w + spread(diag_ref) * u)
     c_t, c_u, c_r = ct_ref[own, :], cu_ref[own, :], cr_ref[own, :]
     inv_ref[...] = jnp.where(hit, c_t, 0.0) - c_u * u
     res_ref[...] = c_u * w - c_t * u - jnp.where(hit, c_r, 0.0)
@@ -490,7 +525,7 @@
             whole((SIZE, BLK), F32),
             whole((KACT, SL, BLK), F32),
         ],
-        scratch_shapes=[pltpu.VMEM((GRP, BLK), F32)] * 3,
+        scratch_shapes=[pltpu.VMEM((GRP, BLK), F32)] * 4,
         compiler_params=PARAMS,
     )(meta, bundle, u, diag, e_slice)
 
@@ -541,12 +576,17 @@
     sums = early_products(place, theta, left, groups[:5])
     across = z_across(jnp.where(s % 2 == 0, down, up))
     groups = [(-3, down), (3, up), (4, across)]
-    bundle, tiny, u = last_products(place, theta, left, groups, sums, e_rows, diag)
-
+    keep, sent, tiny, u = last_products(place, theta, left, groups, sums, e_rows, diag)
+
+    near = core_swap(tiny)
+    other = core_swap(sent)
+    tiny = jnp.concatenate(
+        [tiny[:GRP] + near[:GRP], tiny[GRP : GRP + 2], near[GRP : GRP + 2], jnp.zeros((4, BLK), F32)]
+    )
     tiny = lax.all_to_all(jnp.broadcast_to(tiny[None], (OWN, 2 * GRP, BLK)), "var", 0, 0)
-    tiny = scalar_rows(tiny)
-    bundle = bundle.at[:, T_AT:].set(jnp.broadcast_to(tiny[None], (GRP, 48, BLK)))
-    bundle = lax.all_to_all(bundle, "samp", 0, 0)
+    bundle = join(tiny, keep, other)
+    sides = [list(range(c, GRP, CORES)) for c in range(CORES)]
+    bundle = lax.all_to_all(bundle, "samp", 0, 0, axis_index_groups=sides)
     return tuple(finish(float(count_rows * GRP), place, bundle, u, diag, e_slice))
 
 

time: 142 us -> 139 us (0.979)
  blocking collectives: 36.2 us -> 13.1 us
  waiting for transfers between devices: 35.4 us -> 48 us
  starting transfers between devices: 34.9 us -> 41.5 us
    all_to_all x2 -> x1, blocking collectives: 36.2 us -> 13.1 us  [per_device(): bundle = lax.all_to_all(bundle, 'samp', 0, 0, axis_index_groups=sides)]
    all_to_all x0 -> x1, waiting for transfers between devices: none -> 9.87 us  [per_device(): lax.all_to_all(jnp.broadcast_to(tiny[None], (OWN, 2 * GRP, BLK)), 'var',...]
    all_to_all x0 -> x1, starting transfers between devices: none -> 6.51 us  [per_device(): lax.all_to_all(jnp.broadcast_to(tiny[None], (OWN, 2 * GRP, BLK)), 'var',...]
    ppermute x0 -> x2, waiting for transfers between devices: none -> 2.8 us  [core_swap(): return lax.ppermute(x, 'samp', [(i, i ^ 1) for i in range(GRP)])]
  transfers between devices with their start and end apart: 13 -> 16, of which waited for: 11 -> 14; matrix products, arithmetic and copies ran while one was open for 10% -> 10% of each run, Pallas kernels for 3% -> 3%
where the time goes in v4:
time: 139 us; the launch traced here: 137 us
  waiting for transfers between devices  48 us (35%)
  starting transfers between devices  41.5 us (30%)
  local copies, waits for them, and re-layouts  17.6 us (13%)
  Pallas kernels  13.9 us (10%)
  blocking collectives  13.1 us (9%)
  other arithmetic  1.71 us (1%)
    all_to_all x1, blocking collectives, per_device(): bundle = lax.all_to_all(bundle, 'samp', 0, 0, axis_index_groups=sides)  13.1 us
    all_to_all x1, starting transfers between devices, per_device(): got = lax.all_to_all(chunks, 'var', 0, 0)  11.7 us
    ppermute x6, starting transfers between devices, z_shift(): lax.ppermute(x, 'var', [(i, i // ZS * ZS + (i % ZS + k) % ZS) for i in ra...  10.2 us
    ppermute x6, waiting for transfers between devices, z_shift(): lax.ppermute(x, 'var', [(i, i // ZS * ZS + (i % ZS + k) % ZS) for i in ra...  9.97 us
    all_to_all x1, waiting for transfers between devices, per_device(): lax.all_to_all(jnp.broadcast_to(tiny[None], (OWN, 2 * GRP, BLK)), 'var',...  9.87 us
    all_to_all x1, waiting for transfers between devices, per_device(): got = lax.all_to_all(chunks, 'var', 0, 0)  8.16 us
    unnamed x29, local copies, waits for them, and re-layouts  7.11 us
    all_to_all x1, starting transfers between devices, per_device(): lax.all_to_all(jnp.broadcast_to(tiny[None], (OWN, 2 * GRP, BLK)), 'var',...  6.51 us
  transfers between devices with their start and end apart: 16, of which 14 were waited for; matrix products, arithmetic and copies ran while one was open for 10% of the time, Pallas kernels for 3%

profile of v4, /device:TPU:8, one launch (start us, length us, event | category | flops | bytes accessed | tf_op | source)
XLA Modules:
  0.0 137.4 jit_solution(4292443900038352726)
XLA Ops:
  0.6 1.1 constant_dynamic-slice_fusion.1.v_ref
  3.4 3.5 %shard_map.103 = (s16[32,96,128]{2,1,0:T(8,128)(2,1)}, f32[32,1024]{1,0:T(8,128)S(1)}) custom-call(s32[75]{0:T(128)S(1)} %pad_add_fusion.meta, f32[64,16,128]{2,1,0:T(8,128)S(1)} %constant_dynamic-slice_fusion.1.v_ref, bf16[32,16,128]{2,1,0:T(8,128)(2,1)S(1)} %bitcast.27), custom_call_target="tpu_custom_call" | custom-call | tf_op jit(solution)/shard_map/pallas_call | solution.py:130
  6.9 11.7 %all-to-all-start = ((s16[32,96,128]{2,1,0:T(8,128)(2,1)}), s16[32,96,128]{2,1,0:T(8,128)(2,1)S(1)}, u32[]{:S(2)}, u32[]{:S(2)}) async-start(s16[32,96,128]{2,1,0:T(8,128)(2,1)} %get-tuple-element.25), calls=%async_computation | async-start | bytes 1572864 | tf_op jit(solution)/shard_map/all_to_all | solution.py:546
  18.6 5.3 %constant_dynamic-slice_fusion = f32[2,32,128,16]{3,2,1,0:T(8,128)} fusion(f32[2,32,128,128]{3,2,1,0:T(8,128)} %bitcast.31, s32[]{:T(128)S(6)} %select_n.37), kind=kLoop, calls=%fused_computation.24 | loop fusion | bytes 1048580 | tf_op jit(solution)/shard_map/dynamic_slice | solution.py:552
  24.0 2.9 %copy.16 = f32[2,32,128,16]{2,1,3,0:T(8,128)S(1)} copy(f32[2,32,128,16]{3,2,1,0:T(8,128)} %constant_dynamic-slice_fusion) | data formatting | bytes 1048576
  31.3 8.2 %all-to-all-done.got_ref = s16[32,96,128]{2,1,0:T(8,128)(2,1)S(1)} async-done(((s16[32,96,128]{2,1,0:T(8,128)(2,1)}), s16[32,96,128]{2,1,0:T(8,128)(2,1)S(1)}, u32[]{:S(2)}, u32[]{:S(2)}) %all-to-all-start) | async-done | bytes 786464 | tf_op jit(solution)/shard_map/all_to_all | solution.py:546
  39.5 1.4 shard_map.104
  40.8 4.3 %all-to-all-start.1 = ((f32[8,32,128]{2,1,0:T(8,128)}), f32[8,32,128]{2,1,0:T(8,128)S(1)}, u32[]{:S(2)}, u32[]{:S(2)}) async-start(f32[8,32,128]{2,1,0:T(8,128)} %get-tuple-element.27), calls=%async_computation.1 | async-start | bytes 262144 | tf_op jit(solution)/shard_map/all_to_all | solution.py:560
  45.2 6.1 %all-to-all-done.1.turned_ref = f32[8,32,128]{2,1,0:T(8,128)S(1)} async-done(((f32[8,32,128]{2,1,0:T(8,128)}), f32[8,32,128]{2,1,0:T(8,128)S(1)}, u32[]{:S(2)}, u32[]{:S(2)}) %all-to-all-start.1) | async-done | bytes 131104 | tf_op jit(solution)/shard_map/all_to_all | solution.py:560
  52.1 1.6 %collective-permute-start = (s16[336,128]{1,0:T(8,128)(2,1)S(1)}, s16[336,128]{1,0:T(8,128)(2,1)S(1)}, u32[]{:S(2)}, u32[]{:S(2)}) collective-permute-start(s16[336,128]{1,0:T(8,128)(2,1)S(1)} %get-tuple-element.31), channel_id=1, source_target_pairs={{0,8},{1,9},{2,10},{3,11},{4,12},{5,13},{6,14},{7,15},{8,16},{9,17... | collective-permute-start | bytes 258056 | tf_op jit(solution)/shard_map/ppermute | solution.py:34
  53.7 1.4 %collective-permute-start.1 = (s16[336,128]{1,0:T(8,128)(2,1)S(1)}, s16[336,128]{1,0:T(8,128)(2,1)S(1)}, u32[]{:S(2)}, u32[]{:S(2)}) collective-permute-start(s16[336,128]{1,0:T(8,128)(2,1)S(1)} %get-tuple-element.31), channel_id=1, source_target_pairs={{0,24},{1,25},{2,26},{3,27},{4,28},{5,29},{6,30},{7,31},{8,0},{9,1... | collective-permute-start | bytes 258056 | tf_op jit(solution)/shard_map/ppermute | solution.py:34
  55.1 2.0 %collective-permute-start.2 = (s16[336,128]{1,0:T(8,128)(2,1)S(1)}, s16[336,128]{1,0:T(8,128)(2,1)S(1)}, u32[]{:S(2)}, u32[]{:S(2)}) collective-permute-start(s16[336,128]{1,0:T(8,128)(2,1)S(1)} %get-tuple-element.31), channel_id=1, source_target_pairs={{0,16},{1,17},{2,18},{3,19},{4,20},{5,21},{6,22},{7,23},{8,24},{9,... | collective-permute-start | bytes 258056 | tf_op jit(solution)/shard_map/ppermute | solution.py:34
  58.2 3.1 %collective-permute-done.2 = s16[336,128]{1,0:T(8,128)(2,1)S(1)} collective-permute-done((s16[336,128]{1,0:T(8,128)(2,1)S(1)}, s16[336,128]{1,0:T(8,128)(2,1)S(1)}, u32[]{:S(2)}, u32[]{:S(2)}) %collective-permute-start.2) | collective-permute-done | bytes 86048 | tf_op jit(solution)/shard_map/ppermute | solution.py:34
  61.3 1.9 %collective-permute-start.3 = (s16[1344,128]{1,0:T(8,128)(2,1)S(1)}, s16[1344,128]{1,0:T(8,128)(2,1)S(1)}, u32[]{:S(2)}, u32[]{:S(2)}) collective-permute-start(s16[1344,128]{1,0:T(8,128)(2,1)S(1)} %constant_dynamic-update-slice_fusion.refs_0_), channel_id=1, source_target_pairs={{0,1},{1,2},{2,3},{3,4},{4,5},{5,6},{6,7},{7,0},{8,9},{9,10},{10,1... | collective-permute-start | bytes 1032200 | tf_op jit(solution)/shard_map/ppermute | solution.py:38
  63.3 1.4 %collective-permute-start.5 = (s16[1344,128]{1,0:T(8,128)(2,1)S(1)}, s16[1344,128]{1,0:T(8,128)(2,1)}, u32[]{:S(2)}, u32[]{:S(2)}) collective-permute-start(s16[1344,128]{1,0:T(8,128)(2,1)S(1)} %constant_dynamic-update-slice_fusion.refs_0_), channel_id=1, source_target_pairs={{0,7},{1,0},{2,1},{3,2},{4,3},{5,4},{6,5},{7,6},{8,15},{9,8},{10,9... | collective-permute-start | bytes 1032200 | tf_op jit(solution)/shard_map/ppermute | solution.py:38
  65.5 3.5 %all-to-all-start.2 = ((s16[8,272,128]{2,1,0:T(8,128)(2,1)}), s16[8,272,128]{2,1,0:T(8,128)(2,1)S(1)}, u32[]{:S(2)}, u32[]{:S(2)}) async-start(s16[8,272,128]{2,1,0:T(8,128)(2,1)} %broadcast_in_dim.38), calls=%async_computation.2 | async-start | bytes 1114112 | tf_op jit(solution)/shard_map/all_to_all | solution.py:564
  69.1 2.4 %collective-permute-done.3.refs_1_ = s16[1344,128]{1,0:T(8,128)(2,1)S(1)} collective-permute-done((s16[1344,128]{1,0:T(8,128)(2,1)S(1)}, s16[1344,128]{1,0:T(8,128)(2,1)S(1)}, u32[]{:S(2)}, u32[]{:S(2)}) %collective-permute-start.3) | collective-permute-done | bytes 344096 | tf_op jit(solution)/shard_map/ppermute | solution.py:38
  72.7 2.8 %collective-permute-start.6 = (s16[1344,128]{1,0:T(8,128)(2,1)}, s16[1344,128]{1,0:T(8,128)(2,1)}, u32[]{:S(2)}, u32[]{:S(2)}) collective-permute-start(s16[1344,128]{1,0:T(8,128)(2,1)} %collective-permute-done.5.refs_2_), channel_id=1, source_target_pairs={{0,7},{1,0},{2,1},{3,2},{4,3},{5,4},{6,5},{7,6},{8,15},{9,8},{10,9... | collective-permute-start | bytes 1032200 | tf_op jit(solution)/shard_map/ppermute | solution.py:38
  75.4 4.3 %all-to-all-done.2.refs_14_ = s16[8,272,128]{2,1,0:T(8,128)(2,1)S(1)} async-done(((s16[8,272,128]{2,1,0:T(8,128)(2,1)}), s16[8,272,128]{2,1,0:T(8,128)(2,1)S(1)}, u32[]{:S(2)}, u32[]{:S(2)}) %all-to-all-start.2) | async-done | bytes 557088 | tf_op jit(solution)/shard_map/all_to_all | solution.py:564
  79.7 1.1 collective-permute-done.4.refs_3_
  81.2 3.5 %collective-permute-start.8 = (s16[1344,128]{1,0:T(8,128)(2,1)}, s16[1344,128]{1,0:T(8,128)(2,1)S(1)}, u32[]{:S(2)}, u32[]{:S(2)}) collective-permute-start(s16[1344,128]{1,0:T(8,128)(2,1)} %collective-permute-done.6.refs_4_), channel_id=1, source_target_pairs={{0,7},{1,0},{2,1},{3,2},{4,3},{5,4},{6,5},{7,6},{8,15},{9,8},{10,9... | collective-permute-start | bytes 1032200 | tf_op jit(solution)/shard_map/ppermute | solution.py:38
  84.7 6.3 %collective-permute-done.7.refs_0_ = s16[1344,128]{1,0:T(8,128)(2,1)S(1)} collective-permute-done((s16[1344,128]{1,0:T(8,128)(2,1)}, s16[1344,128]{1,0:T(8,128)(2,1)S(1)}, u32[]{:S(2)}, u32[]{:S(2)}) %collective-permute-start.7) | collective-permute-done | bytes 344096 | tf_op jit(solution)/shard_map/ppermute | solution.py:38
  92.6 1.0 copy-done.5
  93.5 3.4 %shard_map.107 = (f32[256,1024]{1,0:T(8,128)S(1)}, f32[256,1024]{1,0:T(8,128)S(1)}) custom-call(s32[19]{0:T(128)S(1)} %concatenate.12.meta, s16[1344,128]{1,0:T(8,128)(2,1)S(1)} %copy-done.1, s16[1344,128]{1,0:T(8,128)(2,1)S(1)} %copy-done.5, s16[1344,128]{1,0:T(8,128)(2,1)} %collective-permute-done.5.refs_2_, ...), custom_call_target="tpu_custom_call" | custom-call | flops 1342177280 | bytes 15000000 | tf_op jit(solution)/shard_map/pallas_call | solution.py:408
  97.0 2.7 %collective-permute-done.9.refs_2_ = s16[1344,128]{1,0:T(8,128)(2,1)S(1)} collective-permute-done((s16[1344,128]{1,0:T(8,128)(2,1)S(1)}, s16[1344,128]{1,0:T(8,128)(2,1)S(1)}, u32[]{:S(2)}, u32[]{:S(2)}) %collective-permute-start.9) | collective-permute-done | bytes 344096 | tf_op jit(solution)/shard_map/ppermute | solution.py:53
  99.6 2.6 %shard_map.108 = (f32[4,384,128]{2,1,0:T(8,128)S(1)}, s16[4,400,128]{2,1,0:T(8,128)(2,1)S(1)}, f32[16,128]{1,0:T(8,128)S(1)}, f32[256,128]{1,0:T(8,128)S(1)}) custom-call(s32[19]{0:T(128)S(1)} %concatenate.12.meta, s16[1344,128]{1,0:T(8,128)(2,1)S(1)} %collective-permute-done.7.refs_0_, s16[1344,128]{1,0:T(8,128)(2,1)S(1)} %collective-permute-done.8.refs_1_, ...), custom_call_target="tpu_custom_call" | custom-call | flops 805306368 | bytes 9000000 | tf_op jit(solution)/shard_map/pallas_call | solution.py:408
  102.4 1.1 collective-permute-done.10
  104.3 6.5 %all-to-all-start.3 = ((f32[32,16,128]{2,1,0:T(8,128)}), f32[32,16,128]{2,1,0:T(8,128)S(1)}, u32[]{:S(2)}, u32[]{:S(2)}) async-start(f32[32,16,128]{2,1,0:T(8,128)} %broadcast_in_dim.41), calls=%async_computation.3 | async-start | bytes 524288 | tf_op jit(solution)/shard_map/all_to_all | solution.py:586
  110.9 1.7 %collective-permute-done.11.got_ref = s16[4,400,128]{2,1,0:T(8,128)(2,1)S(1)} collective-permute-done((s16[4,400,128]{2,1,0:T(8,128)(2,1)S(1)}, s16[4,400,128]{2,1,0:T(8,128)(2,1)S(1)}, u32[]{:S(2)}, u32[]{:S(2)}) %collective-permute-start.11) | collective-permute-done | bytes 409632 | tf_op jit(solution)/shard_map/ppermute | solution.py:44
  112.6 9.9 %all-to-all-done.3.tiny_ref = f32[32,16,128]{2,1,0:T(8,128)S(1)} async-done(((f32[32,16,128]{2,1,0:T(8,128)}), f32[32,16,128]{2,1,0:T(8,128)S(1)}, u32[]{:S(2)}, u32[]{:S(2)}) %all-to-all-start.3) | async-done | bytes 262176 | tf_op jit(solution)/shard_map/all_to_all | solution.py:586
  122.9 13.1 %all_to_all.25.bundle_ref = s16[4,448,128]{2,1,0:T(8,128)(2,1)S(1)} all-to-all(s16[4,448,128]{2,1,0:T(8,128)(2,1)S(1)} %shard_map.109), channel_id=1, replica_groups={{0,64,128,192},{32,96,160,224},{1,65,129,193},{33,97,161,225},{2,66,130..., dimensions={0} | all-to-all | bytes 917504 | tf_op jit(solution)/shard_map/all_to_all | solution.py:589
  136.0 1.4 %shard_map.110 = (f32[256,128]{1,0:T(8,128)}, f32[256,128]{1,0:T(8,128)}, f32[8,16,128]{2,1,0:T(8,128)}) custom-call(s32[19]{0:T(128)S(1)} %concatenate.12.meta, s16[4,448,128]{2,1,0:T(8,128)(2,1)S(1)} %all_to_all.25.bundle_ref, f32[256,128]{1,0:T(8,128)S(1)} %get-tuple-element.45.u_ref, f32[2,128]{1,0:T(2,128)S(1)} %bitcast.30, ...), custom_call_target="tpu_custom_call" | custom-call | tf_op jit(solution)/shard_map/pallas_call | solution.py:519
  (62 shorter events, 13.5 us)
Async XLA Ops:
  2.5 0.9 copy-start.2
  6.9 32.5 %all-to-all-start = ((s16[32,96,128]{2,1,0:T(8,128)(2,1)}), s16[32,96,128]{2,1,0:T(8,128)(2,1)S(1)}, u32[]{:S(2)}, u32[]{:S(2)}) async-start(s16[32,96,128]{2,1,0:T(8,128)(2,1)} %get-tuple-element.25), calls=%async_computation | async-start | bytes 1572864 | tf_op jit(solution)/shard_map/all_to_all | solution.py:546
  23.9 3.5 %copy-start.8 = (s32[64,1]{0,1:T(1,128)S(1)}, s32[64,1]{0,1:T(1,128)}, u32[]{:S(2)}) copy-start(s32[64,1]{0,1:T(1,128)} %param.11) | copy-start | bytes 772
  23.9 4.3 %copy-start.9 = (s32[2]{0:T(128)S(1)}, s32[2]{0:T(128)}, u32[]{:S(2)}) copy-start(s32[2]{0:T(128)} %param.12) | copy-start | bytes 28
  23.9 6.7 %copy-start.11 = (s32[4]{0:T(128)S(1)}, s32[4]{0:T(128)}, u32[]{:S(2)}) copy-start(s32[4]{0:T(128)} %constant.68.clone) | copy-start | bytes 52
  23.9 6.7 %copy-start.3 = (bf16[256,256]{1,0:T(8,128)(2,1)S(1)}, bf16[256,256]{1,0:T(8,128)(2,1)}, u32[]{:S(2)}) copy-start(bf16[256,256]{1,0:T(8,128)(2,1)} %param.8) | copy-start | bytes 393220
  26.9 12.5 %copy-start.6 = (s32[8]{0:T(128)S(1)}, s32[8]{0:T(128)}, u32[]{:S(2)}) copy-start(s32[8]{0:T(128)} %pan.1) | copy-start | bytes 100
  26.9 18.2 %copy-start.10 = (s32[8]{0:T(128)S(1)}, s32[8]{0:T(128)}, u32[]{:S(2)}) copy-start(s32[8]{0:T(128)} %param.14) | copy-start | bytes 100
  40.8 10.4 %all-to-all-start.1 = ((f32[8,32,128]{2,1,0:T(8,128)}), f32[8,32,128]{2,1,0:T(8,128)S(1)}, u32[]{:S(2)}, u32[]{:S(2)}) async-start(f32[8,32,128]{2,1,0:T(8,128)} %get-tuple-element.27), calls=%async_computation.1 | async-start | bytes 262144 | tf_op jit(solution)/shard_map/all_to_all | solution.py:560
  52.1 5.3 %collective-permute-start = (s16[336,128]{1,0:T(8,128)(2,1)S(1)}, s16[336,128]{1,0:T(8,128)(2,1)S(1)}, u32[]{:S(2)}, u32[]{:S(2)}) collective-permute-start(s16[336,128]{1,0:T(8,128)(2,1)S(1)} %get-tuple-element.31), channel_id=1, source_target_pairs={{0,8},{1,9},{2,10},{3,11},{4,12},{5,13},{6,14},{7,15},{8,16},{9,17... | collective-permute-start | bytes 258056 | tf_op jit(solution)/shard_map/ppermute | solution.py:34
  53.7 4.5 %collective-permute-start.1 = (s16[336,128]{1,0:T(8,128)(2,1)S(1)}, s16[336,128]{1,0:T(8,128)(2,1)S(1)}, u32[]{:S(2)}, u32[]{:S(2)}) collective-permute-start(s16[336,128]{1,0:T(8,128)(2,1)S(1)} %get-tuple-element.31), channel_id=1, source_target_pairs={{0,24},{1,25},{2,26},{3,27},{4,28},{5,29},{6,30},{7,31},{8,0},{9,1... | collective-permute-start | bytes 258056 | tf_op jit(solution)/shard_map/ppermute | solution.py:34
  55.1 6.2 %collective-permute-start.2 = (s16[336,128]{1,0:T(8,128)(2,1)S(1)}, s16[336,128]{1,0:T(8,128)(2,1)S(1)}, u32[]{:S(2)}, u32[]{:S(2)}) collective-permute-start(s16[336,128]{1,0:T(8,128)(2,1)S(1)} %get-tuple-element.31), channel_id=1, source_target_pairs={{0,16},{1,17},{2,18},{3,19},{4,20},{5,21},{6,22},{7,23},{8,24},{9,... | collective-permute-start | bytes 258056 | tf_op jit(solution)/shard_map/ppermute | solution.py:34
  61.3 19.4 %copy-start = (s16[1344,128]{1,0:T(8,128)(2,1)}, s16[1344,128]{1,0:T(8,128)(2,1)S(1)}, u32[]{:S(2)}) copy-start(s16[1344,128]{1,0:T(8,128)(2,1)S(1)} %constant_dynamic-update-slice_fusion.refs_0_) | copy-start | bytes 1032196
  61.3 10.1 %collective-permute-start.3 = (s16[1344,128]{1,0:T(8,128)(2,1)S(1)}, s16[1344,128]{1,0:T(8,128)(2,1)S(1)}, u32[]{:S(2)}, u32[]{:S(2)}) collective-permute-start(s16[1344,128]{1,0:T(8,128)(2,1)S(1)} %constant_dynamic-update-slice_fusion.refs_0_), channel_id=1, source_target_pairs={{0,1},{1,2},{2,3},{3,4},{4,5},{5,6},{6,7},{7,0},{8,9},{9,10},{10,1... | collective-permute-start | bytes 1032200 | tf_op jit(solution)/shard_map/ppermute | solution.py:38
  63.3 9.4 %collective-permute-start.5 = (s16[1344,128]{1,0:T(8,128)(2,1)S(1)}, s16[1344,128]{1,0:T(8,128)(2,1)}, u32[]{:S(2)}, u32[]{:S(2)}) collective-permute-start(s16[1344,128]{1,0:T(8,128)(2,1)S(1)} %constant_dynamic-update-slice_fusion.refs_0_), channel_id=1, source_target_pairs={{0,7},{1,0},{2,1},{3,2},{4,3},{5,4},{6,5},{7,6},{8,15},{9,8},{10,9... | collective-permute-start | bytes 1032200 | tf_op jit(solution)/shard_map/ppermute | solution.py:38
  65.5 14.2 %all-to-all-start.2 = ((s16[8,272,128]{2,1,0:T(8,128)(2,1)}), s16[8,272,128]{2,1,0:T(8,128)(2,1)S(1)}, u32[]{:S(2)}, u32[]{:S(2)}) async-start(s16[8,272,128]{2,1,0:T(8,128)(2,1)} %broadcast_in_dim.38), calls=%async_computation.2 | async-start | bytes 1114112 | tf_op jit(solution)/shard_map/all_to_all | solution.py:564
  71.4 9.3 %collective-permute-start.4 = (s16[1344,128]{1,0:T(8,128)(2,1)S(1)}, s16[1344,128]{1,0:T(8,128)(2,1)}, u32[]{:S(2)}, u32[]{:S(2)}) collective-permute-start(s16[1344,128]{1,0:T(8,128)(2,1)S(1)} %collective-permute-done.3.refs_1_), channel_id=1, source_target_pairs={{0,1},{1,2},{2,3},{3,4},{4,5},{5,6},{6,7},{7,0},{8,9},{9,10},{10,1... | collective-permute-start | bytes 1032200 | tf_op jit(solution)/shard_map/ppermute | solution.py:38
  71.9 0.7 copy-start.4
  72.7 8.3 %collective-permute-start.6 = (s16[1344,128]{1,0:T(8,128)(2,1)}, s16[1344,128]{1,0:T(8,128)(2,1)}, u32[]{:S(2)}, u32[]{:S(2)}) collective-permute-start(s16[1344,128]{1,0:T(8,128)(2,1)} %collective-permute-done.5.refs_2_), channel_id=1, source_target_pairs={{0,7},{1,0},{2,1},{3,2},{4,3},{5,4},{6,5},{7,6},{8,15},{9,8},{10,9... | collective-permute-start | bytes 1032200 | tf_op jit(solution)/shard_map/ppermute | solution.py:38
  81.0 10.0 %collective-permute-start.7 = (s16[1344,128]{1,0:T(8,128)(2,1)}, s16[1344,128]{1,0:T(8,128)(2,1)S(1)}, u32[]{:S(2)}, u32[]{:S(2)}) collective-permute-start(s16[1344,128]{1,0:T(8,128)(2,1)} %collective-permute-done.4.refs_3_), channel_id=1, source_target_pairs={{0,1},{1,2},{2,3},{3,4},{4,5},{5,6},{6,7},{7,0},{8,9},{9,10},{10,1... | collective-permute-start | bytes 1032200 | tf_op jit(solution)/shard_map/ppermute | solution.py:38
  81.2 9.8 %collective-permute-start.8 = (s16[1344,128]{1,0:T(8,128)(2,1)}, s16[1344,128]{1,0:T(8,128)(2,1)S(1)}, u32[]{:S(2)}, u32[]{:S(2)}) collective-permute-start(s16[1344,128]{1,0:T(8,128)(2,1)} %collective-permute-done.6.refs_4_), channel_id=1, source_target_pairs={{0,7},{1,0},{2,1},{3,2},{4,3},{5,4},{6,5},{7,6},{8,15},{9,8},{10,9... | collective-permute-start | bytes 1032200 | tf_op jit(solution)/shard_map/ppermute | solution.py:38
  91.1 8.5 %collective-permute-start.9 = (s16[1344,128]{1,0:T(8,128)(2,1)S(1)}, s16[1344,128]{1,0:T(8,128)(2,1)S(1)}, u32[]{:S(2)}, u32[]{:S(2)}) collective-permute-start(s16[1344,128]{1,0:T(8,128)(2,1)S(1)} %broadcast_select_fusion), channel_id=1, source_target_pairs={{0,1},{1,2},{2,3},{3,4},{4,5},{5,6},{6,7},{7,0},{8,9},{9,10},{10,1... | collective-permute-start | bytes 1032200 | tf_op jit(solution)/shard_map/ppermute | solution.py:53
  91.6 1.0 copy-start.1
  92.5 1.0 copy-start.5
  93.5 6.1 %copy-start.7 = (f32[256]{0:T(256)S(1)}, f32[256]{0:T(256)}, u32[]{:S(2)}) copy-start(f32[256]{0:T(256)} %param.9) | copy-start | bytes 3076
  102.2 1.3 collective-permute-start.10
  104.3 18.2 %all-to-all-start.3 = ((f32[32,16,128]{2,1,0:T(8,128)}), f32[32,16,128]{2,1,0:T(8,128)S(1)}, u32[]{:S(2)}, u32[]{:S(2)}) async-start(f32[32,16,128]{2,1,0:T(8,128)} %broadcast_in_dim.41), calls=%async_computation.3 | async-start | bytes 524288 | tf_op jit(solution)/shard_map/all_to_all | solution.py:586
  110.8 1.8 %collective-permute-start.11 = (s16[4,400,128]{2,1,0:T(8,128)(2,1)S(1)}, s16[4,400,128]{2,1,0:T(8,128)(2,1)S(1)}, u32[]{:S(2)}, u32[]{:S(2)}) collective-permute-start(s16[4,400,128]{2,1,0:T(8,128)(2,1)S(1)} %get-tuple-element.44), channel_id=1, source_target_pairs={{0,32},{32,0},{64,96},{96,64},{128,160},{160,128},{192,224},{224,1... | collective-permute-start | bytes 1228808 | tf_op jit(solution)/shard_map/ppermute | solution.py:44

commit v5 on v4

--- a/solution.py
+++ b/solution.py
@@ -89,6 +89,7 @@
 X_ROWS = BLK_DEV * ROWS
 S_ROWS = 16
 CHUNK = X_ROWS + S_ROWS + 16
+S_EXP = X_ROWS // SL
 
 
 def prep_kernel(meta, v_ref, smp_ref, out_ref, rows_ref, acc, exps):
@@ -106,9 +107,9 @@
             return carry
 
         lax.fori_loop(0, SLOTS, body, 0)
-    for c in range(BLK_DEV):
-        q, e = code(acc[:, c * ROWS : (c + 1) * ROWS, :], 1)
-        out_ref[:, c * ROWS : (c + 1) * ROWS, :] = q
+    for c in range(X_ROWS // SL):
+        q, e = code(acc[:, c * SL : (c + 1) * SL, :], 1)
+        out_ref[:, c * SL : (c + 1) * SL, :] = q
         exps[:, c : c + 1, :] = e
     few = S_ROWS // BLK_DEV
     smp = smp_ref[...].astype(F32)
@@ -116,7 +117,7 @@
     for c in range(BLK_DEV):
         q, e = code(smp[:, c * few : (c + 1) * few], 1)
         parts.append(value(q))
-        exps[:, BLK_DEV + c : BLK_DEV + c + 1, :] = e
+        exps[:, S_EXP + c : S_EXP + c + 1, :] = e
     smp = jnp.concatenate(parts, axis=1).astype(jnp.int32)
     out_ref[:, X_ROWS : X_ROWS + S_ROWS, :] = smp.astype(I16)
     out_ref[:, X_ROWS + S_ROWS : CHUNK, :] = exps[...].astype(jnp.int32).astype(I16)
@@ -146,14 +147,15 @@
         e = value(got_ref[pan[p] // BLK_DEV, X_ROWS + S_ROWS : CHUNK, :])
         exps.append(e)
         r = pan[p] % BLK_DEV
-        exp_ref[p : p + 1, :] = jnp.where(r == 0, e[2:3], e[3:4])
+        exp_ref[p : p + 1, :] = jnp.where(r == 0, e[S_EXP : S_EXP + 1], e[S_EXP + 1 : S_EXP + 2])
     for c in range(BLK_DEV):
         stack = []
         for p in range(GRP):
             b = pan[p]
             at = pl.multiple_of(c * ROWS + (b % BLK_DEV) * SL, SL)
             q = value(got_ref[b // BLK_DEV, pl.ds(at, SL), :])
-            stack.append(q * scale_of(exps[p][c : c + 1]))
+            e = exps[p][BLK_DEV * c : BLK_DEV * (c + 1)]
+            stack.append(q * scale_of(jnp.where(b % BLK_DEV == 0, e[0:1], e[1:2])))
         turned = jnp.concatenate(stack, axis=0).T
         for g in range(GRP):
             out_ref[g, c * SL : (c + 1) * SL, :] = turned[g * SL : (g + 1) * SL]
@@ -236,8 +238,11 @@
             sc = scale_of(value(got_ref[i, X_ROWS + S_ROWS : CHUNK, :]))
             cols = []
             for c in range(BLK_DEV):
-                q = value(got_ref[i, c * ROWS : (c + 1) * ROWS, :])
-                cols.append(q * sc[c : c + 1])
+                part = []
+                for k in range(BLK_DEV * c, BLK_DEV * (c + 1)):
+                    q = value(got_ref[i, k * SL : (k + 1) * SL, :])
+                    part.append(q * sc[k : k + 1])
+                cols.append(jnp.concatenate(part, axis=0))
             stack.append(jnp.concatenate(cols, axis=1) + own_ref[i])
         x = jnp.concatenate(stack, axis=0).T
         hi = x.astype(BF16)
@@ -573,9 +578,9 @@
         groups += [(-step, down), (step, up)]
 
     theta = theta_parts(y[None], got, own)
-    sums = early_products(place, theta, left, groups[:5])
+    sums = early_products(place, theta, left, groups)
     across = z_across(jnp.where(s % 2 == 0, down, up))
-    groups = [(-3, down), (3, up), (4, across)]
+    groups = [(4, across)]
     keep, sent, tiny, u = last_products(place, theta, left, groups, sums, e_rows, diag)
 
     near = core_swap(tiny)

time: 139 us -> 139 us (level)
  no operation moved by 1% of the time
where the time goes in v5:
time: 139 us; the launch traced here: 137 us
  waiting for transfers between devices  47.3 us (34%)
  starting transfers between devices  42.1 us (30%)
  local copies, waits for them, and re-layouts  17.6 us (13%)
  Pallas kernels  14.1 us (10%)
  blocking collectives  12.8 us (9%)
  other arithmetic  1.71 us (1%)
    all_to_all x1, blocking collectives, per_device(): bundle = lax.all_to_all(bundle, 'samp', 0, 0, axis_index_groups=sides)  12.8 us
    all_to_all x1, starting transfers between devices, per_device(): got = lax.all_to_all(chunks, 'var', 0, 0)  11.8 us
    ppermute x6, starting transfers between devices, z_shift(): lax.ppermute(x, 'var', [(i, i // ZS * ZS + (i % ZS + k) % ZS) for i in ra...  10.2 us
    ppermute x6, waiting for transfers between devices, z_shift(): lax.ppermute(x, 'var', [(i, i // ZS * ZS + (i % ZS + k) % ZS) for i in ra...  9.97 us
    all_to_all x1, waiting for transfers between devices, per_device(): lax.all_to_all(jnp.broadcast_to(tiny[None], (OWN, 2 * GRP, BLK)), 'var',...  9.72 us
    all_to_all x1, waiting for transfers between devices, per_device(): got = lax.all_to_all(chunks, 'var', 0, 0)  8.16 us
    unnamed x29, local copies, waits for them, and re-layouts  7.11 us
    all_to_all x1, starting transfers between devices, per_device(): lax.all_to_all(jnp.broadcast_to(tiny[None], (OWN, 2 * GRP, BLK)), 'var',...  7.04 us
  transfers between devices with their start and end apart: 16, of which 14 were waited for; matrix products, arithmetic and copies ran while one was open for 10% of the time, Pallas kernels for 3%

profile of v5, /device:TPU:8, one launch (start us, length us, event | category | flops | bytes accessed | tf_op | source)
XLA Modules:
  0.0 137.1 jit_solution(3790503131744358721)
XLA Ops:
  0.6 1.1 constant_dynamic-slice_fusion.1.v_ref
  3.4 3.6 %shard_map.103 = (s16[32,96,128]{2,1,0:T(8,128)(2,1)}, f32[32,1024]{1,0:T(8,128)S(1)}) custom-call(s32[75]{0:T(128)S(1)} %pad_add_fusion.meta, f32[64,16,128]{2,1,0:T(8,128)S(1)} %constant_dynamic-slice_fusion.1.v_ref, bf16[32,16,128]{2,1,0:T(8,128)(2,1)S(1)} %bitcast.27), custom_call_target="tpu_custom_call" | custom-call | tf_op jit(solution)/shard_map/pallas_call | solution.py:131
  7.0 11.8 %all-to-all-start = ((s16[32,96,128]{2,1,0:T(8,128)(2,1)}), s16[32,96,128]{2,1,0:T(8,128)(2,1)S(1)}, u32[]{:S(2)}, u32[]{:S(2)}) async-start(s16[32,96,128]{2,1,0:T(8,128)(2,1)} %get-tuple-element.25), calls=%async_computation | async-start | bytes 1572864 | tf_op jit(solution)/shard_map/all_to_all | solution.py:551
  18.8 5.3 %constant_dynamic-slice_fusion = f32[2,32,128,16]{3,2,1,0:T(8,128)} fusion(f32[2,32,128,128]{3,2,1,0:T(8,128)} %bitcast.31, s32[]{:T(128)S(6)} %select_n.39), kind=kLoop, calls=%fused_computation.24 | loop fusion | bytes 1048580 | tf_op jit(solution)/shard_map/dynamic_slice | solution.py:557
  24.1 2.9 %copy.16 = f32[2,32,128,16]{2,1,3,0:T(8,128)S(1)} copy(f32[2,32,128,16]{3,2,1,0:T(8,128)} %constant_dynamic-slice_fusion) | data formatting | bytes 1048576
  31.4 8.2 %all-to-all-done.got_ref = s16[32,96,128]{2,1,0:T(8,128)(2,1)S(1)} async-done(((s16[32,96,128]{2,1,0:T(8,128)(2,1)}), s16[32,96,128]{2,1,0:T(8,128)(2,1)S(1)}, u32[]{:S(2)}, u32[]{:S(2)}) %all-to-all-start) | async-done | bytes 786464 | tf_op jit(solution)/shard_map/all_to_all | solution.py:551
  39.6 1.4 shard_map.104
  41.0 4.3 %all-to-all-start.1 = ((f32[8,32,128]{2,1,0:T(8,128)}), f32[8,32,128]{2,1,0:T(8,128)S(1)}, u32[]{:S(2)}, u32[]{:S(2)}) async-start(f32[8,32,128]{2,1,0:T(8,128)} %get-tuple-element.27), calls=%async_computation.1 | async-start | bytes 262144 | tf_op jit(solution)/shard_map/all_to_all | solution.py:565
  45.3 6.1 %all-to-all-done.1.turned_ref = f32[8,32,128]{2,1,0:T(8,128)S(1)} async-done(((f32[8,32,128]{2,1,0:T(8,128)}), f32[8,32,128]{2,1,0:T(8,128)S(1)}, u32[]{:S(2)}, u32[]{:S(2)}) %all-to-all-start.1) | async-done | bytes 131104 | tf_op jit(solution)/shard_map/all_to_all | solution.py:565
  52.3 1.6 %collective-permute-start = (s16[336,128]{1,0:T(8,128)(2,1)S(1)}, s16[336,128]{1,0:T(8,128)(2,1)S(1)}, u32[]{:S(2)}, u32[]{:S(2)}) collective-permute-start(s16[336,128]{1,0:T(8,128)(2,1)S(1)} %get-tuple-element.31), channel_id=1, source_target_pairs={{0,8},{1,9},{2,10},{3,11},{4,12},{5,13},{6,14},{7,15},{8,16},{9,17... | collective-permute-start | bytes 258056 | tf_op jit(solution)/shard_map/ppermute | solution.py:34
  53.9 1.4 %collective-permute-start.1 = (s16[336,128]{1,0:T(8,128)(2,1)S(1)}, s16[336,128]{1,0:T(8,128)(2,1)S(1)}, u32[]{:S(2)}, u32[]{:S(2)}) collective-permute-start(s16[336,128]{1,0:T(8,128)(2,1)S(1)} %get-tuple-element.31), channel_id=1, source_target_pairs={{0,24},{1,25},{2,26},{3,27},{4,28},{5,29},{6,30},{7,31},{8,0},{9,1... | collective-permute-start | bytes 258056 | tf_op jit(solution)/shard_map/ppermute | solution.py:34
  55.2 2.0 %collective-permute-start.2 = (s16[336,128]{1,0:T(8,128)(2,1)S(1)}, s16[336,128]{1,0:T(8,128)(2,1)S(1)}, u32[]{:S(2)}, u32[]{:S(2)}) collective-permute-start(s16[336,128]{1,0:T(8,128)(2,1)S(1)} %get-tuple-element.31), channel_id=1, source_target_pairs={{0,16},{1,17},{2,18},{3,19},{4,20},{5,21},{6,22},{7,23},{8,24},{9,... | collective-permute-start | bytes 258056 | tf_op jit(solution)/shard_map/ppermute | solution.py:34
  58.4 3.1 %collective-permute-done.2 = s16[336,128]{1,0:T(8,128)(2,1)S(1)} collective-permute-done((s16[336,128]{1,0:T(8,128)(2,1)S(1)}, s16[336,128]{1,0:T(8,128)(2,1)S(1)}, u32[]{:S(2)}, u32[]{:S(2)}) %collective-permute-start.2) | collective-permute-done | bytes 86048 | tf_op jit(solution)/shard_map/ppermute | solution.py:34
  61.5 1.9 %collective-permute-start.3 = (s16[1344,128]{1,0:T(8,128)(2,1)S(1)}, s16[1344,128]{1,0:T(8,128)(2,1)S(1)}, u32[]{:S(2)}, u32[]{:S(2)}) collective-permute-start(s16[1344,128]{1,0:T(8,128)(2,1)S(1)} %constant_dynamic-update-slice_fusion.refs_0_), channel_id=1, source_target_pairs={{0,1},{1,2},{2,3},{3,4},{4,5},{5,6},{6,7},{7,0},{8,9},{9,10},{10,1... | collective-permute-start | bytes 1032200 | tf_op jit(solution)/shard_map/ppermute | solution.py:38
  63.4 1.4 %collective-permute-start.5 = (s16[1344,128]{1,0:T(8,128)(2,1)S(1)}, s16[1344,128]{1,0:T(8,128)(2,1)}, u32[]{:S(2)}, u32[]{:S(2)}) collective-permute-start(s16[1344,128]{1,0:T(8,128)(2,1)S(1)} %constant_dynamic-update-slice_fusion.refs_0_), channel_id=1, source_target_pairs={{0,7},{1,0},{2,1},{3,2},{4,3},{5,4},{6,5},{7,6},{8,15},{9,8},{10,9... | collective-permute-start | bytes 1032200 | tf_op jit(solution)/shard_map/ppermute | solution.py:38
  65.7 3.5 %all-to-all-start.2 = ((s16[8,272,128]{2,1,0:T(8,128)(2,1)}), s16[8,272,128]{2,1,0:T(8,128)(2,1)S(1)}, u32[]{:S(2)}, u32[]{:S(2)}) async-start(s16[8,272,128]{2,1,0:T(8,128)(2,1)} %broadcast_in_dim.38), calls=%async_computation.2 | async-start | bytes 1114112 | tf_op jit(solution)/shard_map/all_to_all | solution.py:569
  69.2 2.4 %collective-permute-done.3.refs_1_ = s16[1344,128]{1,0:T(8,128)(2,1)S(1)} collective-permute-done((s16[1344,128]{1,0:T(8,128)(2,1)S(1)}, s16[1344,128]{1,0:T(8,128)(2,1)S(1)}, u32[]{:S(2)}, u32[]{:S(2)}) %collective-permute-start.3) | collective-permute-done | bytes 344096 | tf_op jit(solution)/shard_map/ppermute | solution.py:38
  72.8 2.8 %collective-permute-start.6 = (s16[1344,128]{1,0:T(8,128)(2,1)}, s16[1344,128]{1,0:T(8,128)(2,1)}, u32[]{:S(2)}, u32[]{:S(2)}) collective-permute-start(s16[1344,128]{1,0:T(8,128)(2,1)} %collective-permute-done.5.refs_2_), channel_id=1, source_target_pairs={{0,7},{1,0},{2,1},{3,2},{4,3},{5,4},{6,5},{7,6},{8,15},{9,8},{10,9... | collective-permute-start | bytes 1032200 | tf_op jit(solution)/shard_map/ppermute | solution.py:38
  75.6 4.3 %all-to-all-done.2.refs_6_ = s16[8,272,128]{2,1,0:T(8,128)(2,1)S(1)} async-done(((s16[8,272,128]{2,1,0:T(8,128)(2,1)}), s16[8,272,128]{2,1,0:T(8,128)(2,1)S(1)}, u32[]{:S(2)}, u32[]{:S(2)}) %all-to-all-start.2) | async-done | bytes 557088 | tf_op jit(solution)/shard_map/all_to_all | solution.py:569
  79.9 1.1 collective-permute-done.4.refs_3_
  81.3 3.5 %collective-permute-start.8 = (s16[1344,128]{1,0:T(8,128)(2,1)}, s16[1344,128]{1,0:T(8,128)(2,1)S(1)}, u32[]{:S(2)}, u32[]{:S(2)}) collective-permute-start(s16[1344,128]{1,0:T(8,128)(2,1)} %collective-permute-done.6.refs_4_), channel_id=1, source_target_pairs={{0,7},{1,0},{2,1},{3,2},{4,3},{5,4},{6,5},{7,6},{8,15},{9,8},{10,9... | collective-permute-start | bytes 1032200 | tf_op jit(solution)/shard_map/ppermute | solution.py:38
  84.8 6.3 %collective-permute-done.7.refs_5_ = s16[1344,128]{1,0:T(8,128)(2,1)S(1)} collective-permute-done((s16[1344,128]{1,0:T(8,128)(2,1)}, s16[1344,128]{1,0:T(8,128)(2,1)S(1)}, u32[]{:S(2)}, u32[]{:S(2)}) %collective-permute-start.7) | collective-permute-done | bytes 344096 | tf_op jit(solution)/shard_map/ppermute | solution.py:38
  92.7 1.0 copy-done.5
  93.7 4.0 %shard_map.107 = (f32[256,1024]{1,0:T(8,128)S(1)}, f32[256,1024]{1,0:T(8,128)S(1)}) custom-call(s32[19]{0:T(128)S(1)} %concatenate.12.meta, s16[1344,128]{1,0:T(8,128)(2,1)S(1)} %copy-done.1, s16[1344,128]{1,0:T(8,128)(2,1)S(1)} %copy-done.5, s16[1344,128]{1,0:T(8,128)(2,1)} %collective-permute-done.5.refs_2_, ...), custom_call_target="tpu_custom_call" | custom-call | flops 1879048192 | bytes 21000000 | tf_op jit(solution)/shard_map/pallas_call | solution.py:413
  97.7 2.1 %collective-permute-done.9.refs_0_ = s16[1344,128]{1,0:T(8,128)(2,1)S(1)} collective-permute-done((s16[1344,128]{1,0:T(8,128)(2,1)S(1)}, s16[1344,128]{1,0:T(8,128)(2,1)S(1)}, u32[]{:S(2)}, u32[]{:S(2)}) %collective-permute-start.9) | collective-permute-done | bytes 344096 | tf_op jit(solution)/shard_map/ppermute | solution.py:53
  99.8 2.1 %shard_map.108 = (f32[4,384,128]{2,1,0:T(8,128)S(1)}, s16[4,400,128]{2,1,0:T(8,128)(2,1)S(1)}, f32[16,128]{1,0:T(8,128)S(1)}, f32[256,128]{1,0:T(8,128)S(1)}) custom-call(s32[19]{0:T(128)S(1)} %concatenate.12.meta, s16[1344,128]{1,0:T(8,128)(2,1)S(1)} %collective-permute-done.9.refs_0_, ...), custom_call_target="tpu_custom_call" | custom-call | flops 268435456 | bytes 3000000 | tf_op jit(solution)/shard_map/pallas_call | solution.py:413
  102.1 1.1 collective-permute-done.10
  103.9 7.0 %all-to-all-start.3 = ((f32[32,16,128]{2,1,0:T(8,128)}), f32[32,16,128]{2,1,0:T(8,128)S(1)}, u32[]{:S(2)}, u32[]{:S(2)}) async-start(f32[32,16,128]{2,1,0:T(8,128)} %broadcast_in_dim.41), calls=%async_computation.3 | async-start | bytes 524288 | tf_op jit(solution)/shard_map/all_to_all | solution.py:591
  111.1 1.7 %collective-permute-done.11.got_ref = s16[4,400,128]{2,1,0:T(8,128)(2,1)S(1)} collective-permute-done((s16[4,400,128]{2,1,0:T(8,128)(2,1)S(1)}, s16[4,400,128]{2,1,0:T(8,128)(2,1)S(1)}, u32[]{:S(2)}, u32[]{:S(2)}) %collective-permute-start.11) | collective-permute-done | bytes 409632 | tf_op jit(solution)/shard_map/ppermute | solution.py:44
  112.8 9.7 %all-to-all-done.3.tiny_ref = f32[32,16,128]{2,1,0:T(8,128)S(1)} async-done(((f32[32,16,128]{2,1,0:T(8,128)}), f32[32,16,128]{2,1,0:T(8,128)S(1)}, u32[]{:S(2)}, u32[]{:S(2)}) %all-to-all-start.3) | async-done | bytes 262176 | tf_op jit(solution)/shard_map/all_to_all | solution.py:591
  122.9 12.8 %all_to_all.25.bundle_ref = s16[4,448,128]{2,1,0:T(8,128)(2,1)S(1)} all-to-all(s16[4,448,128]{2,1,0:T(8,128)(2,1)S(1)} %shard_map.109), channel_id=1, replica_groups={{0,64,128,192},{32,96,160,224},{1,65,129,193},{33,97,161,225},{2,66,130..., dimensions={0} | all-to-all | bytes 917504 | tf_op jit(solution)/shard_map/all_to_all | solution.py:594
  135.7 1.4 %shard_map.110 = (f32[256,128]{1,0:T(8,128)}, f32[256,128]{1,0:T(8,128)}, f32[8,16,128]{2,1,0:T(8,128)}) custom-call(s32[19]{0:T(128)S(1)} %concatenate.12.meta, s16[4,448,128]{2,1,0:T(8,128)(2,1)S(1)} %all_to_all.25.bundle_ref, f32[256,128]{1,0:T(8,128)S(1)} %get-tuple-element.45.u_ref, f32[2,128]{1,0:T(2,128)S(1)} %bitcast.30, ...), custom_call_target="tpu_custom_call" | custom-call | tf_op jit(solution)/shard_map/pallas_call | solution.py:524
  (62 shorter events, 13.5 us)
Async XLA Ops:
  2.5 0.9 copy-start.2
  7.0 32.6 %all-to-all-start = ((s16[32,96,128]{2,1,0:T(8,128)(2,1)}), s16[32,96,128]{2,1,0:T(8,128)(2,1)S(1)}, u32[]{:S(2)}, u32[]{:S(2)}) async-start(s16[32,96,128]{2,1,0:T(8,128)(2,1)} %get-tuple-element.25), calls=%async_computation | async-start | bytes 1572864 | tf_op jit(solution)/shard_map/all_to_all | solution.py:551
  24.1 3.5 %copy-start.8 = (s32[64,1]{0,1:T(1,128)S(1)}, s32[64,1]{0,1:T(1,128)}, u32[]{:S(2)}) copy-start(s32[64,1]{0,1:T(1,128)} %param.11) | copy-start | bytes 772
  24.1 4.3 %copy-start.9 = (s32[2]{0:T(128)S(1)}, s32[2]{0:T(128)}, u32[]{:S(2)}) copy-start(s32[2]{0:T(128)} %param.12) | copy-start | bytes 28
  24.1 6.7 %copy-start.11 = (s32[4]{0:T(128)S(1)}, s32[4]{0:T(128)}, u32[]{:S(2)}) copy-start(s32[4]{0:T(128)} %constant.68.clone) | copy-start | bytes 52
  24.1 6.7 %copy-start.3 = (bf16[256,256]{1,0:T(8,128)(2,1)S(1)}, bf16[256,256]{1,0:T(8,128)(2,1)}, u32[]{:S(2)}) copy-start(bf16[256,256]{1,0:T(8,128)(2,1)} %param.8) | copy-start | bytes 393220
  27.1 12.5 %copy-start.6 = (s32[8]{0:T(128)S(1)}, s32[8]{0:T(128)}, u32[]{:S(2)}) copy-start(s32[8]{0:T(128)} %pan.1) | copy-start | bytes 100
  27.1 18.2 %copy-start.10 = (s32[8]{0:T(128)S(1)}, s32[8]{0:T(128)}, u32[]{:S(2)}) copy-start(s32[8]{0:T(128)} %param.14) | copy-start | bytes 100
  41.0 10.4 %all-to-all-start.1 = ((f32[8,32,128]{2,1,0:T(8,128)}), f32[8,32,128]{2,1,0:T(8,128)S(1)}, u32[]{:S(2)}, u32[]{:S(2)}) async-start(f32[8,32,128]{2,1,0:T(8,128)} %get-tuple-element.27), calls=%async_computation.1 | async-start | bytes 262144 | tf_op jit(solution)/shard_map/all_to_all | solution.py:565
  52.3 5.3 %collective-permute-start = (s16[336,128]{1,0:T(8,128)(2,1)S(1)}, s16[336,128]{1,0:T(8,128)(2,1)S(1)}, u32[]{:S(2)}, u32[]{:S(2)}) collective-permute-start(s16[336,128]{1,0:T(8,128)(2,1)S(1)} %get-tuple-element.31), channel_id=1, source_target_pairs={{0,8},{1,9},{2,10},{3,11},{4,12},{5,13},{6,14},{7,15},{8,16},{9,17... | collective-permute-start | bytes 258056 | tf_op jit(solution)/shard_map/ppermute | solution.py:34
  53.9 4.5 %collective-permute-start.1 = (s16[336,128]{1,0:T(8,128)(2,1)S(1)}, s16[336,128]{1,0:T(8,128)(2,1)S(1)}, u32[]{:S(2)}, u32[]{:S(2)}) collective-permute-start(s16[336,128]{1,0:T(8,128)(2,1)S(1)} %get-tuple-element.31), channel_id=1, source_target_pairs={{0,24},{1,25},{2,26},{3,27},{4,28},{5,29},{6,30},{7,31},{8,0},{9,1... | collective-permute-start | bytes 258056 | tf_op jit(solution)/shard_map/ppermute | solution.py:34
  55.2 6.2 %collective-permute-start.2 = (s16[336,128]{1,0:T(8,128)(2,1)S(1)}, s16[336,128]{1,0:T(8,128)(2,1)S(1)}, u32[]{:S(2)}, u32[]{:S(2)}) collective-permute-start(s16[336,128]{1,0:T(8,128)(2,1)S(1)} %get-tuple-element.31), channel_id=1, source_target_pairs={{0,16},{1,17},{2,18},{3,19},{4,20},{5,21},{6,22},{7,23},{8,24},{9,... | collective-permute-start | bytes 258056 | tf_op jit(solution)/shard_map/ppermute | solution.py:34
  61.5 19.4 %copy-start = (s16[1344,128]{1,0:T(8,128)(2,1)}, s16[1344,128]{1,0:T(8,128)(2,1)S(1)}, u32[]{:S(2)}) copy-start(s16[1344,128]{1,0:T(8,128)(2,1)S(1)} %constant_dynamic-update-slice_fusion.refs_0_) | copy-start | bytes 1032196
  61.5 10.1 %collective-permute-start.3 = (s16[1344,128]{1,0:T(8,128)(2,1)S(1)}, s16[1344,128]{1,0:T(8,128)(2,1)S(1)}, u32[]{:S(2)}, u32[]{:S(2)}) collective-permute-start(s16[1344,128]{1,0:T(8,128)(2,1)S(1)} %constant_dynamic-update-slice_fusion.refs_0_), channel_id=1, source_target_pairs={{0,1},{1,2},{2,3},{3,4},{4,5},{5,6},{6,7},{7,0},{8,9},{9,10},{10,1... | collective-permute-start | bytes 1032200 | tf_op jit(solution)/shard_map/ppermute | solution.py:38
  63.4 9.4 %collective-permute-start.5 = (s16[1344,128]{1,0:T(8,128)(2,1)S(1)}, s16[1344,128]{1,0:T(8,128)(2,1)}, u32[]{:S(2)}, u32[]{:S(2)}) collective-permute-start(s16[1344,128]{1,0:T(8,128)(2,1)S(1)} %constant_dynamic-update-slice_fusion.refs_0_), channel_id=1, source_target_pairs={{0,7},{1,0},{2,1},{3,2},{4,3},{5,4},{6,5},{7,6},{8,15},{9,8},{10,9... | collective-permute-start | bytes 1032200 | tf_op jit(solution)/shard_map/ppermute | solution.py:38
  65.7 14.2 %all-to-all-start.2 = ((s16[8,272,128]{2,1,0:T(8,128)(2,1)}), s16[8,272,128]{2,1,0:T(8,128)(2,1)S(1)}, u32[]{:S(2)}, u32[]{:S(2)}) async-start(s16[8,272,128]{2,1,0:T(8,128)(2,1)} %broadcast_in_dim.38), calls=%async_computation.2 | async-start | bytes 1114112 | tf_op jit(solution)/shard_map/all_to_all | solution.py:569
  71.6 9.3 %collective-permute-start.4 = (s16[1344,128]{1,0:T(8,128)(2,1)S(1)}, s16[1344,128]{1,0:T(8,128)(2,1)}, u32[]{:S(2)}, u32[]{:S(2)}) collective-permute-start(s16[1344,128]{1,0:T(8,128)(2,1)S(1)} %collective-permute-done.3.refs_1_), channel_id=1, source_target_pairs={{0,1},{1,2},{2,3},{3,4},{4,5},{5,6},{6,7},{7,0},{8,9},{9,10},{10,1... | collective-permute-start | bytes 1032200 | tf_op jit(solution)/shard_map/ppermute | solution.py:38
  72.1 0.7 copy-start.4
  72.8 8.3 %collective-permute-start.6 = (s16[1344,128]{1,0:T(8,128)(2,1)}, s16[1344,128]{1,0:T(8,128)(2,1)}, u32[]{:S(2)}, u32[]{:S(2)}) collective-permute-start(s16[1344,128]{1,0:T(8,128)(2,1)} %collective-permute-done.5.refs_2_), channel_id=1, source_target_pairs={{0,7},{1,0},{2,1},{3,2},{4,3},{5,4},{6,5},{7,6},{8,15},{9,8},{10,9... | collective-permute-start | bytes 1032200 | tf_op jit(solution)/shard_map/ppermute | solution.py:38
  81.1 10.0 %collective-permute-start.7 = (s16[1344,128]{1,0:T(8,128)(2,1)}, s16[1344,128]{1,0:T(8,128)(2,1)S(1)}, u32[]{:S(2)}, u32[]{:S(2)}) collective-permute-start(s16[1344,128]{1,0:T(8,128)(2,1)} %collective-permute-done.4.refs_3_), channel_id=1, source_target_pairs={{0,1},{1,2},{2,3},{3,4},{4,5},{5,6},{6,7},{7,0},{8,9},{9,10},{10,1... | collective-permute-start | bytes 1032200 | tf_op jit(solution)/shard_map/ppermute | solution.py:38
  81.3 9.8 %collective-permute-start.8 = (s16[1344,128]{1,0:T(8,128)(2,1)}, s16[1344,128]{1,0:T(8,128)(2,1)S(1)}, u32[]{:S(2)}, u32[]{:S(2)}) collective-permute-start(s16[1344,128]{1,0:T(8,128)(2,1)} %collective-permute-done.6.refs_4_), channel_id=1, source_target_pairs={{0,7},{1,0},{2,1},{3,2},{4,3},{5,4},{6,5},{7,6},{8,15},{9,8},{10,9... | collective-permute-start | bytes 1032200 | tf_op jit(solution)/shard_map/ppermute | solution.py:38
  91.2 8.5 %collective-permute-start.9 = (s16[1344,128]{1,0:T(8,128)(2,1)S(1)}, s16[1344,128]{1,0:T(8,128)(2,1)S(1)}, u32[]{:S(2)}, u32[]{:S(2)}) collective-permute-start(s16[1344,128]{1,0:T(8,128)(2,1)S(1)} %broadcast_select_fusion), channel_id=1, source_target_pairs={{0,1},{1,2},{2,3},{3,4},{4,5},{5,6},{6,7},{7,0},{8,9},{9,10},{10,1... | collective-permute-start | bytes 1032200 | tf_op jit(solution)/shard_map/ppermute | solution.py:53
  91.7 1.0 copy-start.1
  92.7 1.0 copy-start.5
  93.7 6.1 %copy-start.7 = (f32[256]{0:T(256)S(1)}, f32[256]{0:T(256)}, u32[]{:S(2)}) copy-start(f32[256]{0:T(256)} %param.9) | copy-start | bytes 3076
  101.9 1.3 collective-permute-start.10
  103.9 18.6 %all-to-all-start.3 = ((f32[32,16,128]{2,1,0:T(8,128)}), f32[32,16,128]{2,1,0:T(8,128)S(1)}, u32[]{:S(2)}, u32[]{:S(2)}) async-start(f32[32,16,128]{2,1,0:T(8,128)} %broadcast_in_dim.41), calls=%async_computation.3 | async-start | bytes 524288 | tf_op jit(solution)/shard_map/all_to_all | solution.py:591
  111.0 1.8 %collective-permute-start.11 = (s16[4,400,128]{2,1,0:T(8,128)(2,1)S(1)}, s16[4,400,128]{2,1,0:T(8,128)(2,1)S(1)}, u32[]{:S(2)}, u32[]{:S(2)}) collective-permute-start(s16[4,400,128]{2,1,0:T(8,128)(2,1)S(1)} %get-tuple-element.44), channel_id=1, source_target_pairs={{0,32},{32,0},{64,96},{96,64},{128,160},{160,128},{192,224},{224,1... | collective-permute-start | bytes 1228808 | tf_op jit(solution)/shard_map/ppermute | solution.py:44
